TPU v7x, 512 devices: a whole 4x8x8 slice. The times are simulated.
512 devices in a mesh: tm: 64 (over y, x, core), space: 8 (over z).
Axes of the slice: x: 4, y: 8, z: 8, core: 2. Of those that a mesh axis runs over, the one named last changes fastest.
Arguments:
- states: float32 [64, 21, 8192], P('tm', None, 'space'), may hold values from -6 to 6
- neighbour: int32 [3, 8192], P(None, 'space'), may hold values from -64 to 64, as said below
- edge_x: float32 [3, 8192], P(None, 'space'), may hold values from -0.3 to 0.3
- edge_y: float32 [3, 8192], P(None, 'space'), may hold values from -0.3 to 0.3
- edge_damp: float32 [3, 8192], P(None, 'space'), may hold values from 0.03 to 0.15
- coriolis: float32 [8192], P('space'), may hold values from -0.2 to 0.2
- flux_x: float32 [21, 21], replicated, may hold values from -0.625 to 0.625
- flux_y: float32 [21, 21], replicated, may hold values from -0.625 to 0.625
- rotation: float32 [21, 21], replicated, may hold values from -1.25 to 1.25
- restrict_matrix: float32 [4, 21], replicated, may hold values from -2.5 to 2.5
- prolong_matrix: float32 [21, 4], replicated, may hold values from -6 to 6
- restrict_index: int32 [8192], P('space'), may hold values from 0 to 31, as said below
- coarse_inverse: float32 [4, 4, 256], replicated, may hold values from -1 to 1
Outputs:
- new_states: float32 [64, 21, 8192], P('tm', None, 'space')
Inputs may be any that keep to these rules, and one draw needn't show every extreme that they name: Triangle c borders triangles (c + neighbour[e, c]) mod 8192 for e = 0, 1, 2. `restrict_index`: every coarse triangle of every partition holds at least one triangle.
All inputs are finite; a program needn't handle non-finite values.
Results may differ from a plain program's by a relative error of at most 0.0003.
Values sent between devices are 32-bit elements; how exact they have to be, the bound alone decides.
No kernel may reach another device: no remote copies, remote signals or barrier semaphores. Data moves between devices by JAX's collectives and lax.ppermute only.
A program may use at most 64 MiB of HBM per device.

v0:
```python
import jax
import jax.numpy as jnp
from jax import lax
from jax.sharding import PartitionSpec as P

CDOF = 4
HW = 64
STEPS = 16
COARSE_STEPS = 4
COARSE_DEV = 32


coupling = 0.1
opposite = 0.25
highest = lax.Precision.HIGHEST


def padded_2(cells, sides, width):
    for axis, dim in sides:
        count = lax.axis_size(axis)
        head = lax.slice_in_dim(cells, 0, width, axis=dim)
        tail = lax.slice_in_dim(cells, cells.shape[dim] - width, cells.shape[dim], axis=dim)
        cells = jnp.concatenate(
            [
                lax.ppermute(tail, axis, [(i, (i + 1) % count) for i in range(count)]),
                cells,
                lax.ppermute(head, axis, [((i + 1) % count, i) for i in range(count)]),
            ],
            axis=dim,
        )
    return cells


def shifted(shard, axis, by):
    count = lax.axis_size(axis)
    pairs = [(i, i + by) for i in range(count) if 0 <= i + by < count]
    return lax.ppermute(shard, axis, pairs)


def tendency(source, offsets, edge_x, edge_y, edge_damp, coriolis, stencil):
    span_cells = offsets.shape[1]
    center = lax.slice_in_dim(source, HW, HW + span_cells, axis=1)
    places = HW + jnp.arange(span_cells, dtype=jnp.int32)
    along_x = jnp.zeros_like(center)
    along_y = jnp.zeros_like(center)
    damped = jnp.zeros_like(center)
    for edge_index in range(3):
        nearby = jnp.take(source, places + offsets[edge_index], axis=1)
        difference = nearby - center
        along_x = along_x + edge_x[edge_index] * difference
        along_y = along_y + edge_y[edge_index] * difference
        damped = damped + edge_damp[edge_index] * difference
    stacked = jnp.concatenate([along_x, along_y, coriolis * center], axis=0)
    return jnp.dot(stencil, stacked, precision=highest) + damped


def restrict(values, onehot, restrict_matrix):
    totals = jnp.einsum("dc,kc->dk", values, onehot, precision=highest)
    counts = jnp.sum(onehot, axis=1)
    return jnp.dot(restrict_matrix, totals, precision=highest) / counts


def prolong(correction, onehot, prolong_matrix):
    return jnp.dot(
        jnp.dot(prolong_matrix, correction, precision=highest), onehot, precision=highest
    )


def coarse_step(vector, inverse_blocks):
    half_cycle = vector.shape[1] // 2
    blended = vector + coupling * (
        jnp.roll(vector, 1, axis=1) + jnp.roll(vector, -1, axis=1) - 2.0 * vector
    )
    blended = blended + opposite * (jnp.roll(vector, half_cycle, axis=1) - vector)
    result = inverse_blocks[:, 0, :] * blended[0]
    for column in range(1, CDOF):
        result = result + inverse_blocks[:, column, :] * blended[column]
    return result


def coarse_slice(vector, inverse_blocks):
    for repeat in range(COARSE_STEPS):
        vector = coarse_step(vector, inverse_blocks)
    return vector


def local(
    states,
    neighbour,
    edge_x,
    edge_y,
    edge_damp,
    coriolis,
    flux_x,
    flux_y,
    rotation,
    restrict_matrix,
    prolong_matrix,
    restrict_index,
    coarse_inverse,
):
    current_state = states[0]
    stencil = jnp.concatenate([flux_x, flux_y, rotation], axis=1)

    def section_rate(values):
        padded = padded_2(values, (("space", 1),), HW)
        return tendency(padded, neighbour, edge_x, edge_y, edge_damp, coriolis, stencil)

    def advance(index_step, current):
        first_rate = section_rate(current)
        middle = current + first_rate
        second_rate = section_rate(middle)
        return current + 0.5 * (first_rate + second_rate)

    finals = lax.fori_loop(0, STEPS, advance, current_state)
    onehot = (restrict_index[None, :] == jnp.arange(COARSE_DEV, dtype=jnp.int32)[:, None]).astype(
        jnp.float32
    )
    starts_local = restrict(current_state, onehot, restrict_matrix)
    ends_local = restrict(finals, onehot, restrict_matrix)
    starts_all, ends_all = (
        lax.all_gather(starts_local, "space", axis=1, tiled=True),
        lax.all_gather(ends_local, "space", axis=1, tiled=True),
    )
    jumps = ends_all - coarse_slice(starts_all, coarse_inverse)
    leading = lax.axis_index("tm") == 0
    slices_here = lax.axis_size("tm")

    def hand_on(repeat, chain_now):
        received = shifted(chain_now, "tm", 1)
        return jnp.where(leading, ends_all, coarse_slice(received, coarse_inverse) + jumps)

    chain_all = lax.fori_loop(0, slices_here, hand_on, jnp.zeros_like(ends_all))
    offset_start = lax.axis_index("space") * COARSE_DEV
    chain_local = lax.dynamic_slice_in_dim(chain_all, offset_start, COARSE_DEV, 1)
    correction = chain_local - ends_local
    updated = finals + prolong(correction, onehot, prolong_matrix)
    return updated[None]


def solution(mesh):
    in_specs = (
        P("tm", None, "space"),
        P(None, "space"),
        P(None, "space"),
        P(None, "space"),
        P(None, "space"),
        P("space"),
        P(),
        P(),
        P(),
        P(),
        P(),
        P("space"),
        P(),
    )
    out_specs = P("tm", None, "space")
    return jax.shard_map(local, mesh=mesh, in_specs=in_specs, out_specs=out_specs, check_vma=False)
```

profile of v0, /device:TPU:32, one launch (start us, length us, event | category | flops | bytes accessed | tf_op | source)
XLA Modules:
  0.0 1254.2 jit_solution(6808930506759061983)
XLA Ops:
  1.8 610.4 %while.21 = (s32[]{:T(128)}, f32[21,1024]{1,0:T(8,128)S(1)}, f32[3,1024]{1,0:T(4,128)S(1)}, s32[3,1024]{1,0:T(4,128)S(1)}, f32[3,1024]{1,0:T(4,128)S(1)}, /*inde...) while((s32[]{:T(128)}, f32[21,1024]{1,0:T(8,128)S(1)}, ...), condition=%wide.region_1.3_spmd, body=%wide.region_0.2_spmd.sunk | while | flops 34018304 | bytes 6586965 | solution.py:115
  6.1 8.6 collective-permute-start.1
  613.5 21.4 %all-gather.1 = f32[8,32,4]{1,2,0:T(4,128)S(1)} all-gather(f32[1,32,4]{1,2,0:T(4,128)S(1)} %fusion.55), channel_id=1, replica_groups=mesh['tm'=64,'space'=8] {'space'}, dimensions={0}, use_global_device_ids=true | all-gather | bytes 4608 | tf_op jit(solution)/shard_map/all_gather | solution.py:122
  636.0 21.8 %all-gather = f32[8,32,4]{1,2,0:T(4,128)S(1)} all-gather(f32[1,32,4]{1,2,0:T(4,128)S(1)} %bitcast.491), channel_id=1, replica_groups=mesh['tm'=64,'space'=8] {'space'}, dimensions={0}, use_global_device_ids=true | all-gather | bytes 4608 | tf_op jit(solution)/shard_map/all_gather | solution.py:123
  657.9 595.1 %while.22 = (s32[]{:T(128)}, f32[4,256]{1,0:T(4,128)S(1)}, pred[]{:T(512)}, f32[4,4,256]{2,0,1:T(4,128)S(1)}, f32[4,256]{1,0:T(4,128)S(1)}, /*index=5*/f32[4,256]{1,0:T(4,128)S(1)}, s32[]{:T(128)}, s32[]{:T(128)}) while((s32[]{:T(128)}, f32[4,256]{1,0:T(4,128)S(1)}, pred[]{:T(512)}, f32[4,4,256]{2,0,1:T(4,128)S(1)}, ...), condition=%wide.region_4.6_spmd.clone, body=%wide.region_3.5_spmd.clone.sunk | while | flops 98307 | bytes 393352 | solution.py:133
  659.8 6.3 collective-permute-done.4
  669.1 6.3 collective-permute-done.4
  678.4 6.3 collective-permute-done.4
  697.0 6.3 collective-permute-done.4
  706.3 6.3 collective-permute-done.4
  724.9 6.3 collective-permute-done.4
  734.2 6.3 collective-permute-done.4
  743.5 6.3 collective-permute-done.4
  752.8 6.3 collective-permute-done.4
  771.4 6.3 collective-permute-done.4
  780.7 6.3 collective-permute-done.4
  799.3 6.3 collective-permute-done.4
  808.6 6.3 collective-permute-done.4
  827.2 6.3 collective-permute-done.4
  836.5 6.3 collective-permute-done.4
  845.8 6.3 collective-permute-done.4
  855.1 6.3 collective-permute-done.4
  873.7 6.3 collective-permute-done.4
  883.0 6.3 collective-permute-done.4
  901.6 6.3 collective-permute-done.4
  910.9 6.3 collective-permute-done.4
  920.2 6.3 collective-permute-done.4
  929.5 6.3 collective-permute-done.4
  948.1 6.3 collective-permute-done.4
  957.4 6.3 collective-permute-done.4
  976.0 6.3 collective-permute-done.4
  985.3 6.3 collective-permute-done.4
  1003.9 6.3 collective-permute-done.4
  1013.2 6.3 collective-permute-done.4
  1022.5 6.3 collective-permute-done.4
  1031.8 6.3 collective-permute-done.4
  1050.4 6.3 collective-permute-done.4
  1059.7 6.3 collective-permute-done.4
  1078.3 6.3 collective-permute-done.4
  1087.6 6.3 collective-permute-done.4
  1096.9 6.3 collective-permute-done.4
  1106.2 6.3 collective-permute-done.4
  1124.8 6.3 collective-permute-done.4
  1134.1 6.3 collective-permute-done.4
  1152.7 6.3 collective-permute-done.4
  1162.0 6.3 collective-permute-done.4
  1180.5 6.3 collective-permute-done.4
  1189.8 6.3 collective-permute-done.4
  (2374 shorter events, 922.1 us)
Async XLA Ops:
  1.9 13.0 %collective-permute-start = (f32[21,64]{1,0:T(8,128)S(1)}, f32[21,64]{1,0:T(8,128)S(1)}, u32[]{:S(2)}, u32[]{:S(2)}) collective-permute-start(f32[21,64]{1,0:T(8,128)S(1)} %get-tuple-element.417), channel_id=1, source_target_pairs={{0,1},{1,2},{2,3},{3,4},{4,5},{5,6},{6,7},{7,0},{8,9},{9,10},{10,1... | collective-permute-start | bytes 16136 | tf_op jit(solution)/shard_map/while/body/eval_jaxpr/ppermute | solution.py:25
  6.1 10.0 collective-permute-start.1
  657.9 8.2 collective-permute-start.4
  667.2 8.2 collective-permute-start.4
  676.5 8.2 collective-permute-start.4
  695.1 8.2 collective-permute-start.4
  704.4 8.2 collective-permute-start.4
  723.0 8.2 collective-permute-start.4
  732.3 8.2 collective-permute-start.4
  741.6 8.2 collective-permute-start.4
  750.9 8.2 collective-permute-start.4
  760.2 8.2 collective-permute-start.4
  769.5 8.2 collective-permute-start.4
  778.8 8.2 collective-permute-start.4
  797.4 8.2 collective-permute-start.4
  806.7 8.2 collective-permute-start.4
  825.3 8.2 collective-permute-start.4
  834.6 8.2 collective-permute-start.4
  843.9 8.2 collective-permute-start.4
  853.2 8.2 collective-permute-start.4
  871.8 8.2 collective-permute-start.4
  881.1 8.2 collective-permute-start.4
  899.7 8.2 collective-permute-start.4
  909.0 8.2 collective-permute-start.4
  918.2 8.2 collective-permute-start.4
  927.5 8.2 collective-permute-start.4
  936.8 8.2 collective-permute-start.4
  946.1 8.2 collective-permute-start.4
  955.4 8.2 collective-permute-start.4
  974.0 8.2 collective-permute-start.4
  983.3 8.2 collective-permute-start.4
  1001.9 8.2 collective-permute-start.4
  1011.2 8.2 collective-permute-start.4
  1020.5 8.2 collective-permute-start.4
  1029.8 8.2 collective-permute-start.4
  1048.4 8.2 collective-permute-start.4
  1057.7 8.2 collective-permute-start.4
  1076.3 8.2 collective-permute-start.4
  1085.6 8.2 collective-permute-start.4
  1094.9 8.2 collective-permute-start.4
  1104.2 8.2 collective-permute-start.4
  1113.5 8.2 collective-permute-start.4
  1122.8 8.2 collective-permute-start.4
  1132.1 8.2 collective-permute-start.4
  1150.7 8.2 collective-permute-start.4
  1160.0 8.2 collective-permute-start.4
  1178.6 8.2 collective-permute-start.4
  1187.9 8.2 collective-permute-start.4
  (93 other events, 3027.8 us)
where the time goes:
time: 1260 us; the launch traced here: 1250 us
  waiting for transfers between devices  462 us (37%)
  starting transfers between devices  355 us (28%)
  local copies, waits for them, and re-layouts  346 us (27%)
  blocking collectives  43.2 us (3%)
  other arithmetic  27.9 us (2%)
    ppermute x64, waiting for transfers between devices, shifted(): return lax.ppermute(shard, axis, pairs)  404 us
    gather x192, local copies, waits for them, and re-layouts, tendency(): nearby = jnp.take(source, places + offsets[edge_index], axis=1)  289 us
    ppermute x32, starting transfers between devices, padded_2(): lax.ppermute(head, axis, [((i + 1) % count, i) for i in range(count)])  124 us
    ppermute x64, starting transfers between devices, shifted(): return lax.ppermute(shard, axis, pairs)  123 us
    ppermute x32, starting transfers between devices, padded_2(): lax.ppermute(tail, axis, [(i, (i + 1) % count) for i in range(count)])  108 us
    ppermute x32, waiting for transfers between devices, padded_2(): lax.ppermute(head, axis, [((i + 1) % count, i) for i in range(count)])  57.8 us
    slice x520, local copies, waits for them, and re-layouts, coarse_step(): jnp.roll(vector, -1, axis=1)  37.6 us
  transfers between devices with their start and end apart: 128, of which 96 were waited for; matrix products, arithmetic and copies ran while one was open for 0% of the time, Pallas kernels for 0%

commit v1 on v0

v1 whole, which is shorter than its diff:
```python
import functools

import jax
import jax.numpy as jnp
from jax import lax
from jax.experimental import pallas as pl
from jax.experimental.pallas import tpu as pltpu
from jax.sharding import PartitionSpec as P

DOF = 21
CDOF = 4
ROWS = 24
LANES = 128
HALF = 64
CELLS_DEV = 1024
COARSE_DEV = 32
COARSE_STEPS = 4
PARTS = 8
SLICES = 64
BLOCKS = CELLS_DEV // LANES
PHASE_STEPS = 8
SEGMENT = 2
WINDOW = 3 * BLOCKS

coupling = 0.1
opposite = 0.25
highest = lax.Precision.HIGHEST
f32 = jnp.float32
bf16 = jnp.bfloat16
vmem = pl.BlockSpec(memory_space=pltpu.VMEM)


def lane_gather(values, index):
    numbers = lax.GatherDimensionNumbers(
        offset_dims=(),
        collapsed_slice_dims=(1,),
        start_index_map=(1,),
        operand_batching_dims=(0,),
        start_indices_batching_dims=(0,),
    )
    return lax.gather(
        values, index[..., None], numbers, (1, 1), mode=lax.GatherScatterMode.PROMISE_IN_BOUNDS
    )


def two_terms(values):
    high = values.astype(bf16)
    return high, (values - high.astype(f32)).astype(bf16)


def lanes_of(block, count=1):
    return slice(block * LANES, (block + count) * LANES)


def fill_window(state_refs, mesh_refs, field, places, coefs):
    inside = lax.broadcasted_iota(jnp.int32, (ROWS, CELLS_DEV), 0) < DOF
    lane = lax.broadcasted_iota(jnp.int32, (8, CELLS_DEV), 1) % LANES
    edge = jnp.zeros((ROWS, LANES), f32)
    field[:, lanes_of(0)] = edge
    field[:, lanes_of(WINDOW + 1)] = edge
    for part, (state_ref, mesh_ref) in enumerate(zip(state_refs, mesh_refs)):
        cells = lanes_of(1 + part * BLOCKS, BLOCKS)
        field[:, cells] = jnp.where(inside, state_ref[0:ROWS, :], 0.0)
        for e in range(3):
            offset = mesh_ref[DOF + e : DOF + e + 1, :].astype(jnp.int32)
            target = jnp.broadcast_to(offset, (8, CELLS_DEV)) + lane
            within = (target >= 0) & (target < LANES)
            places[e, :, cells] = (target & (LANES - 1)) + jnp.where(within, 0, LANES)
        for row in range(10):
            coefs[row, :, cells] = jnp.broadcast_to(
                mesh_ref[DOF + 3 + row : DOF + 4 + row, :], (8, CELLS_DEV)
            )


def block_rate(source, block, places, coefs, stencil, low_half):
    here = lanes_of(block)
    centre = []
    around = []
    for r in range(3):
        rows = slice(8 * r, 8 * r + 8)
        centre.append(source[rows, here])
        around.append(
            jnp.where(low_half, source[rows, lanes_of(block + 1)], source[rows, lanes_of(block - 1)])
        )
    sums = [[None] * 3 for _ in range(3)]
    for e in range(3):
        place = places[e, :, here]
        index = place & (LANES - 1)
        within = place < LANES
        found = [lane_gather(piece, index) for piece in centre + around]
        for r in range(3):
            difference = jnp.where(within, found[r], found[3 + r]) - centre[r]
            for a in range(3):
                term = coefs[3 * a + e, :, here] * difference
                sums[a][r] = term if e == 0 else sums[a][r] + term
    turned = [coefs[9, :, here] * piece for piece in centre]
    stacked = jnp.concatenate(sums[0] + sums[1] + turned + [jnp.zeros((8, LANES), f32)], axis=0)
    high, low = two_terms(stacked)
    mixed = jnp.dot(
        stencil, jnp.concatenate([high, low, high], axis=0), preferred_element_type=f32
    )
    return mixed + jnp.concatenate(sums[2], axis=0)


def march(field, middle, places, coefs, stencil_ref):
    low_half = lax.broadcasted_iota(jnp.int32, (8, LANES), 1) < HALF
    edge = jnp.zeros((ROWS, LANES), f32)
    middle[:, lanes_of(0)] = edge
    middle[:, lanes_of(WINDOW + 1)] = edge

    for first in range(0, PHASE_STEPS, SEGMENT):
        blocks = range(1 + first, 1 + WINDOW - first)

        def step(index, carry):
            stencil = stencil_ref[...]
            for b in blocks:
                rate = block_rate(field, b, places, coefs, stencil, low_half)
                middle[:, lanes_of(b)] = field[:, lanes_of(b)] + rate
            for b in blocks:
                rate = block_rate(middle, b, places, coefs, stencil, low_half)
                here = lanes_of(b)
                field[:, here] = 0.5 * (field[:, here] + middle[:, here] + rate)
            return carry

        lax.fori_loop(0, SEGMENT, step, 0)


def first_phase_kernel(left, centre, right, stencil_ref, out, field, middle, places, coefs):
    packs = (left, centre, right)
    fill_window(packs, packs, field, places, coefs)
    march(field, middle, places, coefs, stencil_ref)
    out[...] = field[:, lanes_of(1 + BLOCKS, BLOCKS)]


def restricted(values, members, restrict_matrix):
    contract = (((1,), (1,)), ((), ()))
    first, rest = two_terms(values)
    second, third = two_terms(values - first.astype(f32))
    totals = jnp.zeros((ROWS, COARSE_DEV), f32)
    for term in (third, second, first):
        totals = totals + lax.dot_general(term, members, contract, preferred_element_type=f32)
    counts = lax.dot_general(
        jnp.ones((16, CELLS_DEV), bf16), members, contract, preferred_element_type=f32
    )[0:1]
    result = jnp.zeros((CDOF, COARSE_DEV), f32)
    for d in range(DOF):
        result = result + restrict_matrix[:, d : d + 1] * totals[d : d + 1, :]
    return result / counts


def in_one_row(coarse):
    return jnp.concatenate([coarse[i : i + 1, :] for i in range(CDOF)], axis=1)


def second_phase_kernel(
    left, centre, right, left_mesh, centre_mesh, right_mesh, stencil_ref, index_ref, matrix_ref,
    out, message, field, middle, places, coefs,
):
    fill_window(
        (left, centre, right), (left_mesh, centre_mesh, right_mesh), field, places, coefs
    )
    march(field, middle, places, coefs, stencil_ref)
    fine = field[:, lanes_of(1 + BLOCKS, BLOCKS)]
    out[...] = fine
    members = (
        lax.broadcasted_iota(jnp.int32, (COARSE_DEV, CELLS_DEV), 0) == index_ref[...]
    ).astype(f32).astype(bf16)
    matrix = matrix_ref[...]
    inside = lax.broadcasted_iota(jnp.int32, (ROWS, CELLS_DEV), 0) < DOF
    start = jnp.where(inside, centre_mesh[0:ROWS, :], 0.0)
    message[0:1, :] = in_one_row(restricted(fine, members, matrix))
    message[1:2, :] = in_one_row(restricted(start, members, matrix))


def coarse_step(vector, blocks, first_lane, last_lane):
    ahead = [[pltpu.roll(piece, 1, axis=1) for piece in pair] for pair in vector]
    behind = [[pltpu.roll(piece, LANES - 1, axis=1) for piece in pair] for pair in vector]
    own = (1.0 - 2.0 * coupling - opposite) / coupling
    other = opposite / coupling
    blended = []
    for i in range(CDOF):
        pair = []
        for h in range(2):
            still = own * vector[i][h] + other * vector[i][1 - h]
            beside = jnp.where(first_lane, ahead[i][1 - h], ahead[i][h]) + jnp.where(
                last_lane, behind[i][1 - h], behind[i][h]
            )
            pair.append(still + beside)
        blended.append(pair)
    return [
        [
            (blocks[i][0][h] * blended[0][h] + blocks[i][1][h] * blended[1][h])
            + (blocks[i][2][h] * blended[2][h] + blocks[i][3][h] * blended[3][h])
            for h in range(2)
        ]
        for i in range(CDOF)
    ]


def chain_kernel(
    where_ref, gathered, inverse_ref, fine_ref, index_ref, matrix_ref, out, ends, jumps, blocks_ref
):
    slice_here = where_ref[0]
    part_here = where_ref[1]
    lane = lax.broadcasted_iota(jnp.int32, (8, LANES), 1)
    first_lane = lane == 0
    last_lane = lane == LANES - 1
    quarter = lax.broadcasted_iota(jnp.int32, (SLICES, LANES), 1) // COARSE_DEV

    def regrouped(kind):
        held = [[jnp.zeros((SLICES, LANES), f32) for _ in range(2)] for _ in range(CDOF)]
        for p in range(PARTS):
            rows = gathered[pl.ds(2 * p + kind, SLICES, stride=2 * PARTS), :]
            for i in range(CDOF):
                by = (p % 4 - i) * COARSE_DEV % LANES
                moved = rows if by == 0 else pltpu.roll(rows, by, axis=1)
                held[i][p // 4] = jnp.where(quarter == p % 4, moved, held[i][p // 4])
        return held

    finish = regrouped(0)
    start = regrouped(1)
    for i in range(CDOF):
        for h in range(2):
            ends[2 * i + h] = finish[i][h]
            jumps[2 * i + h] = start[i][h]
            for j in range(CDOF):
                blocks_ref[i, j, h] = coupling * jnp.broadcast_to(
                    inverse_ref[i, j : j + 1, lanes_of(h)], (8, LANES)
                )
    blocks = [
        [[blocks_ref[i, j, h] for h in range(2)] for j in range(CDOF)] for i in range(CDOF)
    ]
    row = lax.broadcasted_iota(jnp.int32, (8, LANES), 0)

    def jump_group(group, carry):
        rows = pl.ds(pl.multiple_of(group * 8, 8), 8)
        vector = [[jumps[2 * i + h, rows, :] for h in range(2)] for i in range(CDOF)]
        for repeat in range(COARSE_STEPS):
            vector = coarse_step(vector, blocks, first_lane, last_lane)
        kept = (group > 0) | (row > 0)
        for i in range(CDOF):
            for h in range(2):
                jumps[2 * i + h, rows, :] = ends[2 * i + h, rows, :] - jnp.where(
                    kept, vector[i][h], 0.0
                )
        return carry

    lax.fori_loop(0, SLICES // 8, jump_group, 0)

    def row_of(ref, n, i, h):
        return jnp.broadcast_to(ref[2 * i + h, pl.ds(n, 1), :], (8, LANES))

    def link(n, flat):
        vector = [[flat[2 * i + h] for h in range(2)] for i in range(CDOF)]
        for repeat in range(COARSE_STEPS):
            vector = coarse_step(vector, blocks, first_lane, last_lane)
        return tuple(
            vector[i][h] + row_of(jumps, n, i, h) for i in range(CDOF) for h in range(2)
        )

    chain = lax.fori_loop(
        1,
        slice_here + 1,
        link,
        tuple(row_of(jumps, 0, i, h) for i in range(CDOF) for h in range(2)),
    )
    upper = part_here >= PARTS // 2
    spread = jnp.zeros((ROWS, LANES), f32)
    for i in range(CDOF):
        change = [chain[2 * i + h] - row_of(ends, slice_here, i, h) for h in range(2)]
        chosen = jnp.where(upper, change[1], change[0])
        spread = spread + matrix_ref[:, i : i + 1] * jnp.concatenate([chosen] * 3, axis=0)
    members = (
        lax.broadcasted_iota(jnp.int32, (LANES, CELLS_DEV), 0)
        == index_ref[...] + COARSE_DEV * (part_here % 4)
    ).astype(f32).astype(bf16)
    total = fine_ref[...]
    first, rest = two_terms(spread)
    second, third = two_terms(spread - first.astype(f32))
    for term in (third, second, first):
        total = total + jnp.dot(term, members, preferred_element_type=f32)
    out[0] = total[0:DOF]


def march_scratch():
    width = (WINDOW + 2) * LANES
    return [
        pltpu.VMEM((ROWS, width), f32),
        pltpu.VMEM((ROWS, width), f32),
        pltpu.VMEM((3, 8, width), jnp.int32),
        pltpu.VMEM((10, 8, width), f32),
    ]


params = pltpu.CompilerParams(vmem_limit_bytes=32 * 1024 * 1024)


def both_sides(values):
    ring = [(i, (i + 1) % PARTS) for i in range(PARTS)]
    back = [((i + 1) % PARTS, i) for i in range(PARTS)]
    return lax.ppermute(values, "space", ring), lax.ppermute(values, "space", back)


def local(
    states,
    neighbour,
    edge_x,
    edge_y,
    edge_damp,
    coriolis,
    flux_x,
    flux_y,
    rotation,
    restrict_matrix,
    prolong_matrix,
    restrict_index,
    coarse_inverse,
):
    pack = jnp.concatenate(
        [states[0], neighbour.astype(f32), edge_x, edge_y, edge_damp, coriolis[None, :]], axis=0
    )
    left, right = both_sides(pack)
    wide = [jnp.pad(m, ((0, ROWS - DOF), (0, ROWS - DOF))) for m in (flux_x, flux_y, rotation)]
    stencil = jnp.concatenate(wide + [jnp.zeros((ROWS, 8), f32)], axis=1)
    high = stencil.astype(bf16)
    low = (stencil - lax.reduce_precision(stencil, 8, 7)).astype(bf16)
    stencil_terms = jnp.concatenate([high, high, low], axis=1)
    index_row = restrict_index[None, :]

    half = pl.pallas_call(
        first_phase_kernel,
        out_shape=jax.ShapeDtypeStruct((ROWS, CELLS_DEV), f32),
        in_specs=[vmem] * 4,
        out_specs=vmem,
        scratch_shapes=march_scratch(),
        compiler_params=params,
    )(left, pack, right, stencil_terms)
    half_left, half_right = both_sides(half)
    fine, message = pl.pallas_call(
        second_phase_kernel,
        out_shape=(
            jax.ShapeDtypeStruct((ROWS, CELLS_DEV), f32),
            jax.ShapeDtypeStruct((2, LANES), f32),
        ),
        in_specs=[vmem] * 9,
        out_specs=(vmem, vmem),
        scratch_shapes=march_scratch(),
        compiler_params=params,
    )(half_left, half, half_right, left, pack, right, stencil_terms, index_row, restrict_matrix)

    copies = jnp.broadcast_to(message, (SLICES * PARTS, 2, LANES))
    gathered = lax.all_to_all(copies, ("tm", "space"), 0, 0, tiled=True)
    gathered = gathered.reshape(SLICES * PARTS * 2, LANES)
    where = jnp.stack([lax.axis_index("tm"), lax.axis_index("space")]).astype(jnp.int32)
    spread_matrix = jnp.pad(prolong_matrix, ((0, ROWS - DOF), (0, 0)))
    return pl.pallas_call(
        chain_kernel,
        out_shape=jax.ShapeDtypeStruct((1, DOF, CELLS_DEV), f32),
        in_specs=[pl.BlockSpec(memory_space=pltpu.SMEM)] + [vmem] * 5,
        out_specs=vmem,
        scratch_shapes=[
            pltpu.VMEM((2 * CDOF, SLICES, LANES), f32),
            pltpu.VMEM((2 * CDOF, SLICES, LANES), f32),
            pltpu.VMEM((CDOF, CDOF, 2, 8, LANES), f32),
        ],
        compiler_params=params,
    )(where, gathered, coarse_inverse, fine, index_row, spread_matrix)


def solution(mesh):
    in_specs = (
        P("tm", None, "space"),
        P(None, "space"),
        P(None, "space"),
        P(None, "space"),
        P(None, "space"),
        P("space"),
        P(),
        P(),
        P(),
        P(),
        P(),
        P("space"),
        P(),
    )
    out_specs = P("tm", None, "space")
    return jax.shard_map(local, mesh=mesh, in_specs=in_specs, out_specs=out_specs, check_vma=False)
```

time: 1260 us -> 114 us (0.09)
  the two profiles are of different devices: /device:TPU:32 before, /device:TPU:63 now
where the time goes in v1:
time: 114 us; the launch traced here: 113 us
  Pallas kernels  49.2 us (43%)
  starting transfers between devices  37.6 us (33%)
  waiting for transfers between devices  21.8 us (19%)
  local copies, waits for them, and re-layouts  4.39 us (4%)
    pallas_call x1, Pallas kernels, local(): pl.pallas_call(chain_kernel, out_shape=jax.ShapeDtypeStruct((1, DOF, CELL...  27.2 us
    all_to_all x1, starting transfers between devices, local(): gathered = lax.all_to_all(copies, ('tm', 'space'), 0, 0, tiled=True)  17.8 us
    all_to_all x1, waiting for transfers between devices, local(): gathered = lax.all_to_all(copies, ('tm', 'space'), 0, 0, tiled=True)  17.6 us
    ppermute x2, starting transfers between devices, both_sides(): lax.ppermute(values, 'space', back)  13.9 us
    pallas_call x1, Pallas kernels, local(): pl.pallas_call(second_phase_kernel, out_shape=(jax.ShapeDtypeStruct((ROWS...  11.1 us
    pallas_call x1, Pallas kernels, local(): pl.pallas_call(first_phase_kernel, out_shape=jax.ShapeDtypeStruct((ROWS,...  10.8 us
    ppermute x2, starting transfers between devices, both_sides(): lax.ppermute(values, 'space', ring)  5.92 us
    unnamed x26, local copies, waits for them, and re-layouts  2.44 us
  transfers between devices with their start and end apart: 5, of which 5 were waited for; matrix products, arithmetic and copies ran while one was open for 0% of the time, Pallas kernels for 0%

profile of v1, /device:TPU:63, one launch (start us, length us, event | category | flops | bytes accessed | tf_op | source)
XLA Modules:
  0.0 113.4 jit_solution(17407585764313761477)
XLA Ops:
  0.0 0.0 copy-start.3
  0.0 0.0 copy-start.6
  0.0 0.0 copy-start.10
  0.0 0.9 copy.18
  1.0 0.0 copy-done.3
  1.0 0.0 copy-start.4
  1.0 0.0 copy-start.5
  1.0 0.0 copy-done.6
  1.0 0.0 copy-done.10
  1.0 0.7 copy-done.4
  1.7 0.0 copy-done.5
  1.7 0.0 copy-start.7
  1.7 0.0 copy-start.8
  1.7 0.0 copy-start.9
  1.7 0.2 concatenate.9.centre.centre_mesh
  1.9 4.0 %collective-permute-start = (f32[34,1024]{1,0:T(8,128)S(1)}, f32[34,1024]{1,0:T(8,128)S(1)}, u32[]{:S(2)}, u32[]{:S(2)}) collective-permute-start(f32[34,1024]{1,0:T(8,128)S(1)} %concatenate.9.centre.centre_mesh), channel_id=1, source_target_pairs={{0,1},{1,2},{2,3},{3,4},{4,5},{5,6},{6,7},{7,0},{8,9},{9,10},{10,1... | collective-permute-start | bytes 417800 | tf_op jit(solution)/shard_map/ppermute | solution.py:301
  5.9 8.6 %collective-permute-start.1 = (f32[34,1024]{1,0:T(8,128)S(1)}, f32[34,1024]{1,0:T(8,128)S(1)}, u32[]{:S(2)}, u32[]{:S(2)}) collective-permute-start(f32[34,1024]{1,0:T(8,128)S(1)} %concatenate.9.centre.centre_mesh), channel_id=1, source_target_pairs={{1,0},{2,1},{3,2},{4,3},{5,4},{6,5},{7,6},{0,7},{9,8},{10,9},{11,1... | collective-permute-start | bytes 417800 | tf_op jit(solution)/shard_map/ppermute | solution.py:301
  14.5 0.1 pad.24.clone
  14.6 0.0 copy-done.7
  14.6 0.0 copy-done.8
  14.6 0.0 copy-done.9
  14.6 0.1 fusion.4
  14.7 0.1 pad_maximum_fusion.stencil_ref
  14.8 1.7 %collective-permute-done.left.left_mesh = f32[34,1024]{1,0:T(8,128)S(1)} collective-permute-done((f32[34,1024]{1,0:T(8,128)S(1)}, f32[34,1024]{1,0:T(8,128)S(1)}, u32[]{:S(2)}, u32[]{:S(2)}) %collective-permute-start) | collective-permute-done | bytes 139296 | tf_op jit(solution)/shard_map/ppermute | solution.py:301
  16.5 0.9 collective-permute-done.1.right.right_mesh
  17.3 0.0 copy-start
  17.4 0.0 copy-start.2
  17.4 10.8 %shard_map.127.centre = f32[24,1024]{1,0:T(8,128)S(1)} custom-call(f32[34,1024]{1,0:T(8,128)S(1)} %collective-permute-done.left.left_mesh, f32[34,1024]{1,0:T(8,128)S(1)} %concatenate.9.centre.centre_mesh, f32[34,1024]{1,0:T(8,128)S(1)} %collective-permute-done.1.right.right_mesh, bf16[24,240]{1,0:T(8,128)(2,1)S(1)} %pad_maximum_fusion.stencil_ref), custom_call_target="tpu_custom_call" | custom-call | tf_op jit(solution)/shard_map/pallas_call | solution.py:330
  28.2 1.9 %collective-permute-start.2 = (f32[24,1024]{1,0:T(8,128)S(1)}, f32[24,1024]{1,0:T(8,128)S(1)}, u32[]{:S(2)}, u32[]{:S(2)}) collective-permute-start(f32[24,1024]{1,0:T(8,128)S(1)} %shard_map.127.centre), channel_id=1, source_target_pairs={{0,1},{1,2},{2,3},{3,4},{4,5},{5,6},{6,7},{7,0},{8,9},{9,10},{10,1... | collective-permute-start | bytes 294920 | tf_op jit(solution)/shard_map/ppermute | solution.py:301
  30.1 5.3 %collective-permute-start.3 = (f32[24,1024]{1,0:T(8,128)S(1)}, f32[24,1024]{1,0:T(8,128)S(1)}, u32[]{:S(2)}, u32[]{:S(2)}) collective-permute-start(f32[24,1024]{1,0:T(8,128)S(1)} %shard_map.127.centre), channel_id=1, source_target_pairs={{1,0},{2,1},{3,2},{4,3},{5,4},{6,5},{7,6},{0,7},{9,8},{10,9},{11,1... | collective-permute-start | bytes 294920 | tf_op jit(solution)/shard_map/ppermute | solution.py:301
  35.4 0.1 collective-permute-done.2.left
  35.5 1.6 %collective-permute-done.3.right = f32[24,1024]{1,0:T(8,128)S(1)} collective-permute-done((f32[24,1024]{1,0:T(8,128)S(1)}, f32[24,1024]{1,0:T(8,128)S(1)}, u32[]{:S(2)}, u32[]{:S(2)}) %collective-permute-start.3) | collective-permute-done | bytes 98336 | tf_op jit(solution)/shard_map/ppermute | solution.py:301
  37.0 0.0 copy-done
  37.0 0.0 copy-done.2
  37.0 11.1 %shard_map.128 = (f32[24,1024]{1,0:T(8,128)S(1)}, f32[2,128]{1,0:T(2,128)S(1)}) custom-call(f32[24,1024]{1,0:T(8,128)S(1)} %collective-permute-done.2.left, f32[24,1024]{1,0:T(8,128)S(1)} %shard_map.127.centre, f32[24,1024]{1,0:T(8,128)S(1)} %collective-permute-done.3.right, f32[34,1024]{1,0:T(8,128)S(1)} %collective-permute-done.left.left_mesh, ...), custom_call_target="tpu_custom_call" | custom-call | tf_op jit(solution)/shard_map/pallas_call | solution.py:339
  48.2 0.9 broadcast_in_dim.15
  49.1 17.8 %all-to-all-start = ((f32[512,2,128]{2,1,0:T(2,128)}), f32[512,2,128]{2,1,0:T(2,128)S(1)}, u32[]{:S(2)}, u32[]{:S(2)}) async-start(f32[512,2,128]{2,1,0:T(2,128)} %broadcast_in_dim.15), calls=%async_computation | async-start | bytes 1048576 | tf_op jit(solution)/shard_map/all_to_all | solution.py:352
  67.0 0.0 copy-start.11
  67.0 0.7 copy-done.11
  67.7 0.1 copy.14
  67.8 0.0 copy-start.1
  67.8 0.1 pad_add_fusion.where_ref
  67.8 17.6 %all-to-all-done = f32[512,2,128]{2,1,0:T(2,128)S(1)} async-done(((f32[512,2,128]{2,1,0:T(2,128)}), f32[512,2,128]{2,1,0:T(2,128)S(1)}, u32[]{:S(2)}, u32[]{:S(2)}) %all-to-all-start) | async-done | bytes 524320 | tf_op jit(solution)/shard_map/all_to_all | solution.py:352
  85.4 0.0 copy-done.1
  85.4 27.2 %shard_map.129 = f32[1,21,1024]{2,1,0:T(8,128)S(1)} custom-call(s32[2]{0:T(128)S(1)} %pad_add_fusion.where_ref, f32[1024,128]{1,0:T(8,128)S(1)} %bitcast.8, f32[4,4,256]{2,1,0:T(4,128)S(1)} %copy-done.1, f32[24,1024]{1,0:T(8,128)S(1)} %get-tuple-element.8.fine_ref, s32[1,1024]{1,0:T(1,128)S(1)} %bitcast.10, f32[24,4]{1,0:T(8,128)S(1)} %pad.17.matrix_ref), custom_call_target="tpu_custom_call" | custom-call | tf_op jit(solution)/shard_map/pallas_call | solution.py:356
  112.6 0.7 copy.15
  (4 shorter events, 0.0 us)
Async XLA Ops:
  0.0 1.0 copy-start.3
  0.0 1.0 copy-start.6
  0.0 1.0 copy-start.10
  1.0 0.7 copy-start.4
  1.0 0.7 copy-start.5
  1.7 12.9 %copy-start.7 = (f32[21,21]{1,0:T(8,128)S(1)}, f32[21,21]{1,0:T(8,128)}, u32[]{:S(2)}) copy-start(f32[21,21]{1,0:T(8,128)} %param.21) | copy-start | bytes 5296
  1.7 12.9 %copy-start.8 = (f32[21,21]{1,0:T(8,128)S(1)}, f32[21,21]{1,0:T(8,128)}, u32[]{:S(2)}) copy-start(f32[21,21]{1,0:T(8,128)} %param.20) | copy-start | bytes 5296
  1.7 12.9 %copy-start.9 = (f32[21,21]{1,0:T(8,128)S(1)}, f32[21,21]{1,0:T(8,128)}, u32[]{:S(2)}) copy-start(f32[21,21]{1,0:T(8,128)} %param.19) | copy-start | bytes 5296
  1.9 14.6 %collective-permute-start = (f32[34,1024]{1,0:T(8,128)S(1)}, f32[34,1024]{1,0:T(8,128)S(1)}, u32[]{:S(2)}, u32[]{:S(2)}) collective-permute-start(f32[34,1024]{1,0:T(8,128)S(1)} %concatenate.9.centre.centre_mesh), channel_id=1, source_target_pairs={{0,1},{1,2},{2,3},{3,4},{4,5},{5,6},{6,7},{7,0},{8,9},{9,10},{10,1... | collective-permute-start | bytes 417800 | tf_op jit(solution)/shard_map/ppermute | solution.py:301
  5.9 11.4 %collective-permute-start.1 = (f32[34,1024]{1,0:T(8,128)S(1)}, f32[34,1024]{1,0:T(8,128)S(1)}, u32[]{:S(2)}, u32[]{:S(2)}) collective-permute-start(f32[34,1024]{1,0:T(8,128)S(1)} %concatenate.9.centre.centre_mesh), channel_id=1, source_target_pairs={{1,0},{2,1},{3,2},{4,3},{5,4},{6,5},{7,6},{0,7},{9,8},{10,9},{11,1... | collective-permute-start | bytes 417800 | tf_op jit(solution)/shard_map/ppermute | solution.py:301
  17.3 19.7 %copy-start = (s32[1024]{0:T(1024)S(1)}, s32[1024]{0:T(1024)}, u32[]{:S(2)}) copy-start(s32[1024]{0:T(1024)} %param.24) | copy-start | bytes 12292
  17.4 19.7 %copy-start.2 = (f32[4,21]{1,0:T(4,128)S(1)}, f32[4,21]{1,0:T(4,128)}, u32[]{:S(2)}) copy-start(f32[4,21]{1,0:T(4,128)} %matrix_ref.1) | copy-start | bytes 1012
  28.2 7.3 %collective-permute-start.2 = (f32[24,1024]{1,0:T(8,128)S(1)}, f32[24,1024]{1,0:T(8,128)S(1)}, u32[]{:S(2)}, u32[]{:S(2)}) collective-permute-start(f32[24,1024]{1,0:T(8,128)S(1)} %shard_map.127.centre), channel_id=1, source_target_pairs={{0,1},{1,2},{2,3},{3,4},{4,5},{5,6},{6,7},{7,0},{8,9},{9,10},{10,1... | collective-permute-start | bytes 294920 | tf_op jit(solution)/shard_map/ppermute | solution.py:301
  30.1 6.9 %collective-permute-start.3 = (f32[24,1024]{1,0:T(8,128)S(1)}, f32[24,1024]{1,0:T(8,128)S(1)}, u32[]{:S(2)}, u32[]{:S(2)}) collective-permute-start(f32[24,1024]{1,0:T(8,128)S(1)} %shard_map.127.centre), channel_id=1, source_target_pairs={{1,0},{2,1},{3,2},{4,3},{5,4},{6,5},{7,6},{0,7},{9,8},{10,9},{11,1... | collective-permute-start | bytes 294920 | tf_op jit(solution)/shard_map/ppermute | solution.py:301
  49.1 36.3 %all-to-all-start = ((f32[512,2,128]{2,1,0:T(2,128)}), f32[512,2,128]{2,1,0:T(2,128)S(1)}, u32[]{:S(2)}, u32[]{:S(2)}) async-start(f32[512,2,128]{2,1,0:T(2,128)} %broadcast_in_dim.15), calls=%async_computation | async-start | bytes 1048576 | tf_op jit(solution)/shard_map/all_to_all | solution.py:352
  67.0 0.7 copy-start.11
  67.8 17.7 %copy-start.1 = (f32[4,4,256]{2,1,0:T(4,128)S(1)}, f32[4,4,256]{2,1,0:T(4,128)}, u32[]{:S(2)}) copy-start(f32[4,4,256]{2,1,0:T(4,128)} %inverse_ref.1) | copy-start | bytes 49156

commit v2 on v1

--- a/solution.py
+++ b/solution.py
@@ -17,6 +17,8 @@
 COARSE_STEPS = 4
 PARTS = 8
 SLICES = 64
+GROUP = 8
+GROUPS = SLICES // GROUP
 BLOCKS = CELLS_DEV // LANES
 PHASE_STEPS = 8
 SEGMENT = 2
@@ -168,118 +170,145 @@
     matrix = matrix_ref[...]
     inside = lax.broadcasted_iota(jnp.int32, (ROWS, CELLS_DEV), 0) < DOF
     start = jnp.where(inside, centre_mesh[0:ROWS, :], 0.0)
-    message[0:1, :] = in_one_row(restricted(fine, members, matrix))
-    message[1:2, :] = in_one_row(restricted(start, members, matrix))
-
-
-def coarse_step(vector, blocks, first_lane, last_lane):
-    ahead = [[pltpu.roll(piece, 1, axis=1) for piece in pair] for pair in vector]
-    behind = [[pltpu.roll(piece, LANES - 1, axis=1) for piece in pair] for pair in vector]
-    own = (1.0 - 2.0 * coupling - opposite) / coupling
-    other = opposite / coupling
-    blended = []
-    for i in range(CDOF):
-        pair = []
-        for h in range(2):
-            still = own * vector[i][h] + other * vector[i][1 - h]
-            beside = jnp.where(first_lane, ahead[i][1 - h], ahead[i][h]) + jnp.where(
-                last_lane, behind[i][1 - h], behind[i][h]
-            )
-            pair.append(still + beside)
-        blended.append(pair)
-    return [
-        [
-            (blocks[i][0][h] * blended[0][h] + blocks[i][1][h] * blended[1][h])
-            + (blocks[i][2][h] * blended[2][h] + blocks[i][3][h] * blended[3][h])
-            for h in range(2)
-        ]
-        for i in range(CDOF)
-    ]
-
-
-def chain_kernel(
-    where_ref, gathered, inverse_ref, fine_ref, index_ref, matrix_ref, out, ends, jumps, blocks_ref
-):
-    slice_here = where_ref[0]
-    part_here = where_ref[1]
-    lane = lax.broadcasted_iota(jnp.int32, (8, LANES), 1)
+    rows = jnp.concatenate(
+        [in_one_row(restricted(fine, members, matrix)), in_one_row(restricted(start, members, matrix))],
+        axis=0,
+    )
+    for copy in range(GROUP * PARTS):
+        message[copy] = rows
+
+
+def flipped(tiles, even_row):
+    up = pltpu.roll(jnp.concatenate([tiles[1:], tiles[:1]], axis=0), 7, axis=1)
+    down = pltpu.roll(jnp.concatenate([tiles[7:], tiles[:7]], axis=0), 1, axis=1)
+    return jnp.where(even_row, up, down)
+
+
+def compose_kernel(inverse_ref, out):
+    shape = (8, 8, LANES)
+    row = lax.broadcasted_iota(jnp.int32, shape, 1)
+    lane = lax.broadcasted_iota(jnp.int32, shape, 2)
+    turn = lax.broadcasted_iota(jnp.int32, shape, 0)
+    even_row = row % 2 == 0
     first_lane = lane == 0
     last_lane = lane == LANES - 1
-    quarter = lax.broadcasted_iota(jnp.int32, (SLICES, LANES), 1) // COARSE_DEV
-
-    def regrouped(kind):
-        held = [[jnp.zeros((SLICES, LANES), f32) for _ in range(2)] for _ in range(CDOF)]
-        for p in range(PARTS):
-            rows = gathered[pl.ds(2 * p + kind, SLICES, stride=2 * PARTS), :]
-            for i in range(CDOF):
-                by = (p % 4 - i) * COARSE_DEV % LANES
-                moved = rows if by == 0 else pltpu.roll(rows, by, axis=1)
-                held[i][p // 4] = jnp.where(quarter == p % 4, moved, held[i][p // 4])
-        return held
-
-    finish = regrouped(0)
-    start = regrouped(1)
-    for i in range(CDOF):
-        for h in range(2):
-            ends[2 * i + h] = finish[i][h]
-            jumps[2 * i + h] = start[i][h]
-            for j in range(CDOF):
-                blocks_ref[i, j, h] = coupling * jnp.broadcast_to(
-                    inverse_ref[i, j : j + 1, lanes_of(h)], (8, LANES)
-                )
-    blocks = [
-        [[blocks_ref[i, j, h] for h in range(2)] for j in range(CDOF)] for i in range(CDOF)
-    ]
-    row = lax.broadcasted_iota(jnp.int32, (8, LANES), 0)
-
-    def jump_group(group, carry):
-        rows = pl.ds(pl.multiple_of(group * 8, 8), 8)
-        vector = [[jumps[2 * i + h, rows, :] for h in range(2)] for i in range(CDOF)]
-        for repeat in range(COARSE_STEPS):
-            vector = coarse_step(vector, blocks, first_lane, last_lane)
-        kept = (group > 0) | (row > 0)
+    own = 1.0 - 2.0 * coupling - opposite
+    blocks = []
+    for by in range(CDOF):
+        pieces = []
+        for i in range(CDOF):
+            j = (i - by) % CDOF
+            for h in range(2):
+                pieces.append(inverse_ref[i, j : j + 1, lanes_of(h)])
+        blocks.append(jnp.concatenate(pieces, axis=0)[None])
+    reach = {0: jnp.where(turn == 0, 1.0, 0.0)}
+    for repeat in range(COARSE_STEPS):
+        swapped = {o: flipped(tiles, even_row) for o, tiles in reach.items()}
+        blended = {}
+        for o in range(-repeat - 1, repeat + 2):
+            total = jnp.zeros(shape, f32)
+            if o in reach:
+                total = own * reach[o] + opposite * swapped[o]
+            if o - 1 in reach:
+                edge = jnp.where(last_lane, swapped[o - 1], reach[o - 1])
+                total = total + coupling * pltpu.roll(edge, 1, axis=2)
+            if o + 1 in reach:
+                edge = jnp.where(first_lane, swapped[o + 1], reach[o + 1])
+                total = total + coupling * pltpu.roll(edge, LANES - 1, axis=2)
+            blended[o] = total
+        reach = {}
+        for o, tiles in blended.items():
+            total = blocks[0] * tiles
+            for by in range(1, CDOF):
+                turned = jnp.concatenate([tiles[8 - 2 * by :], tiles[: 8 - 2 * by]], axis=0)
+                total = total + blocks[by] * pltpu.roll(turned, 2 * by, axis=1)
+            reach[o] = total
+    for o, tiles in reach.items():
+        out[o + COARSE_STEPS] = tiles if o == 0 else pltpu.roll(tiles, -o % LANES, axis=2)
+
+
+def added(terms):
+    while len(terms) > 1:
+        terms = [sum(terms[i : i + 2][1:], terms[i]) for i in range(0, len(terms), 2)]
+    return terms[0]
+
+
+def coarse_slice(vector, operator_ref):
+    turns = [vector] + [pltpu.roll(vector, d, axis=0) for d in range(1, 8)]
+    shares = []
+    for o in range(-COARSE_STEPS, COARSE_STEPS + 1):
+        share = added([operator_ref[o + COARSE_STEPS, d] * turns[d] for d in range(8)])
+        shares.append(share if o == 0 else pltpu.roll(share, o % LANES, axis=1))
+    return added(shares)
+
+
+def group_kernel(where_ref, gathered, operator_ref, ends_out, own_out, finish, start):
+    group = where_ref[0]
+    place = where_ref[1]
+    quarter = lax.broadcasted_iota(jnp.int32, (GROUP, LANES), 1) // COARSE_DEV
+    for kind, ref in enumerate((finish, start)):
         for i in range(CDOF):
             for h in range(2):
-                jumps[2 * i + h, rows, :] = ends[2 * i + h, rows, :] - jnp.where(
-                    kept, vector[i][h], 0.0
-                )
-        return carry
-
-    lax.fori_loop(0, SLICES // 8, jump_group, 0)
-
-    def row_of(ref, n, i, h):
-        return jnp.broadcast_to(ref[2 * i + h, pl.ds(n, 1), :], (8, LANES))
-
-    def link(n, flat):
-        vector = [[flat[2 * i + h] for h in range(2)] for i in range(CDOF)]
-        for repeat in range(COARSE_STEPS):
-            vector = coarse_step(vector, blocks, first_lane, last_lane)
-        return tuple(
-            vector[i][h] + row_of(jumps, n, i, h) for i in range(CDOF) for h in range(2)
-        )
-
-    chain = lax.fori_loop(
-        1,
-        slice_here + 1,
-        link,
-        tuple(row_of(jumps, 0, i, h) for i in range(CDOF) for h in range(2)),
-    )
-    upper = part_here >= PARTS // 2
+                held = jnp.zeros((GROUP, LANES), f32)
+                for q in range(4):
+                    p = 4 * h + q
+                    rows = gathered[pl.ds(2 * p + kind, GROUP, stride=2 * PARTS), :]
+                    by = (q - i) * COARSE_DEV % LANES
+                    moved = rows if by == 0 else pltpu.roll(rows, by, axis=1)
+                    held = jnp.where(quarter == q, moved, held)
+                ref[pl.ds((2 * i + h) * GROUP, GROUP), :] = held
+
+    def of_slice(ref, n):
+        return ref[pl.ds(n, 8, stride=GROUP), :]
+
+    chain = None
+    own = jnp.zeros((8, LANES), f32)
+    for n in range(GROUP):
+        coarse = coarse_slice(of_slice(start, n), operator_ref)
+        if n == 0:
+            coarse = jnp.where(group > 0, coarse, 0.0)
+        jump = of_slice(finish, n) - coarse
+        chain = jump if n == 0 else coarse_slice(chain, operator_ref) + jump
+        own = jnp.where(place == n, chain, own)
+    for copy in range(GROUPS):
+        ends_out[copy] = chain
+    own_out[0] = own
+    own_out[1] = finish[pl.ds(place, 8, stride=GROUP), :]
+
+
+def correct_kernel(
+    where_ref, ends, own_ref, operator_ref, fine_ref, index_ref, matrix_ref, out
+):
+    group = where_ref[0]
+    place = where_ref[1]
+    part = where_ref[2]
+
+    def advance(count, vector):
+        return lax.fori_loop(0, count, lambda n, now: coarse_slice(now, operator_ref), vector)
+
+    def link(k, vector):
+        return advance(GROUP, vector) + ends[k]
+
+    before = lax.fori_loop(1, group, link, ends[0])
+    before = advance(jnp.where(group > 0, place + 1, 0), before)
+    chain = own_ref[0] + jnp.where(group > 0, before, 0.0)
+    change = chain - own_ref[1]
+    upper = part >= PARTS // 2
     spread = jnp.zeros((ROWS, LANES), f32)
     for i in range(CDOF):
-        change = [chain[2 * i + h] - row_of(ends, slice_here, i, h) for h in range(2)]
-        chosen = jnp.where(upper, change[1], change[0])
-        spread = spread + matrix_ref[:, i : i + 1] * jnp.concatenate([chosen] * 3, axis=0)
+        chosen = jnp.where(upper, change[2 * i + 1 : 2 * i + 2], change[2 * i : 2 * i + 1])
+        spread = spread + matrix_ref[:, i : i + 1] * jnp.broadcast_to(chosen, (ROWS, LANES))
     members = (
         lax.broadcasted_iota(jnp.int32, (LANES, CELLS_DEV), 0)
-        == index_ref[...] + COARSE_DEV * (part_here % 4)
+        == index_ref[...] + COARSE_DEV * (part % 4)
     ).astype(f32).astype(bf16)
     total = fine_ref[...]
     first, rest = two_terms(spread)
     second, third = two_terms(spread - first.astype(f32))
     for term in (third, second, first):
         total = total + jnp.dot(term, members, preferred_element_type=f32)
-    out[0] = total[0:DOF]
+    for d in range(DOF):
+        out[d] = total[d : d + 1, :]
 
 
 def march_scratch():
@@ -326,6 +355,14 @@
     low = (stencil - lax.reduce_precision(stencil, 8, 7)).astype(bf16)
     stencil_terms = jnp.concatenate([high, high, low], axis=1)
     index_row = restrict_index[None, :]
+    operator = pl.pallas_call(
+        compose_kernel,
+        out_shape=jax.ShapeDtypeStruct((2 * COARSE_STEPS + 1, 8, 8, LANES), f32),
+        in_specs=[vmem],
+        out_specs=vmem,
+        compiler_params=params,
+        cost_estimate=pl.CostEstimate(flops=4000000, bytes_accessed=300000, transcendentals=0),
+    )(coarse_inverse)
 
     half = pl.pallas_call(
         first_phase_kernel,
@@ -340,7 +377,7 @@
         second_phase_kernel,
         out_shape=(
             jax.ShapeDtypeStruct((ROWS, CELLS_DEV), f32),
-            jax.ShapeDtypeStruct((2, LANES), f32),
+            jax.ShapeDtypeStruct((GROUP * PARTS, 2, LANES), f32),
         ),
         in_specs=[vmem] * 9,
         out_specs=(vmem, vmem),
@@ -348,23 +385,36 @@
         compiler_params=params,
     )(half_left, half, half_right, left, pack, right, stencil_terms, index_row, restrict_matrix)
 
-    copies = jnp.broadcast_to(message, (SLICES * PARTS, 2, LANES))
-    gathered = lax.all_to_all(copies, ("tm", "space"), 0, 0, tiled=True)
-    gathered = gathered.reshape(SLICES * PARTS * 2, LANES)
-    where = jnp.stack([lax.axis_index("tm"), lax.axis_index("space")]).astype(jnp.int32)
+    axes = ("tm", "space")
+    members = GROUP * PARTS
+    inside = [[g * members + m for m in range(members)] for g in range(GROUPS)]
+    across = [[g * members + m for g in range(GROUPS)] for m in range(members)]
+    gathered = lax.all_to_all(message, axes, 0, 0, tiled=True, axis_index_groups=inside)
+    slice_here = lax.axis_index("tm")
+    where = jnp.stack([slice_here // GROUP, slice_here % GROUP, lax.axis_index("space")])
+    where = where.astype(jnp.int32)
+    smem = pl.BlockSpec(memory_space=pltpu.SMEM)
+    ends, own = pl.pallas_call(
+        group_kernel,
+        out_shape=(
+            jax.ShapeDtypeStruct((GROUPS, 8, LANES), f32),
+            jax.ShapeDtypeStruct((2, 8, LANES), f32),
+        ),
+        in_specs=[smem, vmem, vmem],
+        out_specs=(vmem, vmem),
+        scratch_shapes=[pltpu.VMEM((8 * GROUP, LANES), f32)] * 2,
+        compiler_params=params,
+    )(where, gathered.reshape(GROUP * PARTS * 2, LANES), operator)
+    ends = lax.all_to_all(ends, axes, 0, 0, tiled=True, axis_index_groups=across)
     spread_matrix = jnp.pad(prolong_matrix, ((0, ROWS - DOF), (0, 0)))
-    return pl.pallas_call(
-        chain_kernel,
-        out_shape=jax.ShapeDtypeStruct((1, DOF, CELLS_DEV), f32),
-        in_specs=[pl.BlockSpec(memory_space=pltpu.SMEM)] + [vmem] * 5,
+    updated = pl.pallas_call(
+        correct_kernel,
+        out_shape=jax.ShapeDtypeStruct((DOF, 1, CELLS_DEV), f32),
+        in_specs=[smem] + [vmem] * 6,
         out_specs=vmem,
-        scratch_shapes=[
-            pltpu.VMEM((2 * CDOF, SLICES, LANES), f32),
-            pltpu.VMEM((2 * CDOF, SLICES, LANES), f32),
-            pltpu.VMEM((CDOF, CDOF, 2, 8, LANES), f32),
-        ],
         compiler_params=params,
-    )(where, gathered, coarse_inverse, fine, index_row, spread_matrix)
+    )(where, ends, own, operator, fine, index_row, spread_matrix)
+    return updated.transpose(1, 0, 2)
 
 
 def solution(mesh):

time: 114 us -> 90.1 us (0.79)
  the two profiles are of different devices: /device:TPU:63 before, /device:TPU:56 now
where the time goes in v2:
time: 90.1 us; the launch traced here: 89.4 us
  starting transfers between devices  36.2 us (40%)
  Pallas kernels  31.1 us (35%)
  waiting for transfers between devices  19 us (21%)
  local copies, waits for them, and re-layouts  2.73 us (3%)
    ppermute x2, starting transfers between devices, both_sides(): lax.ppermute(values, 'space', back)  14.2 us
    pallas_call x1, Pallas kernels, local(): pl.pallas_call(second_phase_kernel, out_shape=(jax.ShapeDtypeStruct((ROWS...  11.8 us
    pallas_call x1, Pallas kernels, local(): pl.pallas_call(first_phase_kernel, out_shape=jax.ShapeDtypeStruct((ROWS,...  10.8 us
    all_to_all x1, starting transfers between devices, local(): lax.all_to_all(message, axes, 0, 0, tiled=True, axis_index_groups=inside)  8.85 us
    all_to_all x1, waiting for transfers between devices, local(): lax.all_to_all(message, axes, 0, 0, tiled=True, axis_index_groups=inside)  8.53 us
    all_to_all x1, starting transfers between devices, local(): lax.all_to_all(ends, axes, 0, 0, tiled=True, axis_index_groups=across)  7 us
    ppermute x2, starting transfers between devices, both_sides(): lax.ppermute(values, 'space', ring)  6.2 us
    pallas_call x1, Pallas kernels, local(): pl.pallas_call(correct_kernel, out_shape=jax.ShapeDtypeStruct((DOF, 1, CE...  5.88 us
  transfers between devices with their start and end apart: 6, of which 6 were waited for; matrix products, arithmetic and copies ran while one was open for 0% of the time, Pallas kernels for 1%

profile of v2, /device:TPU:56, one launch (start us, length us, event | category | flops | bytes accessed | tf_op | source)
XLA Modules:
  0.0 89.4 jit_solution(9303514269259821788)
XLA Ops:
  0.0 0.0 copy-start.3
  0.0 0.0 copy-start.6
  0.0 0.0 copy-start.10
  0.0 0.9 %copy.17 = f32[1,21,1024]{2,1,0:T(8,128)S(1)} copy(f32[1,21,1024]{2,0,1:T(1,128)} %param.13) | data formatting | bytes 172032
  1.0 0.0 copy-done.3
  1.0 0.0 copy-start.4
  1.0 0.0 copy-start.5
  1.0 0.0 copy-done.6
  1.0 0.0 copy-done.10
  1.0 0.7 copy-done.4
  1.7 0.0 copy-done.5
  1.7 0.0 copy-start.7
  1.7 0.0 copy-start.8
  1.7 0.0 copy-start.9
  1.7 0.2 concatenate.9.centre.centre_mesh
  1.9 4.3 %collective-permute-start = (f32[34,1024]{1,0:T(8,128)S(1)}, f32[34,1024]{1,0:T(8,128)S(1)}, u32[]{:S(2)}, u32[]{:S(2)}) collective-permute-start(f32[34,1024]{1,0:T(8,128)S(1)} %concatenate.9.centre.centre_mesh), channel_id=1, source_target_pairs={{0,1},{1,2},{2,3},{3,4},{4,5},{5,6},{6,7},{7,0},{8,9},{9,10},{10,1... | collective-permute-start | bytes 417800 | tf_op jit(solution)/shard_map/ppermute | solution.py:330
  6.2 8.6 %collective-permute-start.1 = (f32[34,1024]{1,0:T(8,128)S(1)}, f32[34,1024]{1,0:T(8,128)S(1)}, u32[]{:S(2)}, u32[]{:S(2)}) collective-permute-start(f32[34,1024]{1,0:T(8,128)S(1)} %concatenate.9.centre.centre_mesh), channel_id=1, source_target_pairs={{1,0},{2,1},{3,2},{4,3},{5,4},{6,5},{7,6},{0,7},{9,8},{10,9},{11,1... | collective-permute-start | bytes 417800 | tf_op jit(solution)/shard_map/ppermute | solution.py:330
  14.8 0.1 pad.24.clone
  14.9 0.0 copy-done.7
  14.9 0.0 copy-done.8
  14.9 0.0 copy-done.9
  14.9 0.1 fusion.4
  15.0 0.1 pad_maximum_fusion.stencil_ref
  15.0 2.0 %collective-permute-done.left.left_mesh = f32[34,1024]{1,0:T(8,128)S(1)} collective-permute-done((f32[34,1024]{1,0:T(8,128)S(1)}, f32[34,1024]{1,0:T(8,128)S(1)}, u32[]{:S(2)}, u32[]{:S(2)}) %collective-permute-start) | collective-permute-done | bytes 139296 | tf_op jit(solution)/shard_map/ppermute | solution.py:330
  17.0 1.2 %collective-permute-done.1.right.right_mesh = f32[34,1024]{1,0:T(8,128)S(1)} collective-permute-done((f32[34,1024]{1,0:T(8,128)S(1)}, f32[34,1024]{1,0:T(8,128)S(1)}, u32[]{:S(2)}, u32[]{:S(2)}) %collective-permute-start.1) | collective-permute-done | bytes 139296 | tf_op jit(solution)/shard_map/ppermute | solution.py:330
  18.2 0.0 copy-start
  18.2 0.0 copy-start.2
  18.2 10.8 %shard_map.127.centre = f32[24,1024]{1,0:T(8,128)S(1)} custom-call(f32[34,1024]{1,0:T(8,128)S(1)} %collective-permute-done.left.left_mesh, f32[34,1024]{1,0:T(8,128)S(1)} %concatenate.9.centre.centre_mesh, f32[34,1024]{1,0:T(8,128)S(1)} %collective-permute-done.1.right.right_mesh, bf16[24,240]{1,0:T(8,128)(2,1)S(1)} %pad_maximum_fusion.stencil_ref), custom_call_target="tpu_custom_call" | custom-call | tf_op jit(solution)/shard_map/pallas_call | solution.py:367
  29.0 1.9 %collective-permute-start.2 = (f32[24,1024]{1,0:T(8,128)S(1)}, f32[24,1024]{1,0:T(8,128)S(1)}, u32[]{:S(2)}, u32[]{:S(2)}) collective-permute-start(f32[24,1024]{1,0:T(8,128)S(1)} %shard_map.127.centre), channel_id=1, source_target_pairs={{0,1},{1,2},{2,3},{3,4},{4,5},{5,6},{6,7},{7,0},{8,9},{9,10},{10,1... | collective-permute-start | bytes 294920 | tf_op jit(solution)/shard_map/ppermute | solution.py:330
  31.0 5.6 %collective-permute-start.3 = (f32[24,1024]{1,0:T(8,128)S(1)}, f32[24,1024]{1,0:T(8,128)S(1)}, u32[]{:S(2)}, u32[]{:S(2)}) collective-permute-start(f32[24,1024]{1,0:T(8,128)S(1)} %shard_map.127.centre), channel_id=1, source_target_pairs={{1,0},{2,1},{3,2},{4,3},{5,4},{6,5},{7,6},{0,7},{9,8},{10,9},{11,1... | collective-permute-start | bytes 294920 | tf_op jit(solution)/shard_map/ppermute | solution.py:330
  36.6 0.7 collective-permute-done.2.left
  37.2 1.5 %collective-permute-done.3.right = f32[24,1024]{1,0:T(8,128)S(1)} collective-permute-done((f32[24,1024]{1,0:T(8,128)S(1)}, f32[24,1024]{1,0:T(8,128)S(1)}, u32[]{:S(2)}, u32[]{:S(2)}) %collective-permute-start.3) | collective-permute-done | bytes 98336 | tf_op jit(solution)/shard_map/ppermute | solution.py:330
  38.8 0.0 copy-done
  38.8 0.0 copy-done.2
  38.8 11.8 %shard_map.128 = (f32[24,1024]{1,0:T(8,128)S(1)}, f32[64,2,128]{2,1,0:T(2,128)}) custom-call(f32[24,1024]{1,0:T(8,128)S(1)} %collective-permute-done.2.left, f32[24,1024]{1,0:T(8,128)S(1)} %shard_map.127.centre, f32[24,1024]{1,0:T(8,128)S(1)} %collective-permute-done.3.right, f32[34,1024]{1,0:T(8,128)S(1)} %collective-permute-done.left.left_mesh, ...), custom_call_target="tpu_custom_call" | custom-call | tf_op jit(solution)/shard_map/pallas_call | solution.py:376
  50.6 8.9 %all-to-all-start = ((f32[64,2,128]{2,1,0:T(2,128)}), f32[64,2,128]{2,1,0:T(2,128)S(1)}, u32[]{:S(2)}, u32[]{:S(2)}) async-start(f32[64,2,128]{2,1,0:T(2,128)} %get-tuple-element.9), calls=%async_computation | async-start | bytes 131072 | tf_op jit(solution)/shard_map/all_to_all | solution.py:392
  59.4 0.0 copy-start.1
  59.5 0.7 copy-done.1
  60.2 0.6 shard_map.129.operator_ref
  60.8 0.1 pad_add_fusion.where_ref
  60.9 8.5 %all-to-all-done = f32[64,2,128]{2,1,0:T(2,128)S(1)} async-done(((f32[64,2,128]{2,1,0:T(2,128)}), f32[64,2,128]{2,1,0:T(2,128)S(1)}, u32[]{:S(2)}, u32[]{:S(2)}) %all-to-all-start) | async-done | bytes 65568 | tf_op jit(solution)/shard_map/all_to_all | solution.py:392
  69.4 2.0 %shard_map.130 = (f32[8,8,128]{2,1,0:T(8,128)}, f32[2,8,128]{2,1,0:T(8,128)S(1)}) custom-call(s32[3]{0:T(128)S(1)} %pad_add_fusion.where_ref, f32[128,128]{1,0:T(8,128)S(1)} %bitcast.10, f32[9,8,8,128]{3,2,1,0:T(8,128)S(1)} %shard_map.129.operator_ref), custom_call_target="tpu_custom_call" | custom-call | tf_op jit(solution)/shard_map/pallas_call | solution.py:397
  71.4 0.0 copy-start.11
  71.4 7.0 %all-to-all-start.1 = ((f32[8,8,128]{2,1,0:T(8,128)}), f32[8,8,128]{2,1,0:T(8,128)S(1)}, u32[]{:S(2)}, u32[]{:S(2)}) async-start(f32[8,8,128]{2,1,0:T(8,128)} %get-tuple-element.10), calls=%async_computation.1 | async-start | bytes 65536 | tf_op jit(solution)/shard_map/all_to_all | solution.py:408
  78.4 0.0 copy-done.11
  78.4 0.1 copy.14
  78.5 5.1 %all-to-all-done.1.ends = f32[8,8,128]{2,1,0:T(8,128)S(1)} async-done(((f32[8,8,128]{2,1,0:T(8,128)}), f32[8,8,128]{2,1,0:T(8,128)S(1)}, u32[]{:S(2)}, u32[]{:S(2)}) %all-to-all-start.1) | async-done | bytes 32800 | tf_op jit(solution)/shard_map/all_to_all | solution.py:408
  83.6 5.9 %shard_map.131 = f32[21,1,1024]{2,1,0:T(1,128)} custom-call(s32[3]{0:T(128)S(1)} %pad_add_fusion.where_ref, f32[8,8,128]{2,1,0:T(8,128)S(1)} %all-to-all-done.1.ends, f32[2,8,128]{2,1,0:T(8,128)S(1)} %get-tuple-element.11.own_ref, f32[9,8,8,128]{3,2,1,0:T(8,128)S(1)} %shard_map.129.operator_ref, f32[24,1024]{1,0:T(8,128)S(1)} %get-tuple-element.12.fine_ref, ...), custom_call_target="tpu_custom_call" | custom-call | tf_op jit(solution)/shard_map/pallas_call | solution.py:410
  (4 shorter events, 0.0 us)
Async XLA Ops:
  0.0 1.0 %copy-start.3 = (s32[3,1024]{1,0:T(4,128)S(1)}, s32[3,1024]{1,0:T(4,128)}, u32[]{:S(2)}) copy-start(s32[3,1024]{1,0:T(4,128)} %param.14) | copy-start | bytes 36868
  0.0 1.0 %copy-start.6 = (f32[3,1024]{1,0:T(4,128)S(1)}, f32[3,1024]{1,0:T(4,128)}, u32[]{:S(2)}) copy-start(f32[3,1024]{1,0:T(4,128)} %param.17) | copy-start | bytes 36868
  0.0 1.0 %copy-start.10 = (f32[1024]{0:T(1024)S(1)}, f32[1024]{0:T(1024)}, u32[]{:S(2)}) copy-start(f32[1024]{0:T(1024)} %param.18) | copy-start | bytes 12292
  1.0 0.7 copy-start.4
  1.0 0.7 copy-start.5
  1.7 13.2 %copy-start.7 = (f32[21,21]{1,0:T(8,128)S(1)}, f32[21,21]{1,0:T(8,128)}, u32[]{:S(2)}) copy-start(f32[21,21]{1,0:T(8,128)} %param.21) | copy-start | bytes 5296
  1.7 13.2 %copy-start.8 = (f32[21,21]{1,0:T(8,128)S(1)}, f32[21,21]{1,0:T(8,128)}, u32[]{:S(2)}) copy-start(f32[21,21]{1,0:T(8,128)} %param.20) | copy-start | bytes 5296
  1.7 13.2 %copy-start.9 = (f32[21,21]{1,0:T(8,128)S(1)}, f32[21,21]{1,0:T(8,128)}, u32[]{:S(2)}) copy-start(f32[21,21]{1,0:T(8,128)} %param.19) | copy-start | bytes 5296
  1.9 15.1 %collective-permute-start = (f32[34,1024]{1,0:T(8,128)S(1)}, f32[34,1024]{1,0:T(8,128)S(1)}, u32[]{:S(2)}, u32[]{:S(2)}) collective-permute-start(f32[34,1024]{1,0:T(8,128)S(1)} %concatenate.9.centre.centre_mesh), channel_id=1, source_target_pairs={{0,1},{1,2},{2,3},{3,4},{4,5},{5,6},{6,7},{7,0},{8,9},{9,10},{10,1... | collective-permute-start | bytes 417800 | tf_op jit(solution)/shard_map/ppermute | solution.py:330
  6.2 12.0 %collective-permute-start.1 = (f32[34,1024]{1,0:T(8,128)S(1)}, f32[34,1024]{1,0:T(8,128)S(1)}, u32[]{:S(2)}, u32[]{:S(2)}) collective-permute-start(f32[34,1024]{1,0:T(8,128)S(1)} %concatenate.9.centre.centre_mesh), channel_id=1, source_target_pairs={{1,0},{2,1},{3,2},{4,3},{5,4},{6,5},{7,6},{0,7},{9,8},{10,9},{11,1... | collective-permute-start | bytes 417800 | tf_op jit(solution)/shard_map/ppermute | solution.py:330
  18.2 20.5 %copy-start = (s32[1024]{0:T(1024)S(1)}, s32[1024]{0:T(1024)}, u32[]{:S(2)}) copy-start(s32[1024]{0:T(1024)} %param.24) | copy-start | bytes 12292
  18.2 20.6 %copy-start.2 = (f32[4,21]{1,0:T(4,128)S(1)}, f32[4,21]{1,0:T(4,128)}, u32[]{:S(2)}) copy-start(f32[4,21]{1,0:T(4,128)} %matrix_ref.1) | copy-start | bytes 1012
  29.0 8.2 %collective-permute-start.2 = (f32[24,1024]{1,0:T(8,128)S(1)}, f32[24,1024]{1,0:T(8,128)S(1)}, u32[]{:S(2)}, u32[]{:S(2)}) collective-permute-start(f32[24,1024]{1,0:T(8,128)S(1)} %shard_map.127.centre), channel_id=1, source_target_pairs={{0,1},{1,2},{2,3},{3,4},{4,5},{5,6},{6,7},{7,0},{8,9},{9,10},{10,1... | collective-permute-start | bytes 294920 | tf_op jit(solution)/shard_map/ppermute | solution.py:330
  31.0 7.8 %collective-permute-start.3 = (f32[24,1024]{1,0:T(8,128)S(1)}, f32[24,1024]{1,0:T(8,128)S(1)}, u32[]{:S(2)}, u32[]{:S(2)}) collective-permute-start(f32[24,1024]{1,0:T(8,128)S(1)} %shard_map.127.centre), channel_id=1, source_target_pairs={{1,0},{2,1},{3,2},{4,3},{5,4},{6,5},{7,6},{0,7},{9,8},{10,9},{11,1... | collective-permute-start | bytes 294920 | tf_op jit(solution)/shard_map/ppermute | solution.py:330
  50.6 18.8 %all-to-all-start = ((f32[64,2,128]{2,1,0:T(2,128)}), f32[64,2,128]{2,1,0:T(2,128)S(1)}, u32[]{:S(2)}, u32[]{:S(2)}) async-start(f32[64,2,128]{2,1,0:T(2,128)} %get-tuple-element.9), calls=%async_computation | async-start | bytes 131072 | tf_op jit(solution)/shard_map/all_to_all | solution.py:392
  59.4 0.7 copy-start.1
  71.4 7.0 %copy-start.11 = (f32[21,4]{0,1:T(4,128)S(1)}, f32[21,4]{0,1:T(4,128)}, u32[]{:S(2)}) copy-start(f32[21,4]{0,1:T(4,128)} %param.23) | copy-start | bytes 1012
  71.4 12.2 %all-to-all-start.1 = ((f32[8,8,128]{2,1,0:T(8,128)}), f32[8,8,128]{2,1,0:T(8,128)S(1)}, u32[]{:S(2)}, u32[]{:S(2)}) async-start(f32[8,8,128]{2,1,0:T(8,128)} %get-tuple-element.10), calls=%async_computation.1 | async-start | bytes 65536 | tf_op jit(solution)/shard_map/all_to_all | solution.py:408

commit v3 on v2

--- a/solution.py
+++ b/solution.py
@@ -21,7 +21,6 @@
 GROUPS = SLICES // GROUP
 BLOCKS = CELLS_DEV // LANES
 PHASE_STEPS = 8
-SEGMENT = 2
 WINDOW = 3 * BLOCKS
 
 coupling = 0.1
@@ -54,24 +53,33 @@
     return slice(block * LANES, (block + count) * LANES)
 
 
-def fill_window(state_refs, mesh_refs, field, places, coefs):
+def sides(odd, first, second, rows):
+    one, two = first[rows, :], second[rows, :]
+    return jnp.where(odd, one, two), jnp.where(odd, two, one)
+
+
+def fill_window(odd, state_refs, mesh_refs, field, places, coefs):
     inside = lax.broadcasted_iota(jnp.int32, (ROWS, CELLS_DEV), 0) < DOF
     lane = lax.broadcasted_iota(jnp.int32, (8, CELLS_DEV), 1) % LANES
     edge = jnp.zeros((ROWS, LANES), f32)
     field[:, lanes_of(0)] = edge
     field[:, lanes_of(WINDOW + 1)] = edge
-    for part, (state_ref, mesh_ref) in enumerate(zip(state_refs, mesh_refs)):
+
+    def in_order(refs, rows):
+        left, right = sides(odd, refs[0], refs[2], rows)
+        return left, refs[1][rows, :], right
+
+    for part, state in enumerate(in_order(state_refs, slice(0, ROWS))):
+        field[:, lanes_of(1 + part * BLOCKS, BLOCKS)] = jnp.where(inside, state, 0.0)
+    for part, mesh in enumerate(in_order(mesh_refs, slice(DOF, DOF + 13))):
         cells = lanes_of(1 + part * BLOCKS, BLOCKS)
-        field[:, cells] = jnp.where(inside, state_ref[0:ROWS, :], 0.0)
         for e in range(3):
-            offset = mesh_ref[DOF + e : DOF + e + 1, :].astype(jnp.int32)
+            offset = mesh[e : e + 1, :].astype(jnp.int32)
             target = jnp.broadcast_to(offset, (8, CELLS_DEV)) + lane
             within = (target >= 0) & (target < LANES)
             places[e, :, cells] = (target & (LANES - 1)) + jnp.where(within, 0, LANES)
         for row in range(10):
-            coefs[row, :, cells] = jnp.broadcast_to(
-                mesh_ref[DOF + 3 + row : DOF + 4 + row, :], (8, CELLS_DEV)
-            )
+            coefs[row, :, cells] = jnp.broadcast_to(mesh[3 + row : 4 + row, :], (8, CELLS_DEV))
 
 
 def block_rate(source, block, places, coefs, stencil, low_half):
@@ -110,36 +118,33 @@
     middle[:, lanes_of(0)] = edge
     middle[:, lanes_of(WINDOW + 1)] = edge
 
-    for first in range(0, PHASE_STEPS, SEGMENT):
-        blocks = range(1 + first, 1 + WINDOW - first)
-
-        def step(index, carry):
-            stencil = stencil_ref[...]
-            for b in blocks:
-                rate = block_rate(field, b, places, coefs, stencil, low_half)
-                middle[:, lanes_of(b)] = field[:, lanes_of(b)] + rate
-            for b in blocks:
-                rate = block_rate(middle, b, places, coefs, stencil, low_half)
-                here = lanes_of(b)
-                field[:, here] = 0.5 * (field[:, here] + middle[:, here] + rate)
-            return carry
-
-        lax.fori_loop(0, SEGMENT, step, 0)
-
-
-def first_phase_kernel(left, centre, right, stencil_ref, out, field, middle, places, coefs):
-    packs = (left, centre, right)
-    fill_window(packs, packs, field, places, coefs)
+    stencil = stencil_ref[...]
+    for index in range(PHASE_STEPS):
+        for b in range(1 + index, 1 + WINDOW - index):
+            rate = block_rate(field, b, places, coefs, stencil, low_half)
+            middle[:, lanes_of(b)] = field[:, lanes_of(b)] + rate
+        for b in range(2 + index, WINDOW - index):
+            rate = block_rate(middle, b, places, coefs, stencil, low_half)
+            here = lanes_of(b)
+            field[:, here] = 0.5 * (field[:, here] + middle[:, here] + rate)
+
+
+def first_phase_kernel(
+    where_ref, first, centre, second, stencil_ref, out, field, middle, places, coefs
+):
+    packs = (first, centre, second)
+    fill_window(where_ref[2] % 2 == 1, packs, packs, field, places, coefs)
     march(field, middle, places, coefs, stencil_ref)
     out[...] = field[:, lanes_of(1 + BLOCKS, BLOCKS)]
 
 
-def restricted(values, members, restrict_matrix):
+def restricted(values, index_row, restrict_matrix):
+    members = (
+        lax.broadcasted_iota(jnp.int32, (COARSE_DEV, CELLS_DEV), 0) == index_row
+    ).astype(f32).astype(bf16)
     contract = (((1,), (1,)), ((), ()))
-    first, rest = two_terms(values)
-    second, third = two_terms(values - first.astype(f32))
     totals = jnp.zeros((ROWS, COARSE_DEV), f32)
-    for term in (third, second, first):
+    for term in two_terms(values):
         totals = totals + lax.dot_general(term, members, contract, preferred_element_type=f32)
     counts = lax.dot_general(
         jnp.ones((16, CELLS_DEV), bf16), members, contract, preferred_element_type=f32
@@ -147,32 +152,28 @@
     result = jnp.zeros((CDOF, COARSE_DEV), f32)
     for d in range(DOF):
         result = result + restrict_matrix[:, d : d + 1] * totals[d : d + 1, :]
-    return result / counts
-
-
-def in_one_row(coarse):
-    return jnp.concatenate([coarse[i : i + 1, :] for i in range(CDOF)], axis=1)
+    result = result / counts
+    return jnp.concatenate([result[i : i + 1, :] for i in range(CDOF)], axis=1)
+
+
+def start_kernel(pack_ref, index_ref, matrix_ref, out):
+    inside = lax.broadcasted_iota(jnp.int32, (ROWS, CELLS_DEV), 0) < DOF
+    start = jnp.where(inside, pack_ref[0:ROWS, :], 0.0)
+    out[...] = restricted(start, index_ref[...], matrix_ref[...])
 
 
 def second_phase_kernel(
-    left, centre, right, left_mesh, centre_mesh, right_mesh, stencil_ref, index_ref, matrix_ref,
-    out, message, field, middle, places, coefs,
+    where_ref, first, centre, second, first_mesh, centre_mesh, second_mesh, stencil_ref, index_ref,
+    matrix_ref, start_ref, out, message, field, middle, places, coefs,
 ):
-    fill_window(
-        (left, centre, right), (left_mesh, centre_mesh, right_mesh), field, places, coefs
-    )
+    odd = where_ref[2] % 2 == 1
+    mesh_refs = (first_mesh, centre_mesh, second_mesh)
+    fill_window(odd, (first, centre, second), mesh_refs, field, places, coefs)
     march(field, middle, places, coefs, stencil_ref)
     fine = field[:, lanes_of(1 + BLOCKS, BLOCKS)]
     out[...] = fine
-    members = (
-        lax.broadcasted_iota(jnp.int32, (COARSE_DEV, CELLS_DEV), 0) == index_ref[...]
-    ).astype(f32).astype(bf16)
-    matrix = matrix_ref[...]
-    inside = lax.broadcasted_iota(jnp.int32, (ROWS, CELLS_DEV), 0) < DOF
-    start = jnp.where(inside, centre_mesh[0:ROWS, :], 0.0)
     rows = jnp.concatenate(
-        [in_one_row(restricted(fine, members, matrix)), in_one_row(restricted(start, members, matrix))],
-        axis=0,
+        [restricted(fine, index_ref[...], matrix_ref[...]), start_ref[...]], axis=0
     )
     for copy in range(GROUP * PARTS):
         message[copy] = rows
@@ -184,7 +185,7 @@
     return jnp.where(even_row, up, down)
 
 
-def compose_kernel(inverse_ref, out):
+def compose_kernel(inverse_ref, out, out_twice):
     shape = (8, 8, LANES)
     row = lax.broadcasted_iota(jnp.int32, shape, 1)
     lane = lax.broadcasted_iota(jnp.int32, shape, 2)
@@ -202,7 +203,7 @@
                 pieces.append(inverse_ref[i, j : j + 1, lanes_of(h)])
         blocks.append(jnp.concatenate(pieces, axis=0)[None])
     reach = {0: jnp.where(turn == 0, 1.0, 0.0)}
-    for repeat in range(COARSE_STEPS):
+    for repeat in range(2 * COARSE_STEPS):
         swapped = {o: flipped(tiles, even_row) for o, tiles in reach.items()}
         blended = {}
         for o in range(-repeat - 1, repeat + 2):
@@ -223,8 +224,10 @@
                 turned = jnp.concatenate([tiles[8 - 2 * by :], tiles[: 8 - 2 * by]], axis=0)
                 total = total + blocks[by] * pltpu.roll(turned, 2 * by, axis=1)
             reach[o] = total
-    for o, tiles in reach.items():
-        out[o + COARSE_STEPS] = tiles if o == 0 else pltpu.roll(tiles, -o % LANES, axis=2)
+        if (repeat + 1) % COARSE_STEPS == 0:
+            held = out if repeat < COARSE_STEPS else out_twice
+            for o, tiles in reach.items():
+                held[o + repeat + 1] = tiles if o == 0 else pltpu.roll(tiles, -o % LANES, axis=2)
 
 
 def added(terms):
@@ -235,9 +238,10 @@
 
 def coarse_slice(vector, operator_ref):
     turns = [vector] + [pltpu.roll(vector, d, axis=0) for d in range(1, 8)]
+    reach = operator_ref.shape[0] // 2
     shares = []
-    for o in range(-COARSE_STEPS, COARSE_STEPS + 1):
-        share = added([operator_ref[o + COARSE_STEPS, d] * turns[d] for d in range(8)])
+    for o in range(-reach, reach + 1):
+        share = added([operator_ref[o + reach, d] * turns[d] for d in range(8)])
         shares.append(share if o == 0 else pltpu.roll(share, o % LANES, axis=1))
     return added(shares)
 
@@ -277,20 +281,21 @@
 
 
 def correct_kernel(
-    where_ref, ends, own_ref, operator_ref, fine_ref, index_ref, matrix_ref, out
+    where_ref, ends, own_ref, operator_ref, twice_ref, fine_ref, index_ref, matrix_ref, out
 ):
     group = where_ref[0]
     place = where_ref[1]
     part = where_ref[2]
 
-    def advance(count, vector):
-        return lax.fori_loop(0, count, lambda n, now: coarse_slice(now, operator_ref), vector)
+    def advance(count, vector, ref):
+        return lax.fori_loop(0, count, lambda n, now: coarse_slice(now, ref), vector)
 
     def link(k, vector):
-        return advance(GROUP, vector) + ends[k]
+        return advance(GROUP // 2, vector, twice_ref) + ends[k]
 
     before = lax.fori_loop(1, group, link, ends[0])
-    before = advance(jnp.where(group > 0, place + 1, 0), before)
+    count = jnp.where(group > 0, place + 1, 0)
+    before = advance(count % 2, advance(count // 2, before, twice_ref), operator_ref)
     chain = own_ref[0] + jnp.where(group > 0, before, 0.0)
     change = chain - own_ref[1]
     upper = part >= PARTS // 2
@@ -303,9 +308,7 @@
         == index_ref[...] + COARSE_DEV * (part % 4)
     ).astype(f32).astype(bf16)
     total = fine_ref[...]
-    first, rest = two_terms(spread)
-    second, third = two_terms(spread - first.astype(f32))
-    for term in (third, second, first):
+    for term in two_terms(spread):
         total = total + jnp.dot(term, members, preferred_element_type=f32)
     for d in range(DOF):
         out[d] = total[d : d + 1, :]
@@ -325,9 +328,12 @@
 
 
 def both_sides(values):
-    ring = [(i, (i + 1) % PARTS) for i in range(PARTS)]
-    back = [((i + 1) % PARTS, i) for i in range(PARTS)]
-    return lax.ppermute(values, "space", ring), lax.ppermute(values, "space", back)
+    pairs = [(i, i ^ 1) for i in range(PARTS)]
+    others = [(i, (((i + 1) ^ 1) - 1) % PARTS) for i in range(PARTS)]
+    return lax.ppermute(values, "space", pairs), lax.ppermute(values, "space", others)
+
+
+smem = pl.BlockSpec(memory_space=pltpu.SMEM)
 
 
 def local(
@@ -348,52 +354,66 @@
     pack = jnp.concatenate(
         [states[0], neighbour.astype(f32), edge_x, edge_y, edge_damp, coriolis[None, :]], axis=0
     )
-    left, right = both_sides(pack)
+    first, second = both_sides(pack)
+    slice_here = lax.axis_index("tm")
+    where = jnp.stack([slice_here // GROUP, slice_here % GROUP, lax.axis_index("space")])
+    where = where.astype(jnp.int32)
     wide = [jnp.pad(m, ((0, ROWS - DOF), (0, ROWS - DOF))) for m in (flux_x, flux_y, rotation)]
     stencil = jnp.concatenate(wide + [jnp.zeros((ROWS, 8), f32)], axis=1)
     high = stencil.astype(bf16)
     low = (stencil - lax.reduce_precision(stencil, 8, 7)).astype(bf16)
     stencil_terms = jnp.concatenate([high, high, low], axis=1)
     index_row = restrict_index[None, :]
-    operator = pl.pallas_call(
-        compose_kernel,
-        out_shape=jax.ShapeDtypeStruct((2 * COARSE_STEPS + 1, 8, 8, LANES), f32),
-        in_specs=[vmem],
+    start = pl.pallas_call(
+        start_kernel,
+        out_shape=jax.ShapeDtypeStruct((1, LANES), f32),
+        in_specs=[vmem] * 3,
         out_specs=vmem,
         compiler_params=params,
-        cost_estimate=pl.CostEstimate(flops=4000000, bytes_accessed=300000, transcendentals=0),
-    )(coarse_inverse)
+        cost_estimate=pl.CostEstimate(flops=4000000, bytes_accessed=200000, transcendentals=0),
+    )(pack, index_row, restrict_matrix)
 
     half = pl.pallas_call(
         first_phase_kernel,
         out_shape=jax.ShapeDtypeStruct((ROWS, CELLS_DEV), f32),
-        in_specs=[vmem] * 4,
+        in_specs=[smem] + [vmem] * 4,
         out_specs=vmem,
         scratch_shapes=march_scratch(),
         compiler_params=params,
-    )(left, pack, right, stencil_terms)
-    half_left, half_right = both_sides(half)
+    )(where, first, pack, second, stencil_terms)
+    half_first, half_second = both_sides(half)
     fine, message = pl.pallas_call(
         second_phase_kernel,
         out_shape=(
             jax.ShapeDtypeStruct((ROWS, CELLS_DEV), f32),
             jax.ShapeDtypeStruct((GROUP * PARTS, 2, LANES), f32),
         ),
-        in_specs=[vmem] * 9,
+        in_specs=[smem] + [vmem] * 10,
         out_specs=(vmem, vmem),
         scratch_shapes=march_scratch(),
         compiler_params=params,
-    )(half_left, half, half_right, left, pack, right, stencil_terms, index_row, restrict_matrix)
-
+    )(
+        where, half_first, half, half_second, first, pack, second, stencil_terms, index_row,
+        restrict_matrix, start,
+    )
+
+    late_inverse, message = lax.optimization_barrier((coarse_inverse, message))
+    operator, operator_twice = pl.pallas_call(
+        compose_kernel,
+        out_shape=tuple(
+            jax.ShapeDtypeStruct((2 * reach + 1, 8, 8, LANES), f32)
+            for reach in (COARSE_STEPS, 2 * COARSE_STEPS)
+        ),
+        in_specs=[vmem],
+        out_specs=(vmem, vmem),
+        compiler_params=params,
+        cost_estimate=pl.CostEstimate(flops=12000000, bytes_accessed=900000, transcendentals=0),
+    )(late_inverse)
     axes = ("tm", "space")
     members = GROUP * PARTS
     inside = [[g * members + m for m in range(members)] for g in range(GROUPS)]
     across = [[g * members + m for g in range(GROUPS)] for m in range(members)]
     gathered = lax.all_to_all(message, axes, 0, 0, tiled=True, axis_index_groups=inside)
-    slice_here = lax.axis_index("tm")
-    where = jnp.stack([slice_here // GROUP, slice_here % GROUP, lax.axis_index("space")])
-    where = where.astype(jnp.int32)
-    smem = pl.BlockSpec(memory_space=pltpu.SMEM)
     ends, own = pl.pallas_call(
         group_kernel,
         out_shape=(
@@ -410,10 +430,10 @@
     updated = pl.pallas_call(
         correct_kernel,
         out_shape=jax.ShapeDtypeStruct((DOF, 1, CELLS_DEV), f32),
-        in_specs=[smem] + [vmem] * 6,
+        in_specs=[smem] + [vmem] * 7,
         out_specs=vmem,
         compiler_params=params,
-    )(where, ends, own, operator, fine, index_row, spread_matrix)
+    )(where, ends, own, operator, operator_twice, fine, index_row, spread_matrix)
     return updated.transpose(1, 0, 2)
 
 

time: 90.1 us -> 85.7 us (0.951)
  starting transfers between devices: 36.2 us -> 32.2 us
  Pallas kernels: 31.1 us -> 28.1 us
  waiting for transfers between devices: 19 us -> 21.7 us
    ppermute x4, waiting for transfers between devices: 5.36 us -> 8.71 us  [the longest x2 4.36 us: both_sides(): lax.ppermute(values, 'space', pairs)]
    ppermute x4, starting transfers between devices: 20.4 us -> 17.2 us  [the longest x2 13.1 us: both_sides(): lax.ppermute(values, 'space', others)]
    pallas_call x1, Pallas kernels: 5.88 us -> 4.1 us  [local(): pl.pallas_call(correct_kernel, out_shape=jax.ShapeDtypeStruct((DOF, 1, CE...]
    pallas_call x1 -> x2, Pallas kernels: 0.6 us -> 2.11 us  [the longest x1 1.84 us: local(): pl.pallas_call(compose_kernel, out_shape=tuple((jax.ShapeDtypeStruct((2 *...]
    pallas_call x1, Pallas kernels: 10.8 us -> 9.45 us  [local(): pl.pallas_call(first_phase_kernel, out_shape=jax.ShapeDtypeStruct((ROWS,...]
    pallas_call x1, Pallas kernels: 11.8 us -> 10.5 us  [local(): pl.pallas_call(second_phase_kernel, out_shape=(jax.ShapeDtypeStruct((ROWS...]
    unnamed x26 -> x24, local copies, waits for them, and re-layouts: 2.46 us -> 1.69 us
  transfers between devices with their start and end apart: 6 -> 6, of which waited for: 6 -> 6; matrix products, arithmetic and copies ran while one was open for 0% -> 1% of each run, Pallas kernels for 1% -> 2%
where the time goes in v3:
time: 85.7 us; the launch traced here: 85.1 us
  starting transfers between devices  32.2 us (38%)
  Pallas kernels  28.1 us (33%)
  waiting for transfers between devices  21.7 us (25%)
  local copies, waits for them, and re-layouts  1.97 us (2%)
  other arithmetic  0.97 us (1%)
    ppermute x2, starting transfers between devices, both_sides(): lax.ppermute(values, 'space', others)  13.1 us
    pallas_call x1, Pallas kernels, local(): pl.pallas_call(second_phase_kernel, out_shape=(jax.ShapeDtypeStruct((ROWS...  10.5 us
    pallas_call x1, Pallas kernels, local(): pl.pallas_call(first_phase_kernel, out_shape=jax.ShapeDtypeStruct((ROWS,...  9.45 us
    all_to_all x1, starting transfers between devices, local(): lax.all_to_all(message, axes, 0, 0, tiled=True, axis_index_groups=inside)  8.04 us
    all_to_all x1, waiting for transfers between devices, local(): lax.all_to_all(message, axes, 0, 0, tiled=True, axis_index_groups=inside)  7.87 us
    all_to_all x1, starting transfers between devices, local(): lax.all_to_all(ends, axes, 0, 0, tiled=True, axis_index_groups=across)  7 us
    all_to_all x1, waiting for transfers between devices, local(): lax.all_to_all(ends, axes, 0, 0, tiled=True, axis_index_groups=across)  5.07 us
    ppermute x2, waiting for transfers between devices, both_sides(): lax.ppermute(values, 'space', pairs)  4.36 us
  transfers between devices with their start and end apart: 6, of which 6 were waited for; matrix products, arithmetic and copies ran while one was open for 1% of the time, Pallas kernels for 2%

profile of v3, /device:TPU:56, one launch (start us, length us, event | category | flops | bytes accessed | tf_op | source)
XLA Modules:
  0.0 85.1 jit_solution(3423525164870005116)
XLA Ops:
  0.0 0.7 convert_element_type.15
  0.7 0.0 copy-start.3
  0.7 0.0 copy-start.4
  0.7 0.0 copy-start.5
  0.7 0.0 copy-start.9
  0.7 0.9 %copy.17 = f32[1,21,1024]{2,1,0:T(8,128)S(1)} copy(f32[1,21,1024]{2,0,1:T(1,128)} %param.13) | data formatting | bytes 172032
  1.7 0.0 copy-done.3
  1.7 0.0 copy-done.4
  1.7 0.0 copy-done.5
  1.7 0.0 copy-done.9
  1.7 0.2 concatenate.9.centre.pack_ref.centre_mesh
  1.9 10.9 %collective-permute-start.1 = (f32[34,1024]{1,0:T(8,128)S(1)}, f32[34,1024]{1,0:T(8,128)S(1)}, u32[]{:S(2)}, u32[]{:S(2)}) collective-permute-start(f32[34,1024]{1,0:T(8,128)S(1)} %concatenate.9.centre.pack_ref.centre_mesh), channel_id=1, source_target_pairs={{0,7},{1,2},{2,1},{3,4},{4,3},{5,6},{6,5},{7,0},{8,15},{9,10},{10,... | collective-permute-start | bytes 417800 | tf_op jit(solution)/shard_map/ppermute | solution.py:333
  12.9 1.9 %collective-permute-start = (f32[34,1024]{1,0:T(8,128)S(1)}, f32[34,1024]{1,0:T(8,128)S(1)}, u32[]{:S(2)}, u32[]{:S(2)}) collective-permute-start(f32[34,1024]{1,0:T(8,128)S(1)} %concatenate.9.centre.pack_ref.centre_mesh), channel_id=1, source_target_pairs={{0,1},{1,0},{2,3},{3,2},{4,5},{5,4},{6,7},{7,6},{8,9},{9,8},{10,11... | collective-permute-start | bytes 417800 | tf_op jit(solution)/shard_map/ppermute | solution.py:333
  14.8 0.0 copy-start.8
  14.8 0.0 copy-start.6
  14.8 0.0 copy-start.7
  14.9 0.1 pad.24.clone
  14.9 0.6 copy-done.8
  15.5 0.0 copy-done.6
  15.5 0.0 copy-done.7
  15.6 0.1 fusion.4
  15.7 0.1 pad_add_fusion.where_ref
  15.7 0.1 pad_maximum_fusion.stencil_ref
  15.8 1.2 %collective-permute-done.1.second.second_mesh = f32[34,1024]{1,0:T(8,128)S(1)} collective-permute-done((f32[34,1024]{1,0:T(8,128)S(1)}, f32[34,1024]{1,0:T(8,128)S(1)}, u32[]{:S(2)}, u32[]{:S(2)}) %collective-permute-start.1) | collective-permute-done | bytes 139296 | tf_op jit(solution)/shard_map/ppermute | solution.py:333
  17.1 3.4 %collective-permute-done.first.first_mesh = f32[34,1024]{1,0:T(8,128)S(1)} collective-permute-done((f32[34,1024]{1,0:T(8,128)S(1)}, f32[34,1024]{1,0:T(8,128)S(1)}, u32[]{:S(2)}, u32[]{:S(2)}) %collective-permute-start) | collective-permute-done | bytes 139296 | tf_op jit(solution)/shard_map/ppermute | solution.py:333
  20.4 0.0 copy-start
  20.4 0.0 copy-start.1
  20.4 9.4 %shard_map.127.centre = f32[24,1024]{1,0:T(8,128)S(1)} custom-call(s32[3]{0:T(128)S(1)} %pad_add_fusion.where_ref, f32[34,1024]{1,0:T(8,128)S(1)} %collective-permute-done.first.first_mesh, f32[34,1024]{1,0:T(8,128)S(1)} %concatenate.9.centre.pack_ref.centre_mesh, f32[34,1024]{1,0:T(8,128)S(1)} %collective-permute-done.1.second.second_mesh, ...), custom_call_target="tpu_custom_call" | custom-call | tf_op jit(solution)/shard_map/pallas_call | solution.py:376
  29.9 2.2 %collective-permute-start.3 = (f32[24,1024]{1,0:T(8,128)S(1)}, f32[24,1024]{1,0:T(8,128)S(1)}, u32[]{:S(2)}, u32[]{:S(2)}) collective-permute-start(f32[24,1024]{1,0:T(8,128)S(1)} %shard_map.127.centre), channel_id=1, source_target_pairs={{0,7},{1,2},{2,1},{3,4},{4,3},{5,6},{6,5},{7,0},{8,15},{9,10},{10,... | collective-permute-start | bytes 294920 | tf_op jit(solution)/shard_map/ppermute | solution.py:333
  32.1 2.1 %collective-permute-start.2 = (f32[24,1024]{1,0:T(8,128)S(1)}, f32[24,1024]{1,0:T(8,128)S(1)}, u32[]{:S(2)}, u32[]{:S(2)}) collective-permute-start(f32[24,1024]{1,0:T(8,128)S(1)} %shard_map.127.centre), channel_id=1, source_target_pairs={{0,1},{1,0},{2,3},{3,2},{4,5},{5,4},{6,7},{7,6},{8,9},{9,8},{10,11... | collective-permute-start | bytes 294920 | tf_op jit(solution)/shard_map/ppermute | solution.py:333
  34.2 0.0 copy-done
  34.2 0.0 copy-done.1
  34.2 0.3 shard_map.128.start_ref
  34.5 3.1 %collective-permute-done.3.second = f32[24,1024]{1,0:T(8,128)S(1)} collective-permute-done((f32[24,1024]{1,0:T(8,128)S(1)}, f32[24,1024]{1,0:T(8,128)S(1)}, u32[]{:S(2)}, u32[]{:S(2)}) %collective-permute-start.3) | collective-permute-done | bytes 98336 | tf_op jit(solution)/shard_map/ppermute | solution.py:333
  37.6 1.0 %collective-permute-done.2.first = f32[24,1024]{1,0:T(8,128)S(1)} collective-permute-done((f32[24,1024]{1,0:T(8,128)S(1)}, f32[24,1024]{1,0:T(8,128)S(1)}, u32[]{:S(2)}, u32[]{:S(2)}) %collective-permute-start.2) | collective-permute-done | bytes 98336 | tf_op jit(solution)/shard_map/ppermute | solution.py:333
  38.6 10.5 %shard_map.129 = (f32[24,1024]{1,0:T(8,128)S(1)}, f32[64,2,128]{2,1,0:T(2,128)}) custom-call(s32[3]{0:T(128)S(1)} %pad_add_fusion.where_ref, f32[24,1024]{1,0:T(8,128)S(1)} %collective-permute-done.2.first, f32[24,1024]{1,0:T(8,128)S(1)} %shard_map.127.centre, f32[24,1024]{1,0:T(8,128)S(1)} %collective-permute-done.3.second, ...), custom_call_target="tpu_custom_call" | custom-call | tf_op jit(solution)/shard_map/pallas_call | solution.py:385
  49.1 0.0 copy-start.2
  49.1 8.0 %all-to-all-start = ((f32[64,2,128]{2,1,0:T(2,128)}), f32[64,2,128]{2,1,0:T(2,128)S(1)}, u32[]{:S(2)}, u32[]{:S(2)}) async-start(f32[64,2,128]{2,1,0:T(2,128)} %get-tuple-element.14), calls=%async_computation | async-start | bytes 131072 | tf_op jit(solution)/shard_map/all_to_all | solution.py:416
  57.1 0.0 copy-done.2
  57.1 1.8 %shard_map.130 = (f32[9,8,8,128]{3,2,1,0:T(8,128)S(1)}, f32[17,8,8,128]{3,2,1,0:T(8,128)S(1)}) custom-call(f32[4,4,256]{2,1,0:T(4,128)S(1)} %copy-done.2), custom_call_target="tpu_custom_call" | custom-call | flops 12000000 | bytes 900000 | tf_op jit(solution)/shard_map/pallas_call | solution.py:401
  59.0 7.9 %all-to-all-done = f32[64,2,128]{2,1,0:T(2,128)S(1)} async-done(((f32[64,2,128]{2,1,0:T(2,128)}), f32[64,2,128]{2,1,0:T(2,128)S(1)}, u32[]{:S(2)}, u32[]{:S(2)}) %all-to-all-start) | async-done | bytes 65568 | tf_op jit(solution)/shard_map/all_to_all | solution.py:416
  66.8 2.0 %shard_map.131 = (f32[8,8,128]{2,1,0:T(8,128)}, f32[2,8,128]{2,1,0:T(8,128)S(1)}) custom-call(s32[3]{0:T(128)S(1)} %pad_add_fusion.where_ref, f32[128,128]{1,0:T(8,128)S(1)} %bitcast.10, f32[9,8,8,128]{3,2,1,0:T(8,128)S(1)} %get-tuple-element.16.operator_ref), custom_call_target="tpu_custom_call" | custom-call | tf_op jit(solution)/shard_map/pallas_call | solution.py:417
  68.8 0.0 copy-start.10
  68.8 7.0 %all-to-all-start.1 = ((f32[8,8,128]{2,1,0:T(8,128)}), f32[8,8,128]{2,1,0:T(8,128)S(1)}, u32[]{:S(2)}, u32[]{:S(2)}) async-start(f32[8,8,128]{2,1,0:T(8,128)} %get-tuple-element.17), calls=%async_computation.1 | async-start | bytes 65536 | tf_op jit(solution)/shard_map/all_to_all | solution.py:428
  75.8 0.0 copy-done.10
  75.8 0.1 copy.14
  76.0 5.1 %all-to-all-done.1.ends = f32[8,8,128]{2,1,0:T(8,128)S(1)} async-done(((f32[8,8,128]{2,1,0:T(8,128)}), f32[8,8,128]{2,1,0:T(8,128)S(1)}, u32[]{:S(2)}, u32[]{:S(2)}) %all-to-all-start.1) | async-done | bytes 32800 | tf_op jit(solution)/shard_map/all_to_all | solution.py:428
  81.0 4.1 %shard_map.132 = f32[21,1,1024]{2,1,0:T(1,128)} custom-call(s32[3]{0:T(128)S(1)} %pad_add_fusion.where_ref, f32[8,8,128]{2,1,0:T(8,128)S(1)} %all-to-all-done.1.ends, f32[2,8,128]{2,1,0:T(8,128)S(1)} %get-tuple-element.18.own_ref, f32[9,8,8,128]{3,2,1,0:T(8,128)S(1)} %get-tuple-element.16.operator_ref, f32[17,8,8,128]{3,2,1,0:T(8,128)S(1)} %get-tuple-element.19.twice_ref, ...), custom_call_target="tpu_custom_call" | custom-call | tf_op jit(solution)/shard_map/pallas_call | solution.py:430
  (3 shorter events, 0.0 us)
Async XLA Ops:
  0.7 1.0 %copy-start.3 = (f32[3,1024]{1,0:T(4,128)S(1)}, f32[3,1024]{1,0:T(4,128)}, u32[]{:S(2)}) copy-start(f32[3,1024]{1,0:T(4,128)} %param.15) | copy-start | bytes 36868
  0.7 1.0 %copy-start.4 = (f32[3,1024]{1,0:T(4,128)S(1)}, f32[3,1024]{1,0:T(4,128)}, u32[]{:S(2)}) copy-start(f32[3,1024]{1,0:T(4,128)} %param.16) | copy-start | bytes 36868
  0.7 1.0 %copy-start.5 = (f32[3,1024]{1,0:T(4,128)S(1)}, f32[3,1024]{1,0:T(4,128)}, u32[]{:S(2)}) copy-start(f32[3,1024]{1,0:T(4,128)} %param.17) | copy-start | bytes 36868
  0.7 1.0 %copy-start.9 = (f32[1024]{0:T(1024)S(1)}, f32[1024]{0:T(1024)}, u32[]{:S(2)}) copy-start(f32[1024]{0:T(1024)} %param.18) | copy-start | bytes 12292
  1.9 15.1 %collective-permute-start.1 = (f32[34,1024]{1,0:T(8,128)S(1)}, f32[34,1024]{1,0:T(8,128)S(1)}, u32[]{:S(2)}, u32[]{:S(2)}) collective-permute-start(f32[34,1024]{1,0:T(8,128)S(1)} %concatenate.9.centre.pack_ref.centre_mesh), channel_id=1, source_target_pairs={{0,7},{1,2},{2,1},{3,4},{4,3},{5,6},{6,5},{7,0},{8,15},{9,10},{10,... | collective-permute-start | bytes 417800 | tf_op jit(solution)/shard_map/ppermute | solution.py:333
  12.9 7.6 %collective-permute-start = (f32[34,1024]{1,0:T(8,128)S(1)}, f32[34,1024]{1,0:T(8,128)S(1)}, u32[]{:S(2)}, u32[]{:S(2)}) collective-permute-start(f32[34,1024]{1,0:T(8,128)S(1)} %concatenate.9.centre.pack_ref.centre_mesh), channel_id=1, source_target_pairs={{0,1},{1,0},{2,3},{3,2},{4,5},{5,4},{6,7},{7,6},{8,9},{9,8},{10,11... | collective-permute-start | bytes 417800 | tf_op jit(solution)/shard_map/ppermute | solution.py:333
  14.8 0.7 copy-start.8
  14.8 0.7 copy-start.6
  14.8 0.7 copy-start.7
  20.4 13.8 %copy-start = (s32[1024]{0:T(1024)S(1)}, s32[1024]{0:T(1024)}, u32[]{:S(2)}) copy-start(s32[1024]{0:T(1024)} %param.24) | copy-start | bytes 12292
  20.4 13.8 %copy-start.1 = (f32[4,21]{1,0:T(4,128)S(1)}, f32[4,21]{1,0:T(4,128)}, u32[]{:S(2)}) copy-start(f32[4,21]{1,0:T(4,128)} %matrix_ref.3) | copy-start | bytes 1012
  29.9 7.7 %collective-permute-start.3 = (f32[24,1024]{1,0:T(8,128)S(1)}, f32[24,1024]{1,0:T(8,128)S(1)}, u32[]{:S(2)}, u32[]{:S(2)}) collective-permute-start(f32[24,1024]{1,0:T(8,128)S(1)} %shard_map.127.centre), channel_id=1, source_target_pairs={{0,7},{1,2},{2,1},{3,4},{4,3},{5,6},{6,5},{7,0},{8,15},{9,10},{10,... | collective-permute-start | bytes 294920 | tf_op jit(solution)/shard_map/ppermute | solution.py:333
  32.1 6.5 %collective-permute-start.2 = (f32[24,1024]{1,0:T(8,128)S(1)}, f32[24,1024]{1,0:T(8,128)S(1)}, u32[]{:S(2)}, u32[]{:S(2)}) collective-permute-start(f32[24,1024]{1,0:T(8,128)S(1)} %shard_map.127.centre), channel_id=1, source_target_pairs={{0,1},{1,0},{2,3},{3,2},{4,5},{5,4},{6,7},{7,6},{8,9},{9,8},{10,11... | collective-permute-start | bytes 294920 | tf_op jit(solution)/shard_map/ppermute | solution.py:333
  49.1 8.1 %copy-start.2 = (f32[4,4,256]{2,1,0:T(4,128)S(1)}, f32[4,4,256]{2,1,0:T(4,128)}, u32[]{:S(2)}) copy-start(f32[4,4,256]{2,1,0:T(4,128)} %inverse_ref) | copy-start | bytes 49156
  49.1 17.8 %all-to-all-start = ((f32[64,2,128]{2,1,0:T(2,128)}), f32[64,2,128]{2,1,0:T(2,128)S(1)}, u32[]{:S(2)}, u32[]{:S(2)}) async-start(f32[64,2,128]{2,1,0:T(2,128)} %get-tuple-element.14), calls=%async_computation | async-start | bytes 131072 | tf_op jit(solution)/shard_map/all_to_all | solution.py:416
  68.8 7.0 %copy-start.10 = (f32[21,4]{0,1:T(4,128)S(1)}, f32[21,4]{0,1:T(4,128)}, u32[]{:S(2)}) copy-start(f32[21,4]{0,1:T(4,128)} %param.23) | copy-start | bytes 1012
  68.8 12.2 %all-to-all-start.1 = ((f32[8,8,128]{2,1,0:T(8,128)}), f32[8,8,128]{2,1,0:T(8,128)S(1)}, u32[]{:S(2)}, u32[]{:S(2)}) async-start(f32[8,8,128]{2,1,0:T(8,128)} %get-tuple-element.17), calls=%async_computation.1 | async-start | bytes 65536 | tf_op jit(solution)/shard_map/all_to_all | solution.py:428

commit v4 on v3

--- a/solution.py
+++ b/solution.py
@@ -58,20 +58,23 @@
     return jnp.where(odd, one, two), jnp.where(odd, two, one)
 
 
-def fill_window(odd, state_refs, mesh_refs, field, places, coefs):
+def in_order(odd, refs, rows):
+    left, right = sides(odd, refs[0], refs[2], rows)
+    return left, refs[1][rows, :], right
+
+
+def fill_field(odd, state_refs, field):
     inside = lax.broadcasted_iota(jnp.int32, (ROWS, CELLS_DEV), 0) < DOF
-    lane = lax.broadcasted_iota(jnp.int32, (8, CELLS_DEV), 1) % LANES
     edge = jnp.zeros((ROWS, LANES), f32)
     field[:, lanes_of(0)] = edge
     field[:, lanes_of(WINDOW + 1)] = edge
-
-    def in_order(refs, rows):
-        left, right = sides(odd, refs[0], refs[2], rows)
-        return left, refs[1][rows, :], right
-
-    for part, state in enumerate(in_order(state_refs, slice(0, ROWS))):
+    for part, state in enumerate(in_order(odd, state_refs, slice(0, ROWS))):
         field[:, lanes_of(1 + part * BLOCKS, BLOCKS)] = jnp.where(inside, state, 0.0)
-    for part, mesh in enumerate(in_order(mesh_refs, slice(DOF, DOF + 13))):
+
+
+def fill_tables(odd, mesh_refs, places, coefs):
+    lane = lax.broadcasted_iota(jnp.int32, (8, CELLS_DEV), 1) % LANES
+    for part, mesh in enumerate(in_order(odd, mesh_refs, slice(DOF, DOF + 13))):
         cells = lanes_of(1 + part * BLOCKS, BLOCKS)
         for e in range(3):
             offset = mesh[e : e + 1, :].astype(jnp.int32)
@@ -129,11 +132,34 @@
             field[:, here] = 0.5 * (field[:, here] + middle[:, here] + rate)
 
 
+def pack_kernel(*refs):
+    sources, out, buffers, done = refs[:6], refs[6], refs[7:13], refs[13]
+    copies = [
+        pltpu.make_async_copy(source, buffer, done.at[i])
+        for i, (source, buffer) in enumerate(zip(sources, buffers))
+    ]
+    for copy in copies:
+        copy.start()
+    row = 0
+    for copy, buffer in zip(copies, buffers):
+        copy.wait()
+        if len(buffer.shape) == 3:
+            for d in range(DOF):
+                out[d : d + 1, :] = buffer[d]
+            row = DOF
+        else:
+            count = buffer.shape[0]
+            out[row : row + count, :] = buffer[...].astype(f32)
+            row += count
+
+
 def first_phase_kernel(
-    where_ref, first, centre, second, stencil_ref, out, field, middle, places, coefs
+    where_ref, first, centre, second, stencil_ref, out, places, coefs, field, middle
 ):
+    odd = where_ref[2] % 2 == 1
     packs = (first, centre, second)
-    fill_window(where_ref[2] % 2 == 1, packs, packs, field, places, coefs)
+    fill_tables(odd, packs, places, coefs)
+    fill_field(odd, packs, field)
     march(field, middle, places, coefs, stencil_ref)
     out[...] = field[:, lanes_of(1 + BLOCKS, BLOCKS)]
 
@@ -163,12 +189,10 @@
 
 
 def second_phase_kernel(
-    where_ref, first, centre, second, first_mesh, centre_mesh, second_mesh, stencil_ref, index_ref,
-    matrix_ref, start_ref, out, message, field, middle, places, coefs,
+    where_ref, first, centre, second, places, coefs, stencil_ref, index_ref, matrix_ref, start_ref,
+    out, message, field, middle,
 ):
-    odd = where_ref[2] % 2 == 1
-    mesh_refs = (first_mesh, centre_mesh, second_mesh)
-    fill_window(odd, (first, centre, second), mesh_refs, field, places, coefs)
+    fill_field(where_ref[2] % 2 == 1, (first, centre, second), field)
     march(field, middle, places, coefs, stencil_ref)
     fine = field[:, lanes_of(1 + BLOCKS, BLOCKS)]
     out[...] = fine
@@ -314,16 +338,11 @@
         out[d] = total[d : d + 1, :]
 
 
-def march_scratch():
-    width = (WINDOW + 2) * LANES
-    return [
-        pltpu.VMEM((ROWS, width), f32),
-        pltpu.VMEM((ROWS, width), f32),
-        pltpu.VMEM((3, 8, width), jnp.int32),
-        pltpu.VMEM((10, 8, width), f32),
-    ]
-
-
+TABLE = (WINDOW + 2) * LANES
+march_scratch = [pltpu.VMEM((ROWS, TABLE), f32)] * 2
+
+
+PACK_BYTES = 63 * 1024 * 1024 + 896 * 1024
 params = pltpu.CompilerParams(vmem_limit_bytes=32 * 1024 * 1024)
 
 
@@ -351,9 +370,18 @@
     restrict_index,
     coarse_inverse,
 ):
-    pack = jnp.concatenate(
-        [states[0], neighbour.astype(f32), edge_x, edge_y, edge_damp, coriolis[None, :]], axis=0
-    )
+    parts = (
+        states.transpose(1, 0, 2), neighbour, edge_x, edge_y, edge_damp, coriolis[None, :]
+    )
+    pack = pl.pallas_call(
+        pack_kernel,
+        out_shape=jax.ShapeDtypeStruct((DOF + 13, CELLS_DEV), f32),
+        in_specs=[pl.BlockSpec(memory_space=pltpu.HBM)] * len(parts),
+        out_specs=vmem,
+        scratch_shapes=[pltpu.VMEM(part.shape, part.dtype) for part in parts]
+        + [pltpu.SemaphoreType.DMA((len(parts),))],
+        compiler_params=pltpu.CompilerParams(vmem_limit_bytes=PACK_BYTES),
+    )(*parts)
     first, second = both_sides(pack)
     slice_here = lax.axis_index("tm")
     where = jnp.stack([slice_here // GROUP, slice_here % GROUP, lax.axis_index("space")])
@@ -373,31 +401,20 @@
         cost_estimate=pl.CostEstimate(flops=4000000, bytes_accessed=200000, transcendentals=0),
     )(pack, index_row, restrict_matrix)
 
-    half = pl.pallas_call(
+    half, places, coefs = pl.pallas_call(
         first_phase_kernel,
-        out_shape=jax.ShapeDtypeStruct((ROWS, CELLS_DEV), f32),
-        in_specs=[smem] + [vmem] * 4,
-        out_specs=vmem,
-        scratch_shapes=march_scratch(),
-        compiler_params=params,
-    )(where, first, pack, second, stencil_terms)
-    half_first, half_second = both_sides(half)
-    fine, message = pl.pallas_call(
-        second_phase_kernel,
         out_shape=(
             jax.ShapeDtypeStruct((ROWS, CELLS_DEV), f32),
-            jax.ShapeDtypeStruct((GROUP * PARTS, 2, LANES), f32),
+            jax.ShapeDtypeStruct((3, 8, TABLE), jnp.int32),
+            jax.ShapeDtypeStruct((10, 8, TABLE), f32),
         ),
-        in_specs=[smem] + [vmem] * 10,
-        out_specs=(vmem, vmem),
-        scratch_shapes=march_scratch(),
-        compiler_params=params,
-    )(
-        where, half_first, half, half_second, first, pack, second, stencil_terms, index_row,
-        restrict_matrix, start,
-    )
-
-    late_inverse, message = lax.optimization_barrier((coarse_inverse, message))
+        in_specs=[smem] + [vmem] * 4,
+        out_specs=(vmem, vmem, vmem),
+        scratch_shapes=march_scratch,
+        compiler_params=params,
+    )(where, first, pack, second, stencil_terms)
+    late_inverse, half = lax.optimization_barrier((coarse_inverse, half))
+    half_first, half_second = both_sides(half)
     operator, operator_twice = pl.pallas_call(
         compose_kernel,
         out_shape=tuple(
@@ -409,6 +426,25 @@
         compiler_params=params,
         cost_estimate=pl.CostEstimate(flops=12000000, bytes_accessed=900000, transcendentals=0),
     )(late_inverse)
+    fine, message = pl.pallas_call(
+        second_phase_kernel,
+        out_shape=(
+            jax.ShapeDtypeStruct((ROWS, CELLS_DEV), f32),
+            jax.ShapeDtypeStruct((GROUP * PARTS, 2, LANES), f32),
+        ),
+        in_specs=[smem] + [vmem] * 9,
+        out_specs=(vmem, vmem),
+        scratch_shapes=march_scratch,
+        compiler_params=params,
+    )(
+        where, half_first, half, half_second, places, coefs, stencil_terms, index_row,
+        restrict_matrix, start,
+    )
+
+    spread_matrix = jnp.pad(prolong_matrix, ((0, ROWS - DOF), (0, 0)))
+    message, operator, operator_twice, spread_matrix, where, index_row = lax.optimization_barrier(
+        (message, operator, operator_twice, spread_matrix, where, index_row)
+    )
     axes = ("tm", "space")
     members = GROUP * PARTS
     inside = [[g * members + m for m in range(members)] for g in range(GROUPS)]
@@ -426,7 +462,6 @@
         compiler_params=params,
     )(where, gathered.reshape(GROUP * PARTS * 2, LANES), operator)
     ends = lax.all_to_all(ends, axes, 0, 0, tiled=True, axis_index_groups=across)
-    spread_matrix = jnp.pad(prolong_matrix, ((0, ROWS - DOF), (0, 0)))
     updated = pl.pallas_call(
         correct_kernel,
         out_shape=jax.ShapeDtypeStruct((DOF, 1, CELLS_DEV), f32),

time: 85.7 us -> 84.5 us (0.986)
  blocking collectives: 0 us -> 29 us
  waiting for transfers between devices: 21.7 us -> 3 us
  starting transfers between devices: 32.2 us -> 20.6 us
  local copies, waits for them, and re-layouts: 1.97 us -> 4.06 us
  Pallas kernels: 28.1 us -> 26.2 us
    all_to_all x0 -> x2, blocking collectives: none -> 29 us  [the longest x1 17.1 us: local(): lax.all_to_all(message, axes, 0, 0, tiled=True, axis_index_groups=inside)]
    all_to_all x2 -> x0, starting transfers between devices: 15 us -> none  [the longest x1 8.04 us: local(): lax.all_to_all(message, axes, 0, 0, tiled=True, axis_index_groups=inside)]
    all_to_all x2 -> x0, waiting for transfers between devices: 12.9 us -> none  [the longest x1 7.87 us: local(): lax.all_to_all(message, axes, 0, 0, tiled=True, axis_index_groups=inside)]
    ppermute x2, waiting for transfers between devices: 4.36 us -> 0.01 us  [both_sides(): lax.ppermute(values, 'space', pairs)]
    unnamed x24 -> x11, local copies, waits for them, and re-layouts: 1.69 us -> 3.98 us
    ppermute x2, starting transfers between devices: 4.02 us -> 6.2 us  [both_sides(): lax.ppermute(values, 'space', pairs)]
    pallas_call x1, Pallas kernels: 10.5 us -> 8.67 us  [local(): pl.pallas_call(second_phase_kernel, out_shape=(jax.ShapeDtypeStruct((ROWS...]
    ppermute x2, waiting for transfers between devices: 4.35 us -> 3 us  [both_sides(): lax.ppermute(values, 'space', others)]
  transfers between devices with their start and end apart: 6 -> 4, of which waited for: 6 -> 1; matrix products, arithmetic and copies ran while one was open for 1% -> 2% of each run, Pallas kernels for 2% -> 3%
where the time goes in v4:
time: 84.5 us; the launch traced here: 84 us
  blocking collectives  29 us (34%)
  Pallas kernels  26.2 us (31%)
  starting transfers between devices  20.6 us (24%)
  local copies, waits for them, and re-layouts  4.06 us (5%)
  waiting for transfers between devices  3 us (4%)
  other arithmetic  0.98 us (1%)
    all_to_all x1, blocking collectives, local(): lax.all_to_all(message, axes, 0, 0, tiled=True, axis_index_groups=inside)  17.1 us
    ppermute x2, starting transfers between devices, both_sides(): lax.ppermute(values, 'space', others)  14.4 us
    all_to_all x1, blocking collectives, local(): lax.all_to_all(ends, axes, 0, 0, tiled=True, axis_index_groups=across)  11.8 us
    pallas_call x1, Pallas kernels, local(): pl.pallas_call(second_phase_kernel, out_shape=(jax.ShapeDtypeStruct((ROWS...  8.67 us
    pallas_call x1, Pallas kernels, local(): pl.pallas_call(first_phase_kernel, out_shape=(jax.ShapeDtypeStruct((ROWS,...  8.3 us
    ppermute x2, starting transfers between devices, both_sides(): lax.ppermute(values, 'space', pairs)  6.2 us
    pallas_call x1, Pallas kernels, local(): pl.pallas_call(correct_kernel, out_shape=jax.ShapeDtypeStruct((DOF, 1, CE...  4.1 us
    unnamed x11, local copies, waits for them, and re-layouts  3.98 us
  transfers between devices with their start and end apart: 4, of which 1 were waited for; matrix products, arithmetic and copies ran while one was open for 2% of the time, Pallas kernels for 3%

profile of v4, /device:TPU:56, one launch (start us, length us, event | category | flops | bytes accessed | tf_op | source)
XLA Modules:
  0.0 84.0 jit_solution(14164769691442636403)
XLA Ops:
  0.0 0.0 copy-start.4
  0.0 1.7 %shard_map.127.centre.pack_ref = f32[34,1024]{1,0:T(8,128)} custom-call(f32[21,1,1024]{2,1,0:T(1,128)} %bitcast.12, s32[3,1024]{1,0:T(4,128)} %refs_1_.1, f32[3,1024]{1,0:T(4,128)} %refs_2_.1, f32[3,1024]{1,0:T(4,128)} %refs_3_.1, f32[3,1024]{1,0:T(4,128)} %refs_4_.1, f32[1,1024]{1,0:T(1,128)} %bitcast.13), custom_call_target="tpu_custom_call" | custom-call | tf_op jit(solution)/shard_map/pallas_call | solution.py:376
  1.7 4.3 %collective-permute-start = (f32[34,1024]{1,0:T(8,128)}, f32[34,1024]{1,0:T(8,128)S(1)}, u32[]{:S(2)}, u32[]{:S(2)}) collective-permute-start(f32[34,1024]{1,0:T(8,128)} %shard_map.127.centre.pack_ref), channel_id=1, source_target_pairs={{0,1},{1,0},{2,3},{3,2},{4,5},{5,4},{6,7},{7,6},{8,9},{9,8},{10,11... | collective-permute-start | bytes 417800 | tf_op jit(solution)/shard_map/ppermute | solution.py:352
  6.0 9.1 %collective-permute-start.1 = (f32[34,1024]{1,0:T(8,128)}, f32[34,1024]{1,0:T(8,128)S(1)}, u32[]{:S(2)}, u32[]{:S(2)}) collective-permute-start(f32[34,1024]{1,0:T(8,128)} %shard_map.127.centre.pack_ref), channel_id=1, source_target_pairs={{0,7},{1,2},{2,1},{3,4},{4,3},{5,6},{6,5},{7,0},{8,15},{9,10},{10,... | collective-permute-start | bytes 417800 | tf_op jit(solution)/shard_map/ppermute | solution.py:352
  15.1 0.1 pad.24.clone
  15.2 0.8 fusion.4
  16.0 0.1 pad_add_fusion.where_ref
  16.1 0.1 pad_maximum_fusion.stencil_ref
  16.2 0.0 collective-permute-done.first
  16.2 3.0 %collective-permute-done.1.second = f32[34,1024]{1,0:T(8,128)S(1)} collective-permute-done((f32[34,1024]{1,0:T(8,128)}, f32[34,1024]{1,0:T(8,128)S(1)}, u32[]{:S(2)}, u32[]{:S(2)}) %collective-permute-start.1) | collective-permute-done | bytes 139296 | tf_op jit(solution)/shard_map/ppermute | solution.py:352
  19.2 0.0 copy-start
  19.2 0.9 %copy-done = f32[34,1024]{1,0:T(8,128)S(1)} copy-done((f32[34,1024]{1,0:T(8,128)S(1)}, f32[34,1024]{1,0:T(8,128)}, u32[]{:S(2)}) %copy-start) | copy-done | bytes 139288
  20.1 8.3 %shard_map.128 = (f32[24,1024]{1,0:T(8,128)S(1)}, s32[3,8,3328]{2,1,0:T(8,128)S(1)}, f32[10,8,3328]{2,1,0:T(8,128)S(1)}) custom-call(s32[3]{0:T(128)S(1)} %pad_add_fusion.where_ref, f32[34,1024]{1,0:T(8,128)S(1)} %collective-permute-done.first, f32[34,1024]{1,0:T(8,128)S(1)} %copy-done, f32[34,1024]{1,0:T(8,128)S(1)} %collective-permute-done.1.second, ...), custom_call_target="tpu_custom_call" | custom-call | tf_op jit(solution)/shard_map/pallas_call | solution.py:404
  28.4 1.9 %collective-permute-start.2 = (f32[24,1024]{1,0:T(8,128)S(1)}, f32[24,1024]{1,0:T(8,128)S(1)}, u32[]{:S(2)}, u32[]{:S(2)}) collective-permute-start(f32[24,1024]{1,0:T(8,128)S(1)} %get-tuple-element.23.centre), channel_id=1, source_target_pairs={{0,1},{1,0},{2,3},{3,2},{4,5},{5,4},{6,7},{7,6},{8,9},{9,8},{10,11... | collective-permute-start | bytes 294920 | tf_op jit(solution)/shard_map/ppermute | solution.py:352
  30.4 5.3 %collective-permute-start.3 = (f32[24,1024]{1,0:T(8,128)S(1)}, f32[24,1024]{1,0:T(8,128)S(1)}, u32[]{:S(2)}, u32[]{:S(2)}) collective-permute-start(f32[24,1024]{1,0:T(8,128)S(1)} %get-tuple-element.23.centre), channel_id=1, source_target_pairs={{0,7},{1,2},{2,1},{3,4},{4,3},{5,6},{6,5},{7,0},{8,15},{9,10},{10,... | collective-permute-start | bytes 294920 | tf_op jit(solution)/shard_map/ppermute | solution.py:352
  35.7 0.8 copy.14
  36.4 0.0 copy-start.1
  36.4 0.9 %copy-done.1 = f32[34,1024]{1,0:T(8,128)S(1)} copy-done((f32[34,1024]{1,0:T(8,128)S(1)}, f32[34,1024]{1,0:T(8,128)}, u32[]{:S(2)}) %copy-start.1) | copy-done | bytes 139288
  37.4 0.0 copy-start.2
  37.4 0.7 copy-done.2
  38.0 0.0 copy-start.3
  38.0 0.7 copy-done.3
  38.7 0.3 shard_map.129.start_ref
  39.0 0.0 copy-done.4
  39.0 1.8 %shard_map.131 = (f32[9,8,8,128]{3,2,1,0:T(8,128)S(1)}, f32[17,8,8,128]{3,2,1,0:T(8,128)S(1)}) custom-call(f32[4,4,256]{2,1,0:T(4,128)S(1)} %copy-done.4), custom_call_target="tpu_custom_call" | custom-call | flops 12000000 | bytes 900000 | tf_op jit(solution)/shard_map/pallas_call | solution.py:418
  40.8 0.0 collective-permute-done.2.first
  40.9 0.0 collective-permute-done.3.second
  40.9 8.7 %shard_map.130 = (f32[24,1024]{1,0:T(8,128)S(1)}, f32[64,2,128]{2,1,0:T(2,128)S(1)}) custom-call(s32[3]{0:T(128)S(1)} %pad_add_fusion.where_ref, f32[24,1024]{1,0:T(8,128)S(1)} %collective-permute-done.2.first, f32[24,1024]{1,0:T(8,128)S(1)} %get-tuple-element.23.centre, f32[24,1024]{1,0:T(8,128)S(1)} %collective-permute-done.3.second, ...), custom_call_target="tpu_custom_call" | custom-call | tf_op jit(solution)/shard_map/pallas_call | solution.py:429
  49.6 17.1 %all_to_all.10 = f32[64,2,128]{2,1,0:T(2,128)S(1)} all-to-all(f32[64,2,128]{2,1,0:T(2,128)S(1)} %get-tuple-element.31), channel_id=1, replica_groups={{0,1,2,3,4,5,6,7,8,9,10,11,12,13,14,15,16,17,18,19,20,21,22,23,24,25,26..., dimensions={0} | all-to-all | bytes 131072 | tf_op jit(solution)/shard_map/all_to_all | solution.py:452
  66.7 1.4 %shard_map.132 = (f32[8,8,128]{2,1,0:T(8,128)S(1)}, f32[2,8,128]{2,1,0:T(8,128)S(1)}) custom-call(s32[3]{0:T(128)S(1)} %pad_add_fusion.where_ref, f32[128,128]{1,0:T(8,128)S(1)} %bitcast.8, f32[9,8,8,128]{3,2,1,0:T(8,128)S(1)} %get-tuple-element.32.operator_ref), custom_call_target="tpu_custom_call" | custom-call | tf_op jit(solution)/shard_map/pallas_call | solution.py:453
  68.1 11.8 %all_to_all.11.ends = f32[8,8,128]{2,1,0:T(8,128)S(1)} all-to-all(f32[8,8,128]{2,1,0:T(8,128)S(1)} %get-tuple-element.33), channel_id=1, replica_groups={{0,64,128,192,256,320,384,448},{1,65,129,193,257,321,385,449},{2,66,130..., dimensions={0} | all-to-all | bytes 65536 | tf_op jit(solution)/shard_map/all_to_all | solution.py:464
  79.9 4.1 %shard_map.133 = f32[21,1,1024]{2,1,0:T(1,128)} custom-call(s32[3]{0:T(128)S(1)} %pad_add_fusion.where_ref, f32[8,8,128]{2,1,0:T(8,128)S(1)} %all_to_all.11.ends, f32[2,8,128]{2,1,0:T(8,128)S(1)} %get-tuple-element.34.own_ref, f32[9,8,8,128]{3,2,1,0:T(8,128)S(1)} %get-tuple-element.32.operator_ref, f32[17,8,8,128]{3,2,1,0:T(8,128)S(1)} %get-tuple-element.35.twice_ref, ...), custom_call_target="tpu_custom_call" | custom-call | tf_op jit(solution)/shard_map/pallas_call | solution.py:465
  (3 shorter events, 0.0 us)
Async XLA Ops:
  0.0 39.0 %copy-start.4 = (f32[4,4,256]{2,1,0:T(4,128)S(1)}, f32[4,4,256]{2,1,0:T(4,128)}, u32[]{:S(2)}) copy-start(f32[4,4,256]{2,1,0:T(4,128)} %inverse_ref) | copy-start | bytes 49156
  1.7 14.5 %collective-permute-start = (f32[34,1024]{1,0:T(8,128)}, f32[34,1024]{1,0:T(8,128)S(1)}, u32[]{:S(2)}, u32[]{:S(2)}) collective-permute-start(f32[34,1024]{1,0:T(8,128)} %shard_map.127.centre.pack_ref), channel_id=1, source_target_pairs={{0,1},{1,0},{2,3},{3,2},{4,5},{5,4},{6,7},{7,6},{8,9},{9,8},{10,11... | collective-permute-start | bytes 417800 | tf_op jit(solution)/shard_map/ppermute | solution.py:352
  6.0 13.2 %collective-permute-start.1 = (f32[34,1024]{1,0:T(8,128)}, f32[34,1024]{1,0:T(8,128)S(1)}, u32[]{:S(2)}, u32[]{:S(2)}) collective-permute-start(f32[34,1024]{1,0:T(8,128)} %shard_map.127.centre.pack_ref), channel_id=1, source_target_pairs={{0,7},{1,2},{2,1},{3,4},{4,3},{5,6},{6,5},{7,0},{8,15},{9,10},{10,... | collective-permute-start | bytes 417800 | tf_op jit(solution)/shard_map/ppermute | solution.py:352
  19.2 0.9 %copy-start = (f32[34,1024]{1,0:T(8,128)S(1)}, f32[34,1024]{1,0:T(8,128)}, u32[]{:S(2)}) copy-start(f32[34,1024]{1,0:T(8,128)} %shard_map.127.centre.pack_ref) | copy-start | bytes 417796
  28.4 12.4 %collective-permute-start.2 = (f32[24,1024]{1,0:T(8,128)S(1)}, f32[24,1024]{1,0:T(8,128)S(1)}, u32[]{:S(2)}, u32[]{:S(2)}) collective-permute-start(f32[24,1024]{1,0:T(8,128)S(1)} %get-tuple-element.23.centre), channel_id=1, source_target_pairs={{0,1},{1,0},{2,3},{3,2},{4,5},{5,4},{6,7},{7,6},{8,9},{9,8},{10,11... | collective-permute-start | bytes 294920 | tf_op jit(solution)/shard_map/ppermute | solution.py:352
  30.4 10.5 %collective-permute-start.3 = (f32[24,1024]{1,0:T(8,128)S(1)}, f32[24,1024]{1,0:T(8,128)S(1)}, u32[]{:S(2)}, u32[]{:S(2)}) collective-permute-start(f32[24,1024]{1,0:T(8,128)S(1)} %get-tuple-element.23.centre), channel_id=1, source_target_pairs={{0,7},{1,2},{2,1},{3,4},{4,3},{5,6},{6,5},{7,0},{8,15},{9,10},{10,... | collective-permute-start | bytes 294920 | tf_op jit(solution)/shard_map/ppermute | solution.py:352
  36.4 0.9 %copy-start.1 = (f32[34,1024]{1,0:T(8,128)S(1)}, f32[34,1024]{1,0:T(8,128)}, u32[]{:S(2)}) copy-start(f32[34,1024]{1,0:T(8,128)} %shard_map.127.centre.pack_ref) | copy-start | bytes 417796
  37.4 0.7 copy-start.2
  38.0 0.7 copy-start.3

commit v5 on v4

--- a/solution.py
+++ b/solution.py
@@ -22,6 +22,7 @@
 BLOCKS = CELLS_DEV // LANES
 PHASE_STEPS = 8
 WINDOW = 3 * BLOCKS
+MESH_END = DOF + 13
 
 coupling = 0.1
 opposite = 0.25
@@ -74,7 +75,7 @@
 
 def fill_tables(odd, mesh_refs, places, coefs):
     lane = lax.broadcasted_iota(jnp.int32, (8, CELLS_DEV), 1) % LANES
-    for part, mesh in enumerate(in_order(odd, mesh_refs, slice(DOF, DOF + 13))):
+    for part, mesh in enumerate(in_order(odd, mesh_refs, slice(DOF, MESH_END))):
         cells = lanes_of(1 + part * BLOCKS, BLOCKS)
         for e in range(3):
             offset = mesh[e : e + 1, :].astype(jnp.int32)
@@ -133,7 +134,7 @@
 
 
 def pack_kernel(*refs):
-    sources, out, buffers, done = refs[:6], refs[6], refs[7:13], refs[13]
+    sources, out, buffers, done = refs[:7], refs[7], refs[8:15], refs[15]
     copies = [
         pltpu.make_async_copy(source, buffer, done.at[i])
         for i, (source, buffer) in enumerate(zip(sources, buffers))
@@ -153,21 +154,7 @@
             row += count
 
 
-def first_phase_kernel(
-    where_ref, first, centre, second, stencil_ref, out, places, coefs, field, middle
-):
-    odd = where_ref[2] % 2 == 1
-    packs = (first, centre, second)
-    fill_tables(odd, packs, places, coefs)
-    fill_field(odd, packs, field)
-    march(field, middle, places, coefs, stencil_ref)
-    out[...] = field[:, lanes_of(1 + BLOCKS, BLOCKS)]
-
-
-def restricted(values, index_row, restrict_matrix):
-    members = (
-        lax.broadcasted_iota(jnp.int32, (COARSE_DEV, CELLS_DEV), 0) == index_row
-    ).astype(f32).astype(bf16)
+def restricted(values, members, restrict_matrix):
     contract = (((1,), (1,)), ((), ()))
     totals = jnp.zeros((ROWS, COARSE_DEV), f32)
     for term in two_terms(values):
@@ -177,19 +164,32 @@
     )[0:1]
     result = jnp.zeros((CDOF, COARSE_DEV), f32)
     for d in range(DOF):
-        result = result + restrict_matrix[:, d : d + 1] * totals[d : d + 1, :]
+        result = result + restrict_matrix[0:CDOF, d : d + 1] * totals[d : d + 1, :]
     result = result / counts
     return jnp.concatenate([result[i : i + 1, :] for i in range(CDOF)], axis=1)
 
 
-def start_kernel(pack_ref, index_ref, matrix_ref, out):
-    inside = lax.broadcasted_iota(jnp.int32, (ROWS, CELLS_DEV), 0) < DOF
-    start = jnp.where(inside, pack_ref[0:ROWS, :], 0.0)
-    out[...] = restricted(start, index_ref[...], matrix_ref[...])
+def first_phase_kernel(
+    where_ref, first, centre, second, stencil_ref, matrix_ref,
+    out, places, coefs, start_out, members_out, field, middle,
+):
+    odd = where_ref[2] % 2 == 1
+    packs = (first, centre, second)
+    fill_tables(odd, packs, places, coefs)
+    fill_field(odd, packs, field)
+    start = field[:, lanes_of(1 + BLOCKS, BLOCKS)]
+    index_row = centre[MESH_END : MESH_END + 1, :].astype(jnp.int32)
+    members = (
+        lax.broadcasted_iota(jnp.int32, (COARSE_DEV, CELLS_DEV), 0) == index_row
+    ).astype(f32).astype(bf16)
+    members_out[...] = members
+    start_out[...] = restricted(start, members, matrix_ref[...])
+    march(field, middle, places, coefs, stencil_ref)
+    out[...] = field[:, lanes_of(1 + BLOCKS, BLOCKS)]
 
 
 def second_phase_kernel(
-    where_ref, first, centre, second, places, coefs, stencil_ref, index_ref, matrix_ref, start_ref,
+    where_ref, first, centre, second, places, coefs, stencil_ref, members_ref, matrix_ref, start_ref,
     out, message, field, middle,
 ):
     fill_field(where_ref[2] % 2 == 1, (first, centre, second), field)
@@ -197,7 +197,7 @@
     fine = field[:, lanes_of(1 + BLOCKS, BLOCKS)]
     out[...] = fine
     rows = jnp.concatenate(
-        [restricted(fine, index_ref[...], matrix_ref[...]), start_ref[...]], axis=0
+        [restricted(fine, members_ref[...], matrix_ref[...]), start_ref[...]], axis=0
     )
     for copy in range(GROUP * PARTS):
         message[copy] = rows
@@ -305,7 +305,7 @@
 
 
 def correct_kernel(
-    where_ref, ends, own_ref, operator_ref, twice_ref, fine_ref, index_ref, matrix_ref, out
+    where_ref, ends, own_ref, operator_ref, twice_ref, fine_ref, members_ref, matrix_ref, out
 ):
     group = where_ref[0]
     place = where_ref[1]
@@ -327,13 +327,10 @@
     for i in range(CDOF):
         chosen = jnp.where(upper, change[2 * i + 1 : 2 * i + 2], change[2 * i : 2 * i + 1])
         spread = spread + matrix_ref[:, i : i + 1] * jnp.broadcast_to(chosen, (ROWS, LANES))
-    members = (
-        lax.broadcasted_iota(jnp.int32, (LANES, CELLS_DEV), 0)
-        == index_ref[...] + COARSE_DEV * (part % 4)
-    ).astype(f32).astype(bf16)
+    spread = pltpu.roll(spread, (4 - part % 4) * COARSE_DEV % LANES, axis=1)[:, 0:COARSE_DEV]
     total = fine_ref[...]
     for term in two_terms(spread):
-        total = total + jnp.dot(term, members, preferred_element_type=f32)
+        total = total + jnp.dot(term, members_ref[...], preferred_element_type=f32)
     for d in range(DOF):
         out[d] = total[d : d + 1, :]
 
@@ -342,7 +339,6 @@
 march_scratch = [pltpu.VMEM((ROWS, TABLE), f32)] * 2
 
 
-PACK_BYTES = 63 * 1024 * 1024 + 896 * 1024
 params = pltpu.CompilerParams(vmem_limit_bytes=32 * 1024 * 1024)
 
 
@@ -371,17 +367,23 @@
     coarse_inverse,
 ):
     parts = (
-        states.transpose(1, 0, 2), neighbour, edge_x, edge_y, edge_damp, coriolis[None, :]
+        states.transpose(1, 0, 2),
+        neighbour,
+        edge_x,
+        edge_y,
+        edge_damp,
+        coriolis[None, :],
+        restrict_index[None, :],
     )
     pack = pl.pallas_call(
         pack_kernel,
-        out_shape=jax.ShapeDtypeStruct((DOF + 13, CELLS_DEV), f32),
+        out_shape=jax.ShapeDtypeStruct((MESH_END + 1, CELLS_DEV), f32),
         in_specs=[pl.BlockSpec(memory_space=pltpu.HBM)] * len(parts),
         out_specs=vmem,
         scratch_shapes=[pltpu.VMEM(part.shape, part.dtype) for part in parts]
         + [pltpu.SemaphoreType.DMA((len(parts),))],
-        compiler_params=pltpu.CompilerParams(vmem_limit_bytes=PACK_BYTES),
-    )(*parts)
+        compiler_params=params,
+    )(*[pltpu.with_memory_space_constraint(part, pltpu.HBM) for part in parts])
     first, second = both_sides(pack)
     slice_here = lax.axis_index("tm")
     where = jnp.stack([slice_here // GROUP, slice_here % GROUP, lax.axis_index("space")])
@@ -391,41 +393,22 @@
     high = stencil.astype(bf16)
     low = (stencil - lax.reduce_precision(stencil, 8, 7)).astype(bf16)
     stencil_terms = jnp.concatenate([high, high, low], axis=1)
-    index_row = restrict_index[None, :]
-    start = pl.pallas_call(
-        start_kernel,
-        out_shape=jax.ShapeDtypeStruct((1, LANES), f32),
-        in_specs=[vmem] * 3,
-        out_specs=vmem,
-        compiler_params=params,
-        cost_estimate=pl.CostEstimate(flops=4000000, bytes_accessed=200000, transcendentals=0),
-    )(pack, index_row, restrict_matrix)
-
-    half, places, coefs = pl.pallas_call(
+    means_matrix = jnp.pad(restrict_matrix, ((0, 4), (0, LANES - DOF)))
+    half, places, coefs, start, members = pl.pallas_call(
         first_phase_kernel,
         out_shape=(
             jax.ShapeDtypeStruct((ROWS, CELLS_DEV), f32),
             jax.ShapeDtypeStruct((3, 8, TABLE), jnp.int32),
             jax.ShapeDtypeStruct((10, 8, TABLE), f32),
+            jax.ShapeDtypeStruct((1, LANES), f32),
+            jax.ShapeDtypeStruct((COARSE_DEV, CELLS_DEV), bf16),
         ),
-        in_specs=[smem] + [vmem] * 4,
-        out_specs=(vmem, vmem, vmem),
+        in_specs=[smem] + [vmem] * 5,
+        out_specs=(vmem,) * 5,
         scratch_shapes=march_scratch,
         compiler_params=params,
-    )(where, first, pack, second, stencil_terms)
-    late_inverse, half = lax.optimization_barrier((coarse_inverse, half))
+    )(where, first, pack, second, stencil_terms, means_matrix)
     half_first, half_second = both_sides(half)
-    operator, operator_twice = pl.pallas_call(
-        compose_kernel,
-        out_shape=tuple(
-            jax.ShapeDtypeStruct((2 * reach + 1, 8, 8, LANES), f32)
-            for reach in (COARSE_STEPS, 2 * COARSE_STEPS)
-        ),
-        in_specs=[vmem],
-        out_specs=(vmem, vmem),
-        compiler_params=params,
-        cost_estimate=pl.CostEstimate(flops=12000000, bytes_accessed=900000, transcendentals=0),
-    )(late_inverse)
     fine, message = pl.pallas_call(
         second_phase_kernel,
         out_shape=(
@@ -437,18 +420,29 @@
         scratch_shapes=march_scratch,
         compiler_params=params,
     )(
-        where, half_first, half, half_second, places, coefs, stencil_terms, index_row,
-        restrict_matrix, start,
-    )
-
-    spread_matrix = jnp.pad(prolong_matrix, ((0, ROWS - DOF), (0, 0)))
-    message, operator, operator_twice, spread_matrix, where, index_row = lax.optimization_barrier(
-        (message, operator, operator_twice, spread_matrix, where, index_row)
-    )
+        where, half_first, half, half_second, places, coefs, stencil_terms, members,
+        means_matrix, start,
+    )
+
+    late_inverse, late_prolong, message = lax.optimization_barrier(
+        (coarse_inverse, prolong_matrix, message)
+    )
+    operator, operator_twice = pl.pallas_call(
+        compose_kernel,
+        out_shape=tuple(
+            jax.ShapeDtypeStruct((2 * reach + 1, 8, 8, LANES), f32)
+            for reach in (COARSE_STEPS, 2 * COARSE_STEPS)
+        ),
+        in_specs=[vmem],
+        out_specs=(vmem, vmem),
+        compiler_params=params,
+        cost_estimate=pl.CostEstimate(flops=12000000, bytes_accessed=900000, transcendentals=0),
+    )(late_inverse)
+    spread_matrix = jnp.pad(late_prolong, ((0, ROWS - DOF), (0, 0)))
     axes = ("tm", "space")
-    members = GROUP * PARTS
-    inside = [[g * members + m for m in range(members)] for g in range(GROUPS)]
-    across = [[g * members + m for g in range(GROUPS)] for m in range(members)]
+    count = GROUP * PARTS
+    inside = [[g * count + m for m in range(count)] for g in range(GROUPS)]
+    across = [[g * count + m for g in range(GROUPS)] for m in range(count)]
     gathered = lax.all_to_all(message, axes, 0, 0, tiled=True, axis_index_groups=inside)
     ends, own = pl.pallas_call(
         group_kernel,
@@ -461,6 +455,7 @@
         scratch_shapes=[pltpu.VMEM((8 * GROUP, LANES), f32)] * 2,
         compiler_params=params,
     )(where, gathered.reshape(GROUP * PARTS * 2, LANES), operator)
+    ends, spread_matrix = lax.optimization_barrier((ends, spread_matrix))
     ends = lax.all_to_all(ends, axes, 0, 0, tiled=True, axis_index_groups=across)
     updated = pl.pallas_call(
         correct_kernel,
@@ -468,7 +463,7 @@
         in_specs=[smem] + [vmem] * 7,
         out_specs=vmem,
         compiler_params=params,
-    )(where, ends, own, operator, operator_twice, fine, index_row, spread_matrix)
+    )(where, ends, own, operator, operator_twice, fine, members, spread_matrix)
     return updated.transpose(1, 0, 2)
 
 

time: 84.5 us -> 81.4 us (0.963)
  blocking collectives: 29 us -> 11.8 us
  waiting for transfers between devices: 3 us -> 16.2 us
  starting transfers between devices: 20.6 us -> 24.9 us
  local copies, waits for them, and re-layouts: 4.06 us -> 0.88 us
    all_to_all x1 -> x0, blocking collectives: 17.1 us -> none  [local(): lax.all_to_all(message, axes, 0, 0, tiled=True, axis_index_groups=inside)]
    all_to_all x0 -> x1, waiting for transfers between devices: none -> 7.98 us  [local(): lax.all_to_all(message, axes, 0, 0, tiled=True, axis_index_groups=inside)]
    all_to_all x0 -> x1, starting transfers between devices: none -> 7.69 us  [local(): lax.all_to_all(message, axes, 0, 0, tiled=True, axis_index_groups=inside)]
    ppermute x2, waiting for transfers between devices: 0.01 us -> 4.37 us  [both_sides(): lax.ppermute(values, 'space', pairs)]
    unnamed x11 -> x4, local copies, waits for them, and re-layouts: 3.98 us -> 0.01 us
    ppermute x2, starting transfers between devices: 6.2 us -> 4.02 us  [both_sides(): lax.ppermute(values, 'space', pairs)]
    ppermute x2, starting transfers between devices: 14.4 us -> 13.2 us  [both_sides(): lax.ppermute(values, 'space', others)]
    pallas_call x2 -> x1, Pallas kernels: 1.93 us -> 0.99 us  [local(): pl.pallas_call(pack_kernel, out_shape=jax.ShapeDtypeStruct((MESH_END + 1,...]
  transfers between devices with their start and end apart: 4 -> 5, of which waited for: 1 -> 5; matrix products, arithmetic and copies ran while one was open for 2% -> 2% of each run, Pallas kernels for 3% -> 2%
where the time goes in v5:
time: 81.4 us; the launch traced here: 81 us
  Pallas kernels  26.1 us (32%)
  starting transfers between devices  24.9 us (31%)
  waiting for transfers between devices  16.2 us (20%)
  blocking collectives  11.8 us (14%)
  other arithmetic  0.98 us (1%)
  local copies, waits for them, and re-layouts  0.88 us (1%)
    ppermute x2, starting transfers between devices, both_sides(): lax.ppermute(values, 'space', others)  13.2 us
    all_to_all x1, blocking collectives, local(): lax.all_to_all(ends, axes, 0, 0, tiled=True, axis_index_groups=across)  11.8 us
    pallas_call x1, Pallas kernels, local(): pl.pallas_call(second_phase_kernel, out_shape=(jax.ShapeDtypeStruct((ROWS...  9.36 us
    pallas_call x1, Pallas kernels, local(): pl.pallas_call(first_phase_kernel, out_shape=(jax.ShapeDtypeStruct((ROWS,...  8.38 us
    all_to_all x1, waiting for transfers between devices, local(): lax.all_to_all(message, axes, 0, 0, tiled=True, axis_index_groups=inside)  7.98 us
    all_to_all x1, starting transfers between devices, local(): lax.all_to_all(message, axes, 0, 0, tiled=True, axis_index_groups=inside)  7.69 us
    ppermute x2, waiting for transfers between devices, both_sides(): lax.ppermute(values, 'space', pairs)  4.37 us
    pallas_call x1, Pallas kernels, local(): pl.pallas_call(correct_kernel, out_shape=jax.ShapeDtypeStruct((DOF, 1, CE...  4.15 us
  transfers between devices with their start and end apart: 5, of which 5 were waited for; matrix products, arithmetic and copies ran while one was open for 2% of the time, Pallas kernels for 2%

profile of v5, /device:TPU:56, one launch (start us, length us, event | category | flops | bytes accessed | tf_op | source)
XLA Modules:
  0.0 81.0 jit_solution(8538124807084157877)
XLA Ops:
  0.0 1.0 %shard_map.127.centre = f32[35,1024]{1,0:T(8,128)S(1)} custom-call(f32[21,1,1024]{2,1,0:T(1,128)} %bitcast.9, s32[3,1024]{1,0:T(4,128)} %refs_1_.1, f32[3,1024]{1,0:T(4,128)} %refs_2_.1, f32[3,1024]{1,0:T(4,128)} %refs_3_.1, f32[3,1024]{1,0:T(4,128)} %refs_4_.1, f32[1,1024]{1,0:T(1,128)} %bitcast.10, s32[1,1024]{1,0:T(1,128)} %bitcast.11), custom_call_target="tpu_custom_call" | custom-call | tf_op jit(solution)/shard_map/pallas_call | solution.py:378
  1.0 10.9 %collective-permute-start.1 = (f32[35,1024]{1,0:T(8,128)S(1)}, f32[35,1024]{1,0:T(8,128)S(1)}, u32[]{:S(2)}, u32[]{:S(2)}) collective-permute-start(f32[35,1024]{1,0:T(8,128)S(1)} %shard_map.127.centre), channel_id=1, source_target_pairs={{0,7},{1,2},{2,1},{3,4},{4,3},{5,6},{6,5},{7,0},{8,15},{9,10},{10,... | collective-permute-start | bytes 430088 | tf_op jit(solution)/shard_map/ppermute | solution.py:348
  12.0 1.9 %collective-permute-start = (f32[35,1024]{1,0:T(8,128)S(1)}, f32[35,1024]{1,0:T(8,128)S(1)}, u32[]{:S(2)}, u32[]{:S(2)}) collective-permute-start(f32[35,1024]{1,0:T(8,128)S(1)} %shard_map.127.centre), channel_id=1, source_target_pairs={{0,1},{1,0},{2,3},{3,2},{4,5},{5,4},{6,7},{7,6},{8,9},{9,8},{10,11... | collective-permute-start | bytes 430088 | tf_op jit(solution)/shard_map/ppermute | solution.py:348
  13.9 0.1 pad.29.clone
  14.0 0.8 %fusion.4 = (bf16[24,80]{1,0:T(8,128)(2,1)S(1)}, f32[24,80]{1,0:T(8,128)S(1)}) fusion(f32[80]{0:T(128)S(1)} %pad.29.clone, f32[21,21]{1,0:T(8,128)} %param.21, f32[21,21]{1,0:T(8,128)} %param.20, f32[21,21]{1,0:T(8,128)} %param.19), kind=kLoop, calls=%fused_computation.14 | loop fusion | flops 26880 | bytes 17132 | tf_op jit(solution)/shard_map/convert_element_type | solution.py:393
  14.8 0.1 pad_add_fusion.where_ref
  14.9 0.7 pad.21.matrix_ref
  15.6 0.1 pad_maximum_fusion.stencil_ref
  15.7 0.5 collective-permute-done.1.second
  16.1 3.4 %collective-permute-done.first = f32[35,1024]{1,0:T(8,128)S(1)} collective-permute-done((f32[35,1024]{1,0:T(8,128)S(1)}, f32[35,1024]{1,0:T(8,128)S(1)}, u32[]{:S(2)}, u32[]{:S(2)}) %collective-permute-start) | collective-permute-done | bytes 143392 | tf_op jit(solution)/shard_map/ppermute | solution.py:348
  19.5 8.4 %shard_map.128 = (f32[24,1024]{1,0:T(8,128)S(1)}, s32[3,8,3328]{2,1,0:T(8,128)S(1)}, f32[10,8,3328]{2,1,0:T(8,128)S(1)}, f32[1,128]{1,0:T(1,128)S(1)}, bf16[32,1024]{1,0:T(8,128)(2,1)S(1)}) custom-call(s32[3]{0:T(128)S(1)} %pad_add_fusion.where_ref, f32[35,1024]{1,0:T(8,128)S(1)} %collective-permute-done.first, f32[35,1024]{1,0:T(8,128)S(1)} %shard_map.127.centre, ...), custom_call_target="tpu_custom_call" | custom-call | tf_op jit(solution)/shard_map/pallas_call | solution.py:397
  27.9 0.0 copy-start.1
  27.9 0.0 copy-start
  27.9 2.2 %collective-permute-start.3 = (f32[24,1024]{1,0:T(8,128)S(1)}, f32[24,1024]{1,0:T(8,128)S(1)}, u32[]{:S(2)}, u32[]{:S(2)}) collective-permute-start(f32[24,1024]{1,0:T(8,128)S(1)} %get-tuple-element.21.centre), channel_id=1, source_target_pairs={{0,7},{1,2},{2,1},{3,4},{4,3},{5,6},{6,5},{7,0},{8,15},{9,10},{10,... | collective-permute-start | bytes 294920 | tf_op jit(solution)/shard_map/ppermute | solution.py:348
  30.1 2.1 %collective-permute-start.2 = (f32[24,1024]{1,0:T(8,128)S(1)}, f32[24,1024]{1,0:T(8,128)S(1)}, u32[]{:S(2)}, u32[]{:S(2)}) collective-permute-start(f32[24,1024]{1,0:T(8,128)S(1)} %get-tuple-element.21.centre), channel_id=1, source_target_pairs={{0,1},{1,0},{2,3},{3,2},{4,5},{5,4},{6,7},{7,6},{8,9},{9,8},{10,11... | collective-permute-start | bytes 294920 | tf_op jit(solution)/shard_map/ppermute | solution.py:348
  32.2 3.4 %collective-permute-done.3.second = f32[24,1024]{1,0:T(8,128)S(1)} collective-permute-done((f32[24,1024]{1,0:T(8,128)S(1)}, f32[24,1024]{1,0:T(8,128)S(1)}, u32[]{:S(2)}, u32[]{:S(2)}) %collective-permute-start.3) | collective-permute-done | bytes 98336 | tf_op jit(solution)/shard_map/ppermute | solution.py:348
  35.6 1.0 %collective-permute-done.2.first = f32[24,1024]{1,0:T(8,128)S(1)} collective-permute-done((f32[24,1024]{1,0:T(8,128)S(1)}, f32[24,1024]{1,0:T(8,128)S(1)}, u32[]{:S(2)}, u32[]{:S(2)}) %collective-permute-start.2) | collective-permute-done | bytes 98336 | tf_op jit(solution)/shard_map/ppermute | solution.py:348
  36.6 9.4 %shard_map.129 = (f32[24,1024]{1,0:T(8,128)S(1)}, f32[64,2,128]{2,1,0:T(2,128)}) custom-call(s32[3]{0:T(128)S(1)} %pad_add_fusion.where_ref, f32[24,1024]{1,0:T(8,128)S(1)} %collective-permute-done.2.first, f32[24,1024]{1,0:T(8,128)S(1)} %get-tuple-element.21.centre, f32[24,1024]{1,0:T(8,128)S(1)} %collective-permute-done.3.second, ...), custom_call_target="tpu_custom_call" | custom-call | tf_op jit(solution)/shard_map/pallas_call | solution.py:412
  46.0 7.7 %all-to-all-start = ((f32[64,2,128]{2,1,0:T(2,128)}), f32[64,2,128]{2,1,0:T(2,128)S(1)}, u32[]{:S(2)}, u32[]{:S(2)}) async-start(f32[64,2,128]{2,1,0:T(2,128)} %get-tuple-element.27), calls=%async_computation | async-start | bytes 131072 | tf_op jit(solution)/shard_map/all_to_all | solution.py:446
  53.7 0.0 copy-done.1
  53.7 0.1 copy.14
  53.8 0.0 copy-done
  53.8 1.8 %shard_map.130 = (f32[9,8,8,128]{3,2,1,0:T(8,128)S(1)}, f32[17,8,8,128]{3,2,1,0:T(8,128)S(1)}) custom-call(f32[4,4,256]{2,1,0:T(4,128)S(1)} %copy-done), custom_call_target="tpu_custom_call" | custom-call | flops 12000000 | bytes 900000 | tf_op jit(solution)/shard_map/pallas_call | solution.py:430
  55.6 8.0 %all-to-all-done = f32[64,2,128]{2,1,0:T(2,128)S(1)} async-done(((f32[64,2,128]{2,1,0:T(2,128)}), f32[64,2,128]{2,1,0:T(2,128)S(1)}, u32[]{:S(2)}, u32[]{:S(2)}) %all-to-all-start) | async-done | bytes 65568 | tf_op jit(solution)/shard_map/all_to_all | solution.py:446
  63.6 1.4 %shard_map.131 = (f32[8,8,128]{2,1,0:T(8,128)S(1)}, f32[2,8,128]{2,1,0:T(8,128)S(1)}) custom-call(s32[3]{0:T(128)S(1)} %pad_add_fusion.where_ref, f32[128,128]{1,0:T(8,128)S(1)} %bitcast.8, f32[9,8,8,128]{3,2,1,0:T(8,128)S(1)} %get-tuple-element.29.operator_ref), custom_call_target="tpu_custom_call" | custom-call | tf_op jit(solution)/shard_map/pallas_call | solution.py:447
  65.0 11.8 %all_to_all.10.ends = f32[8,8,128]{2,1,0:T(8,128)S(1)} all-to-all(f32[8,8,128]{2,1,0:T(8,128)S(1)} %get-tuple-element.32), channel_id=1, replica_groups={{0,64,128,192,256,320,384,448},{1,65,129,193,257,321,385,449},{2,66,130..., dimensions={0} | all-to-all | bytes 65536 | tf_op jit(solution)/shard_map/all_to_all | solution.py:459
  76.8 4.1 %shard_map.132 = f32[21,1,1024]{2,1,0:T(1,128)} custom-call(s32[3]{0:T(128)S(1)} %pad_add_fusion.where_ref, f32[8,8,128]{2,1,0:T(8,128)S(1)} %all_to_all.10.ends, f32[2,8,128]{2,1,0:T(8,128)S(1)} %get-tuple-element.33.own_ref, f32[9,8,8,128]{3,2,1,0:T(8,128)S(1)} %get-tuple-element.29.operator_ref, f32[17,8,8,128]{3,2,1,0:T(8,128)S(1)} %get-tuple-element.34.twice_ref, ...), custom_call_target="tpu_custom_call" | custom-call | tf_op jit(solution)/shard_map/pallas_call | solution.py:460
  (3 shorter events, 0.0 us)
Async XLA Ops:
  1.0 15.1 %collective-permute-start.1 = (f32[35,1024]{1,0:T(8,128)S(1)}, f32[35,1024]{1,0:T(8,128)S(1)}, u32[]{:S(2)}, u32[]{:S(2)}) collective-permute-start(f32[35,1024]{1,0:T(8,128)S(1)} %shard_map.127.centre), channel_id=1, source_target_pairs={{0,7},{1,2},{2,1},{3,4},{4,3},{5,6},{6,5},{7,0},{8,15},{9,10},{10,... | collective-permute-start | bytes 430088 | tf_op jit(solution)/shard_map/ppermute | solution.py:348
  12.0 7.6 %collective-permute-start = (f32[35,1024]{1,0:T(8,128)S(1)}, f32[35,1024]{1,0:T(8,128)S(1)}, u32[]{:S(2)}, u32[]{:S(2)}) collective-permute-start(f32[35,1024]{1,0:T(8,128)S(1)} %shard_map.127.centre), channel_id=1, source_target_pairs={{0,1},{1,0},{2,3},{3,2},{4,5},{5,4},{6,7},{7,6},{8,9},{9,8},{10,11... | collective-permute-start | bytes 430088 | tf_op jit(solution)/shard_map/ppermute | solution.py:348
  27.9 25.8 %copy-start.1 = (f32[21,4]{0,1:T(4,128)S(1)}, f32[21,4]{0,1:T(4,128)}, u32[]{:S(2)}) copy-start(f32[21,4]{0,1:T(4,128)} %param.23) | copy-start | bytes 1012
  27.9 25.9 %copy-start = (f32[4,4,256]{2,1,0:T(4,128)S(1)}, f32[4,4,256]{2,1,0:T(4,128)}, u32[]{:S(2)}) copy-start(f32[4,4,256]{2,1,0:T(4,128)} %inverse_ref) | copy-start | bytes 49156
  27.9 7.7 %collective-permute-start.3 = (f32[24,1024]{1,0:T(8,128)S(1)}, f32[24,1024]{1,0:T(8,128)S(1)}, u32[]{:S(2)}, u32[]{:S(2)}) collective-permute-start(f32[24,1024]{1,0:T(8,128)S(1)} %get-tuple-element.21.centre), channel_id=1, source_target_pairs={{0,7},{1,2},{2,1},{3,4},{4,3},{5,6},{6,5},{7,0},{8,15},{9,10},{10,... | collective-permute-start | bytes 294920 | tf_op jit(solution)/shard_map/ppermute | solution.py:348
  30.1 6.5 %collective-permute-start.2 = (f32[24,1024]{1,0:T(8,128)S(1)}, f32[24,1024]{1,0:T(8,128)S(1)}, u32[]{:S(2)}, u32[]{:S(2)}) collective-permute-start(f32[24,1024]{1,0:T(8,128)S(1)} %get-tuple-element.21.centre), channel_id=1, source_target_pairs={{0,1},{1,0},{2,3},{3,2},{4,5},{5,4},{6,7},{7,6},{8,9},{9,8},{10,11... | collective-permute-start | bytes 294920 | tf_op jit(solution)/shard_map/ppermute | solution.py:348
  46.0 17.6 %all-to-all-start = ((f32[64,2,128]{2,1,0:T(2,128)}), f32[64,2,128]{2,1,0:T(2,128)S(1)}, u32[]{:S(2)}, u32[]{:S(2)}) async-start(f32[64,2,128]{2,1,0:T(2,128)} %get-tuple-element.27), calls=%async_computation | async-start | bytes 131072 | tf_op jit(solution)/shard_map/all_to_all | solution.py:446

commit v6 on v5

--- a/solution.py
+++ b/solution.py
@@ -154,6 +154,12 @@
             row += count
 
 
+def added(terms):
+    while len(terms) > 1:
+        terms = [sum(terms[i : i + 2][1:], terms[i]) for i in range(0, len(terms), 2)]
+    return terms[0]
+
+
 def restricted(values, members, restrict_matrix):
     contract = (((1,), (1,)), ((), ()))
     totals = jnp.zeros((ROWS, COARSE_DEV), f32)
@@ -162,9 +168,9 @@
     counts = lax.dot_general(
         jnp.ones((16, CELLS_DEV), bf16), members, contract, preferred_element_type=f32
     )[0:1]
-    result = jnp.zeros((CDOF, COARSE_DEV), f32)
-    for d in range(DOF):
-        result = result + restrict_matrix[0:CDOF, d : d + 1] * totals[d : d + 1, :]
+    result = added(
+        [restrict_matrix[0:CDOF, d : d + 1] * totals[d : d + 1, :] for d in range(DOF)]
+    )
     result = result / counts
     return jnp.concatenate([result[i : i + 1, :] for i in range(CDOF)], axis=1)
 
@@ -209,11 +215,10 @@
     return jnp.where(even_row, up, down)
 
 
-def compose_kernel(inverse_ref, out, out_twice):
+def composed(reach, inverse_ref, first, last):
     shape = (8, 8, LANES)
     row = lax.broadcasted_iota(jnp.int32, shape, 1)
     lane = lax.broadcasted_iota(jnp.int32, shape, 2)
-    turn = lax.broadcasted_iota(jnp.int32, shape, 0)
     even_row = row % 2 == 0
     first_lane = lane == 0
     last_lane = lane == LANES - 1
@@ -226,8 +231,7 @@
             for h in range(2):
                 pieces.append(inverse_ref[i, j : j + 1, lanes_of(h)])
         blocks.append(jnp.concatenate(pieces, axis=0)[None])
-    reach = {0: jnp.where(turn == 0, 1.0, 0.0)}
-    for repeat in range(2 * COARSE_STEPS):
+    for repeat in range(first, last):
         swapped = {o: flipped(tiles, even_row) for o, tiles in reach.items()}
         blended = {}
         for o in range(-repeat - 1, repeat + 2):
@@ -248,19 +252,31 @@
                 turned = jnp.concatenate([tiles[8 - 2 * by :], tiles[: 8 - 2 * by]], axis=0)
                 total = total + blocks[by] * pltpu.roll(turned, 2 * by, axis=1)
             reach[o] = total
-        if (repeat + 1) % COARSE_STEPS == 0:
-            held = out if repeat < COARSE_STEPS else out_twice
-            for o, tiles in reach.items():
-                held[o + repeat + 1] = tiles if o == 0 else pltpu.roll(tiles, -o % LANES, axis=2)
-
-
-def added(terms):
-    while len(terms) > 1:
-        terms = [sum(terms[i : i + 2][1:], terms[i]) for i in range(0, len(terms), 2)]
-    return terms[0]
-
-
-def coarse_slice(vector, operator_ref):
+    return reach
+
+
+def keep_operator(out, reach):
+    size = max(reach)
+    for o, tiles in reach.items():
+        out[o + size] = tiles if o == 0 else pltpu.roll(tiles, -o % LANES, axis=2)
+
+
+def compose_kernel(inverse_ref, out, half_way):
+    turn = lax.broadcasted_iota(jnp.int32, (8, 8, LANES), 0)
+    reach = composed({0: jnp.where(turn == 0, 1.0, 0.0)}, inverse_ref, 0, COARSE_STEPS)
+    keep_operator(out, reach)
+    reach = composed(reach, inverse_ref, COARSE_STEPS, 2 * COARSE_STEPS)
+    for o, tiles in reach.items():
+        half_way[o + 2 * COARSE_STEPS] = tiles
+
+
+def extend_kernel(half_way, inverse_ref, out):
+    size = 2 * COARSE_STEPS
+    reach = {o: half_way[o + size] for o in range(-size, size + 1)}
+    keep_operator(out, composed(reach, inverse_ref, size, 2 * size))
+
+
+def coarse_slices(vector, operator_ref):
     turns = [vector] + [pltpu.roll(vector, d, axis=0) for d in range(1, 8)]
     reach = operator_ref.shape[0] // 2
     shares = []
@@ -292,11 +308,11 @@
     chain = None
     own = jnp.zeros((8, LANES), f32)
     for n in range(GROUP):
-        coarse = coarse_slice(of_slice(start, n), operator_ref)
+        coarse = coarse_slices(of_slice(start, n), operator_ref)
         if n == 0:
             coarse = jnp.where(group > 0, coarse, 0.0)
         jump = of_slice(finish, n) - coarse
-        chain = jump if n == 0 else coarse_slice(chain, operator_ref) + jump
+        chain = jump if n == 0 else coarse_slices(chain, operator_ref) + jump
         own = jnp.where(place == n, chain, own)
     for copy in range(GROUPS):
         ends_out[copy] = chain
@@ -305,21 +321,21 @@
 
 
 def correct_kernel(
-    where_ref, ends, own_ref, operator_ref, twice_ref, fine_ref, members_ref, matrix_ref, out
+    where_ref, ends, own_ref, operator_ref, fourfold_ref, fine_ref, members_ref, matrix_ref, out
 ):
     group = where_ref[0]
     place = where_ref[1]
     part = where_ref[2]
 
     def advance(count, vector, ref):
-        return lax.fori_loop(0, count, lambda n, now: coarse_slice(now, ref), vector)
+        return lax.fori_loop(0, count, lambda n, now: coarse_slices(now, ref), vector)
 
     def link(k, vector):
-        return advance(GROUP // 2, vector, twice_ref) + ends[k]
+        return advance(GROUP // 4, vector, fourfold_ref) + ends[k]
 
     before = lax.fori_loop(1, group, link, ends[0])
     count = jnp.where(group > 0, place + 1, 0)
-    before = advance(count % 2, advance(count // 2, before, twice_ref), operator_ref)
+    before = advance(count % 4, advance(count // 4, before, fourfold_ref), operator_ref)
     chain = own_ref[0] + jnp.where(group > 0, before, 0.0)
     change = chain - own_ref[1]
     upper = part >= PARTS // 2
@@ -409,25 +425,8 @@
         compiler_params=params,
     )(where, first, pack, second, stencil_terms, means_matrix)
     half_first, half_second = both_sides(half)
-    fine, message = pl.pallas_call(
-        second_phase_kernel,
-        out_shape=(
-            jax.ShapeDtypeStruct((ROWS, CELLS_DEV), f32),
-            jax.ShapeDtypeStruct((GROUP * PARTS, 2, LANES), f32),
-        ),
-        in_specs=[smem] + [vmem] * 9,
-        out_specs=(vmem, vmem),
-        scratch_shapes=march_scratch,
-        compiler_params=params,
-    )(
-        where, half_first, half, half_second, places, coefs, stencil_terms, members,
-        means_matrix, start,
-    )
-
-    late_inverse, late_prolong, message = lax.optimization_barrier(
-        (coarse_inverse, prolong_matrix, message)
-    )
-    operator, operator_twice = pl.pallas_call(
+    late_inverse, half = lax.optimization_barrier((coarse_inverse, half))
+    operator, half_way = pl.pallas_call(
         compose_kernel,
         out_shape=tuple(
             jax.ShapeDtypeStruct((2 * reach + 1, 8, 8, LANES), f32)
@@ -438,12 +437,39 @@
         compiler_params=params,
         cost_estimate=pl.CostEstimate(flops=12000000, bytes_accessed=900000, transcendentals=0),
     )(late_inverse)
+    fine, message = pl.pallas_call(
+        second_phase_kernel,
+        out_shape=(
+            jax.ShapeDtypeStruct((ROWS, CELLS_DEV), f32),
+            pltpu.VMEM((GROUP * PARTS, 2, LANES), f32),
+        ),
+        in_specs=[smem] + [vmem] * 9,
+        out_specs=(vmem, vmem),
+        scratch_shapes=march_scratch,
+        compiler_params=params,
+    )(
+        where, half_first, half, half_second, places, coefs, stencil_terms, members,
+        means_matrix, start,
+    )
+
+    half_way, late_prolong, message = lax.optimization_barrier(
+        (half_way, prolong_matrix, message)
+    )
+    fourfold = pl.pallas_call(
+        extend_kernel,
+        out_shape=jax.ShapeDtypeStruct((8 * COARSE_STEPS + 1, 8, 8, LANES), f32),
+        in_specs=[vmem, vmem],
+        out_specs=vmem,
+        compiler_params=params,
+        cost_estimate=pl.CostEstimate(flops=30000000, bytes_accessed=1700000, transcendentals=0),
+    )(half_way, coarse_inverse)
     spread_matrix = jnp.pad(late_prolong, ((0, ROWS - DOF), (0, 0)))
     axes = ("tm", "space")
     count = GROUP * PARTS
     inside = [[g * count + m for m in range(count)] for g in range(GROUPS)]
     across = [[g * count + m for g in range(GROUPS)] for m in range(count)]
     gathered = lax.all_to_all(message, axes, 0, 0, tiled=True, axis_index_groups=inside)
+    gathered, fourfold, spread_matrix = lax.optimization_barrier((gathered, fourfold, spread_matrix))
     ends, own = pl.pallas_call(
         group_kernel,
         out_shape=(
@@ -455,7 +481,6 @@
         scratch_shapes=[pltpu.VMEM((8 * GROUP, LANES), f32)] * 2,
         compiler_params=params,
     )(where, gathered.reshape(GROUP * PARTS * 2, LANES), operator)
-    ends, spread_matrix = lax.optimization_barrier((ends, spread_matrix))
     ends = lax.all_to_all(ends, axes, 0, 0, tiled=True, axis_index_groups=across)
     updated = pl.pallas_call(
         correct_kernel,
@@ -463,7 +488,7 @@
         in_specs=[smem] + [vmem] * 7,
         out_specs=vmem,
         compiler_params=params,
-    )(where, ends, own, operator, operator_twice, fine, members, spread_matrix)
+    )(where, ends, own, operator, fourfold, fine, members, spread_matrix)
     return updated.transpose(1, 0, 2)
 
 

time: 81.4 us -> 81.8 us (level)
  waiting for transfers between devices: 16.2 us -> 6.86 us
  starting transfers between devices: 24.9 us -> 29.3 us
  Pallas kernels: 26.1 us -> 29.9 us
    pallas_call x0 -> x1, Pallas kernels: none -> 4.85 us  [local(): pl.pallas_call(extend_kernel, out_shape=jax.ShapeDtypeStruct((8 * COARSE_...]
    ppermute x2, waiting for transfers between devices: 4.37 us -> 0.01 us  [both_sides(): lax.ppermute(values, 'space', pairs)]
    all_to_all x1, waiting for transfers between devices: 7.98 us -> 4.75 us  [local(): lax.all_to_all(message, axes, 0, 0, tiled=True, axis_index_groups=inside)]
    ppermute x2, starting transfers between devices: 4.02 us -> 6.2 us  [both_sides(): lax.ppermute(values, 'space', pairs)]
    ppermute x2, waiting for transfers between devices: 3.86 us -> 2.1 us  [both_sides(): lax.ppermute(values, 'space', others)]
    ppermute x2, starting transfers between devices: 13.2 us -> 14.4 us  [both_sides(): lax.ppermute(values, 'space', others)]
    all_to_all x1, starting transfers between devices: 7.69 us -> 8.72 us  [local(): lax.all_to_all(message, axes, 0, 0, tiled=True, axis_index_groups=inside)]
    pallas_call x1, Pallas kernels: 4.15 us -> 3.26 us  [local(): pl.pallas_call(correct_kernel, out_shape=jax.ShapeDtypeStruct((DOF, 1, CE...]
  transfers between devices with their start and end apart: 5 -> 5, of which waited for: 5 -> 2; matrix products, arithmetic and copies ran while one was open for 2% -> 2% of each run, Pallas kernels for 2% -> 8%
where the time goes in v6:
time: 81.8 us; the launch traced here: 80.7 us
  Pallas kernels  29.9 us (37%)
  starting transfers between devices  29.3 us (36%)
  blocking collectives  11.8 us (14%)
  waiting for transfers between devices  6.86 us (8%)
  local copies, waits for them, and re-layouts  1.59 us (2%)
  other arithmetic  0.98 us (1%)
    ppermute x2, starting transfers between devices, both_sides(): lax.ppermute(values, 'space', others)  14.4 us
    all_to_all x1, blocking collectives, local(): lax.all_to_all(ends, axes, 0, 0, tiled=True, axis_index_groups=across)  11.8 us
    pallas_call x1, Pallas kernels, local(): pl.pallas_call(second_phase_kernel, out_shape=(jax.ShapeDtypeStruct((ROWS...  9.33 us
    all_to_all x1, starting transfers between devices, local(): lax.all_to_all(message, axes, 0, 0, tiled=True, axis_index_groups=inside)  8.72 us
    pallas_call x1, Pallas kernels, local(): pl.pallas_call(first_phase_kernel, out_shape=(jax.ShapeDtypeStruct((ROWS,...  8.37 us
    ppermute x2, starting transfers between devices, both_sides(): lax.ppermute(values, 'space', pairs)  6.2 us
    pallas_call x1, Pallas kernels, local(): pl.pallas_call(extend_kernel, out_shape=jax.ShapeDtypeStruct((8 * COARSE_...  4.85 us
    all_to_all x1, waiting for transfers between devices, local(): lax.all_to_all(message, axes, 0, 0, tiled=True, axis_index_groups=inside)  4.75 us
  transfers between devices with their start and end apart: 5, of which 2 were waited for; matrix products, arithmetic and copies ran while one was open for 2% of the time, Pallas kernels for 8%

profile of v6, /device:TPU:56, one launch (start us, length us, event | category | flops | bytes accessed | tf_op | source)
XLA Modules:
  0.0 80.7 jit_solution(2476277842704994205)
XLA Ops:
  0.0 1.0 %shard_map.127.centre = f32[35,1024]{1,0:T(8,128)S(1)} custom-call(f32[21,1,1024]{2,1,0:T(1,128)} %bitcast.9, s32[3,1024]{1,0:T(4,128)} %refs_1_.1, f32[3,1024]{1,0:T(4,128)} %refs_2_.1, f32[3,1024]{1,0:T(4,128)} %refs_3_.1, f32[3,1024]{1,0:T(4,128)} %refs_4_.1, f32[1,1024]{1,0:T(1,128)} %bitcast.10, s32[1,1024]{1,0:T(1,128)} %bitcast.11), custom_call_target="tpu_custom_call" | custom-call | tf_op jit(solution)/shard_map/pallas_call | solution.py:394
  1.0 4.3 %collective-permute-start = (f32[35,1024]{1,0:T(8,128)S(1)}, f32[35,1024]{1,0:T(8,128)S(1)}, u32[]{:S(2)}, u32[]{:S(2)}) collective-permute-start(f32[35,1024]{1,0:T(8,128)S(1)} %shard_map.127.centre), channel_id=1, source_target_pairs={{0,1},{1,0},{2,3},{3,2},{4,5},{5,4},{6,7},{7,6},{8,9},{9,8},{10,11... | collective-permute-start | bytes 430088 | tf_op jit(solution)/shard_map/ppermute | solution.py:364
  5.3 9.1 %collective-permute-start.1 = (f32[35,1024]{1,0:T(8,128)S(1)}, f32[35,1024]{1,0:T(8,128)S(1)}, u32[]{:S(2)}, u32[]{:S(2)}) collective-permute-start(f32[35,1024]{1,0:T(8,128)S(1)} %shard_map.127.centre), channel_id=1, source_target_pairs={{0,7},{1,2},{2,1},{3,4},{4,3},{5,6},{6,5},{7,0},{8,15},{9,10},{10,... | collective-permute-start | bytes 430088 | tf_op jit(solution)/shard_map/ppermute | solution.py:364
  14.4 0.1 pad.29.clone
  14.5 0.8 %fusion.4 = (bf16[24,80]{1,0:T(8,128)(2,1)S(1)}, f32[24,80]{1,0:T(8,128)S(1)}) fusion(f32[80]{0:T(128)S(1)} %pad.29.clone, f32[21,21]{1,0:T(8,128)} %param.21, f32[21,21]{1,0:T(8,128)} %param.20, f32[21,21]{1,0:T(8,128)} %param.19), kind=kLoop, calls=%fused_computation.14 | loop fusion | flops 26880 | bytes 17132 | tf_op jit(solution)/shard_map/convert_element_type | solution.py:409
  15.4 0.1 pad_add_fusion.where_ref
  15.4 0.7 pad.21.matrix_ref
  16.1 0.1 pad_maximum_fusion.stencil_ref
  16.2 0.0 collective-permute-done.first
  16.2 2.1 %collective-permute-done.1.second = f32[35,1024]{1,0:T(8,128)S(1)} collective-permute-done((f32[35,1024]{1,0:T(8,128)S(1)}, f32[35,1024]{1,0:T(8,128)S(1)}, u32[]{:S(2)}, u32[]{:S(2)}) %collective-permute-start.1) | collective-permute-done | bytes 143392 | tf_op jit(solution)/shard_map/ppermute | solution.py:364
  18.3 0.0 copy-start.2
  18.3 0.0 copy-start.1
  18.3 8.4 %shard_map.128 = (f32[24,1024]{1,0:T(8,128)S(1)}, s32[3,8,3328]{2,1,0:T(8,128)S(1)}, f32[10,8,3328]{2,1,0:T(8,128)S(1)}, f32[1,128]{1,0:T(1,128)S(1)}, bf16[32,1024]{1,0:T(8,128)(2,1)S(1)}) custom-call(s32[3]{0:T(128)S(1)} %pad_add_fusion.where_ref, f32[35,1024]{1,0:T(8,128)S(1)} %collective-permute-done.first, f32[35,1024]{1,0:T(8,128)S(1)} %shard_map.127.centre, ...), custom_call_target="tpu_custom_call" | custom-call | tf_op jit(solution)/shard_map/pallas_call | solution.py:413
  26.7 1.9 %collective-permute-start.2 = (f32[24,1024]{1,0:T(8,128)S(1)}, f32[24,1024]{1,0:T(8,128)S(1)}, u32[]{:S(2)}, u32[]{:S(2)}) collective-permute-start(f32[24,1024]{1,0:T(8,128)S(1)} %get-tuple-element.27.centre), channel_id=1, source_target_pairs={{0,1},{1,0},{2,3},{3,2},{4,5},{5,4},{6,7},{7,6},{8,9},{9,8},{10,11... | collective-permute-start | bytes 294920 | tf_op jit(solution)/shard_map/ppermute | solution.py:364
  28.6 5.3 %collective-permute-start.3 = (f32[24,1024]{1,0:T(8,128)S(1)}, f32[24,1024]{1,0:T(8,128)S(1)}, u32[]{:S(2)}, u32[]{:S(2)}) collective-permute-start(f32[24,1024]{1,0:T(8,128)S(1)} %get-tuple-element.27.centre), channel_id=1, source_target_pairs={{0,7},{1,2},{2,1},{3,4},{4,3},{5,6},{6,5},{7,0},{8,15},{9,10},{10,... | collective-permute-start | bytes 294920 | tf_op jit(solution)/shard_map/ppermute | solution.py:364
  33.9 0.0 copy-start
  33.9 0.7 copy-done
  34.6 1.8 %shard_map.129 = (f32[9,8,8,128]{3,2,1,0:T(8,128)S(1)}, f32[17,8,8,128]{3,2,1,0:T(8,128)S(1)}) custom-call(f32[4,4,256]{2,1,0:T(4,128)S(1)} %copy-done), custom_call_target="tpu_custom_call" | custom-call | flops 12000000 | bytes 900000 | tf_op jit(solution)/shard_map/pallas_call | solution.py:429
  36.4 0.0 collective-permute-done.2.first
  36.4 0.0 collective-permute-done.3.second
  36.4 9.3 %shard_map.130 = (f32[24,1024]{1,0:T(8,128)S(1)}, f32[64,2,128]{2,1,0:T(2,128)}) custom-call(s32[3]{0:T(128)S(1)} %pad_add_fusion.where_ref, f32[24,1024]{1,0:T(8,128)S(1)} %collective-permute-done.2.first, f32[24,1024]{1,0:T(8,128)S(1)} %get-tuple-element.27.centre, f32[24,1024]{1,0:T(8,128)S(1)} %collective-permute-done.3.second, ...), custom_call_target="tpu_custom_call" | custom-call | tf_op jit(solution)/shard_map/pallas_call | solution.py:440
  45.8 8.7 %all-to-all-start = ((f32[64,2,128]{2,1,0:T(2,128)}), f32[64,2,128]{2,1,0:T(2,128)S(1)}, u32[]{:S(2)}, u32[]{:S(2)}) async-start(f32[64,2,128]{2,1,0:T(2,128)} %get-tuple-element.33), calls=%async_computation | async-start | bytes 131072 | tf_op jit(solution)/shard_map/all_to_all | solution.py:471
  54.5 0.0 copy-done.2
  54.5 0.1 copy.14
  54.6 0.0 copy-done.1
  54.6 4.8 %shard_map.131.fourfold_ref = f32[33,8,8,128]{3,2,1,0:T(8,128)S(1)} custom-call(f32[17,8,8,128]{3,2,1,0:T(8,128)S(1)} %get-tuple-element.34.half_way, f32[4,4,256]{2,1,0:T(4,128)S(1)} %copy-done.1), custom_call_target="tpu_custom_call" | custom-call | flops 30000000 | bytes 1700000 | tf_op jit(solution)/shard_map/pallas_call | solution.py:458
  59.5 4.7 %all-to-all-done = f32[64,2,128]{2,1,0:T(2,128)S(1)} async-done(((f32[64,2,128]{2,1,0:T(2,128)}), f32[64,2,128]{2,1,0:T(2,128)S(1)}, u32[]{:S(2)}, u32[]{:S(2)}) %all-to-all-start) | async-done | bytes 65568 | tf_op jit(solution)/shard_map/all_to_all | solution.py:471
  64.2 1.4 %shard_map.132 = (f32[8,8,128]{2,1,0:T(8,128)S(1)}, f32[2,8,128]{2,1,0:T(8,128)S(1)}) custom-call(s32[3]{0:T(128)S(1)} %pad_add_fusion.where_ref, f32[128,128]{1,0:T(8,128)S(1)} %bitcast.8, f32[9,8,8,128]{3,2,1,0:T(8,128)S(1)} %get-tuple-element.37.operator_ref), custom_call_target="tpu_custom_call" | custom-call | tf_op jit(solution)/shard_map/pallas_call | solution.py:473
  65.6 11.8 %all_to_all.10.ends = f32[8,8,128]{2,1,0:T(8,128)S(1)} all-to-all(f32[8,8,128]{2,1,0:T(8,128)S(1)} %get-tuple-element.38), channel_id=1, replica_groups={{0,64,128,192,256,320,384,448},{1,65,129,193,257,321,385,449},{2,66,130..., dimensions={0} | all-to-all | bytes 65536 | tf_op jit(solution)/shard_map/all_to_all | solution.py:484
  77.4 3.3 %shard_map.133 = f32[21,1,1024]{2,1,0:T(1,128)} custom-call(s32[3]{0:T(128)S(1)} %pad_add_fusion.where_ref, f32[8,8,128]{2,1,0:T(8,128)S(1)} %all_to_all.10.ends, f32[2,8,128]{2,1,0:T(8,128)S(1)} %get-tuple-element.39.own_ref, f32[9,8,8,128]{3,2,1,0:T(8,128)S(1)} %get-tuple-element.37.operator_ref, f32[33,8,8,128]{3,2,1,0:T(8,128)S(1)} %shard_map.131.fourfold_ref, ...), custom_call_target="tpu_custom_call" | custom-call | tf_op jit(solution)/shard_map/pallas_call | solution.py:485
  (3 shorter events, 0.0 us)
Async XLA Ops:
  1.0 15.2 %collective-permute-start = (f32[35,1024]{1,0:T(8,128)S(1)}, f32[35,1024]{1,0:T(8,128)S(1)}, u32[]{:S(2)}, u32[]{:S(2)}) collective-permute-start(f32[35,1024]{1,0:T(8,128)S(1)} %shard_map.127.centre), channel_id=1, source_target_pairs={{0,1},{1,0},{2,3},{3,2},{4,5},{5,4},{6,7},{7,6},{8,9},{9,8},{10,11... | collective-permute-start | bytes 430088 | tf_op jit(solution)/shard_map/ppermute | solution.py:364
  5.3 13.0 %collective-permute-start.1 = (f32[35,1024]{1,0:T(8,128)S(1)}, f32[35,1024]{1,0:T(8,128)S(1)}, u32[]{:S(2)}, u32[]{:S(2)}) collective-permute-start(f32[35,1024]{1,0:T(8,128)S(1)} %shard_map.127.centre), channel_id=1, source_target_pairs={{0,7},{1,2},{2,1},{3,4},{4,3},{5,6},{6,5},{7,0},{8,15},{9,10},{10,... | collective-permute-start | bytes 430088 | tf_op jit(solution)/shard_map/ppermute | solution.py:364
  18.3 36.2 %copy-start.2 = (f32[21,4]{0,1:T(4,128)S(1)}, f32[21,4]{0,1:T(4,128)}, u32[]{:S(2)}) copy-start(f32[21,4]{0,1:T(4,128)} %param.23) | copy-start | bytes 1012
  18.3 36.3 %copy-start.1 = (f32[4,4,256]{2,1,0:T(4,128)S(1)}, f32[4,4,256]{2,1,0:T(4,128)}, u32[]{:S(2)}) copy-start(f32[4,4,256]{2,1,0:T(4,128)} %inverse_ref.2) | copy-start | bytes 49156
  26.7 9.7 %collective-permute-start.2 = (f32[24,1024]{1,0:T(8,128)S(1)}, f32[24,1024]{1,0:T(8,128)S(1)}, u32[]{:S(2)}, u32[]{:S(2)}) collective-permute-start(f32[24,1024]{1,0:T(8,128)S(1)} %get-tuple-element.27.centre), channel_id=1, source_target_pairs={{0,1},{1,0},{2,3},{3,2},{4,5},{5,4},{6,7},{7,6},{8,9},{9,8},{10,11... | collective-permute-start | bytes 294920 | tf_op jit(solution)/shard_map/ppermute | solution.py:364
  28.6 7.8 %collective-permute-start.3 = (f32[24,1024]{1,0:T(8,128)S(1)}, f32[24,1024]{1,0:T(8,128)S(1)}, u32[]{:S(2)}, u32[]{:S(2)}) collective-permute-start(f32[24,1024]{1,0:T(8,128)S(1)} %get-tuple-element.27.centre), channel_id=1, source_target_pairs={{0,7},{1,2},{2,1},{3,4},{4,3},{5,6},{6,5},{7,0},{8,15},{9,10},{10,... | collective-permute-start | bytes 294920 | tf_op jit(solution)/shard_map/ppermute | solution.py:364
  33.9 0.7 copy-start
  45.8 18.5 %all-to-all-start = ((f32[64,2,128]{2,1,0:T(2,128)}), f32[64,2,128]{2,1,0:T(2,128)S(1)}, u32[]{:S(2)}, u32[]{:S(2)}) async-start(f32[64,2,128]{2,1,0:T(2,128)} %get-tuple-element.33), calls=%async_computation | async-start | bytes 131072 | tf_op jit(solution)/shard_map/all_to_all | solution.py:471

commit v7 on v5

--- a/solution.py
+++ b/solution.py
@@ -154,6 +154,12 @@
             row += count
 
 
+def added(terms):
+    while len(terms) > 1:
+        terms = [sum(terms[i : i + 2][1:], terms[i]) for i in range(0, len(terms), 2)]
+    return terms[0]
+
+
 def restricted(values, members, restrict_matrix):
     contract = (((1,), (1,)), ((), ()))
     totals = jnp.zeros((ROWS, COARSE_DEV), f32)
@@ -162,11 +168,33 @@
     counts = lax.dot_general(
         jnp.ones((16, CELLS_DEV), bf16), members, contract, preferred_element_type=f32
     )[0:1]
-    result = jnp.zeros((CDOF, COARSE_DEV), f32)
-    for d in range(DOF):
-        result = result + restrict_matrix[0:CDOF, d : d + 1] * totals[d : d + 1, :]
+    result = added(
+        [restrict_matrix[0:CDOF, d : d + 1] * totals[d : d + 1, :] for d in range(DOF)]
+    )
     result = result / counts
     return jnp.concatenate([result[i : i + 1, :] for i in range(CDOF)], axis=1)
+
+
+def prepare_kernel(*refs):
+    sources, outs, buffers, done = refs[:6], refs[6:10], refs[10:15], refs[15]
+    stencil_out, means_out, spread_out, inverse_out = outs
+    copies = [
+        pltpu.make_async_copy(source, buffer, done.at[i])
+        for i, (source, buffer) in enumerate(zip(sources, buffers + (inverse_out,)))
+    ]
+    for copy in copies:
+        copy.start()
+    for copy in copies:
+        copy.wait()
+    flux_x, flux_y, rotation, means, spread = [buffer[...] for buffer in buffers]
+    side = ROWS - DOF
+    wide = [jnp.pad(m, ((0, side), (0, side))) for m in (flux_x, flux_y, rotation)]
+    stencil = jnp.concatenate(wide + [jnp.zeros((ROWS, 8), f32)], axis=1)
+    high = stencil.astype(bf16).astype(f32)
+    stencil_out[...] = jnp.concatenate([high, high, stencil - high], axis=1).astype(bf16)
+    means_out[...] = jnp.pad(means, ((0, 8 - CDOF), (0, LANES - DOF)))
+    turned = jnp.pad(spread, ((0, 8 - CDOF), (0, LANES - DOF))).T
+    spread_out[...] = turned[0:ROWS, :]
 
 
 def first_phase_kernel(
@@ -254,12 +282,6 @@
                 held[o + repeat + 1] = tiles if o == 0 else pltpu.roll(tiles, -o % LANES, axis=2)
 
 
-def added(terms):
-    while len(terms) > 1:
-        terms = [sum(terms[i : i + 2][1:], terms[i]) for i in range(0, len(terms), 2)]
-    return terms[0]
-
-
 def coarse_slice(vector, operator_ref):
     turns = [vector] + [pltpu.roll(vector, d, axis=0) for d in range(1, 8)]
     reach = operator_ref.shape[0] // 2
@@ -388,12 +410,22 @@
     slice_here = lax.axis_index("tm")
     where = jnp.stack([slice_here // GROUP, slice_here % GROUP, lax.axis_index("space")])
     where = where.astype(jnp.int32)
-    wide = [jnp.pad(m, ((0, ROWS - DOF), (0, ROWS - DOF))) for m in (flux_x, flux_y, rotation)]
-    stencil = jnp.concatenate(wide + [jnp.zeros((ROWS, 8), f32)], axis=1)
-    high = stencil.astype(bf16)
-    low = (stencil - lax.reduce_precision(stencil, 8, 7)).astype(bf16)
-    stencil_terms = jnp.concatenate([high, high, low], axis=1)
-    means_matrix = jnp.pad(restrict_matrix, ((0, 4), (0, LANES - DOF)))
+    small = (flux_x, flux_y, rotation, restrict_matrix, prolong_matrix.T, coarse_inverse)
+    stencil_terms, means_matrix, spread_matrix, near_inverse = pl.pallas_call(
+        prepare_kernel,
+        out_shape=(
+            jax.ShapeDtypeStruct((ROWS, 240), bf16),
+            jax.ShapeDtypeStruct((8, LANES), f32),
+            jax.ShapeDtypeStruct((ROWS, 8), f32),
+            jax.ShapeDtypeStruct(coarse_inverse.shape, f32),
+        ),
+        in_specs=[pl.BlockSpec(memory_space=pltpu.HBM)] * len(small),
+        out_specs=(vmem,) * 4,
+        scratch_shapes=[pltpu.VMEM(part.shape, part.dtype) for part in small[:5]]
+        + [pltpu.SemaphoreType.DMA((len(small),))],
+        compiler_params=params,
+        cost_estimate=pl.CostEstimate(flops=2000000, bytes_accessed=200000, transcendentals=0),
+    )(*[pltpu.with_memory_space_constraint(part, pltpu.HBM) for part in small])
     half, places, coefs, start, members = pl.pallas_call(
         first_phase_kernel,
         out_shape=(
@@ -409,6 +441,18 @@
         compiler_params=params,
     )(where, first, pack, second, stencil_terms, means_matrix)
     half_first, half_second = both_sides(half)
+    late_inverse, half = lax.optimization_barrier((near_inverse, half))
+    operator, operator_twice = pl.pallas_call(
+        compose_kernel,
+        out_shape=tuple(
+            jax.ShapeDtypeStruct((2 * reach + 1, 8, 8, LANES), f32)
+            for reach in (COARSE_STEPS, 2 * COARSE_STEPS)
+        ),
+        in_specs=[vmem],
+        out_specs=(vmem, vmem),
+        compiler_params=params,
+        cost_estimate=pl.CostEstimate(flops=12000000, bytes_accessed=900000, transcendentals=0),
+    )(late_inverse)
     fine, message = pl.pallas_call(
         second_phase_kernel,
         out_shape=(
@@ -424,21 +468,9 @@
         means_matrix, start,
     )
 
-    late_inverse, late_prolong, message = lax.optimization_barrier(
-        (coarse_inverse, prolong_matrix, message)
-    )
-    operator, operator_twice = pl.pallas_call(
-        compose_kernel,
-        out_shape=tuple(
-            jax.ShapeDtypeStruct((2 * reach + 1, 8, 8, LANES), f32)
-            for reach in (COARSE_STEPS, 2 * COARSE_STEPS)
-        ),
-        in_specs=[vmem],
-        out_specs=(vmem, vmem),
-        compiler_params=params,
-        cost_estimate=pl.CostEstimate(flops=12000000, bytes_accessed=900000, transcendentals=0),
-    )(late_inverse)
-    spread_matrix = jnp.pad(late_prolong, ((0, ROWS - DOF), (0, 0)))
+    message, operator, operator_twice, spread_matrix = lax.optimization_barrier(
+        (message, operator, operator_twice, spread_matrix)
+    )
     axes = ("tm", "space")
     count = GROUP * PARTS
     inside = [[g * count + m for m in range(count)] for g in range(GROUPS)]
@@ -455,7 +487,6 @@
         scratch_shapes=[pltpu.VMEM((8 * GROUP, LANES), f32)] * 2,
         compiler_params=params,
     )(where, gathered.reshape(GROUP * PARTS * 2, LANES), operator)
-    ends, spread_matrix = lax.optimization_barrier((ends, spread_matrix))
     ends = lax.all_to_all(ends, axes, 0, 0, tiled=True, axis_index_groups=across)
     updated = pl.pallas_call(
         correct_kernel,

time: 81.4 us -> 80.5 us (0.989)
  blocking collectives: 11.8 us -> 29.3 us
  waiting for transfers between devices: 16.2 us -> 7.05 us
  starting transfers between devices: 24.9 us -> 17.2 us
  other arithmetic: 0.98 us -> 0.08 us
  local copies, waits for them, and re-layouts: 0.88 us -> 0 us
    all_to_all x0 -> x1, blocking collectives: none -> 17.4 us  [local(): lax.all_to_all(message, axes, 0, 0, tiled=True, axis_index_groups=inside)]
    all_to_all x1 -> x0, waiting for transfers between devices: 7.98 us -> none  [local(): lax.all_to_all(message, axes, 0, 0, tiled=True, axis_index_groups=inside)]
    all_to_all x1 -> x0, starting transfers between devices: 7.69 us -> none  [local(): lax.all_to_all(message, axes, 0, 0, tiled=True, axis_index_groups=inside)]
    ppermute x2, waiting for transfers between devices: 3.86 us -> 2.68 us  [both_sides(): lax.ppermute(values, 'space', others)]
    pallas_call x0 -> x1, Pallas kernels: none -> 1.03 us  [local(): pl.pallas_call(prepare_kernel, out_shape=(jax.ShapeDtypeStruct((ROWS, 240...]
    convert_element_type x2 -> x0, other arithmetic: 0.83 us -> none  [the longest x1 0.82 us: local(): high = stencil.astype(bf16)]
  transfers between devices with their start and end apart: 5 -> 4, of which waited for: 5 -> 4; matrix products, arithmetic and copies ran while one was open for 2% -> 0% of each run, Pallas kernels for 2% -> 4%
where the time goes in v7:
time: 80.5 us; the launch traced here: 80.1 us
  blocking collectives  29.3 us (36%)
  Pallas kernels  26.5 us (33%)
  starting transfers between devices  17.2 us (21%)
  waiting for transfers between devices  7.05 us (9%)
    all_to_all x1, blocking collectives, local(): lax.all_to_all(message, axes, 0, 0, tiled=True, axis_index_groups=inside)  17.4 us
    ppermute x2, starting transfers between devices, both_sides(): lax.ppermute(values, 'space', others)  13.1 us
    all_to_all x1, blocking collectives, local(): lax.all_to_all(ends, axes, 0, 0, tiled=True, axis_index_groups=across)  11.8 us
    pallas_call x1, Pallas kernels, local(): pl.pallas_call(second_phase_kernel, out_shape=(jax.ShapeDtypeStruct((ROWS...  8.71 us
    pallas_call x1, Pallas kernels, local(): pl.pallas_call(first_phase_kernel, out_shape=(jax.ShapeDtypeStruct((ROWS,...  8.38 us
    ppermute x2, waiting for transfers between devices, both_sides(): lax.ppermute(values, 'space', pairs)  4.37 us
    pallas_call x1, Pallas kernels, local(): pl.pallas_call(correct_kernel, out_shape=jax.ShapeDtypeStruct((DOF, 1, CE...  4.15 us
    ppermute x2, starting transfers between devices, both_sides(): lax.ppermute(values, 'space', pairs)  4.02 us
  transfers between devices with their start and end apart: 4, of which 4 were waited for; matrix products, arithmetic and copies ran while one was open for 0% of the time, Pallas kernels for 4%

profile of v7, /device:TPU:56, one launch (start us, length us, event | category | flops | bytes accessed | tf_op | source)
XLA Modules:
  0.0 80.1 jit_solution(13645552684784926416)
XLA Ops:
  0.0 1.0 %shard_map.127.centre = f32[35,1024]{1,0:T(8,128)S(1)} custom-call(f32[21,1,1024]{2,1,0:T(1,128)} %bitcast.10, s32[3,1024]{1,0:T(4,128)} %refs_1_.2, f32[3,1024]{1,0:T(4,128)} %refs_2_.2, f32[3,1024]{1,0:T(4,128)} %refs_3_.2, f32[3,1024]{1,0:T(4,128)} %refs_4_.1, f32[1,1024]{1,0:T(1,128)} %bitcast.11, s32[1,1024]{1,0:T(1,128)} %bitcast.12), custom_call_target="tpu_custom_call" | custom-call | tf_op jit(solution)/shard_map/pallas_call | solution.py:400
  1.0 10.9 %collective-permute-start.1 = (f32[35,1024]{1,0:T(8,128)S(1)}, f32[35,1024]{1,0:T(8,128)S(1)}, u32[]{:S(2)}, u32[]{:S(2)}) collective-permute-start(f32[35,1024]{1,0:T(8,128)S(1)} %shard_map.127.centre), channel_id=1, source_target_pairs={{0,7},{1,2},{2,1},{3,4},{4,3},{5,6},{6,5},{7,0},{8,15},{9,10},{10,... | collective-permute-start | bytes 430088 | tf_op jit(solution)/shard_map/ppermute | solution.py:370
  12.0 1.9 %collective-permute-start = (f32[35,1024]{1,0:T(8,128)S(1)}, f32[35,1024]{1,0:T(8,128)S(1)}, u32[]{:S(2)}, u32[]{:S(2)}) collective-permute-start(f32[35,1024]{1,0:T(8,128)S(1)} %shard_map.127.centre), channel_id=1, source_target_pairs={{0,1},{1,0},{2,3},{3,2},{4,5},{5,4},{6,7},{7,6},{8,9},{9,8},{10,11... | collective-permute-start | bytes 430088 | tf_op jit(solution)/shard_map/ppermute | solution.py:370
  13.9 1.0 %shard_map.128 = (bf16[24,240]{1,0:T(8,128)(2,1)S(1)}, f32[8,128]{1,0:T(8,128)S(1)}, f32[24,8]{1,0:T(8,128)S(1)}, f32[4,4,256]{2,1,0:T(4,128)S(1)}) custom-call(f32[21,21]{1,0:T(8,128)} %refs_0_.1, f32[21,21]{1,0:T(8,128)} %refs_1_.3, f32[21,21]{1,0:T(8,128)} %refs_2_.3, f32[4,21]{1,0:T(4,128)} %refs_3_.3, f32[4,21]{1,0:T(4,128)} %bitcast.13, ...), custom_call_target="tpu_custom_call" | custom-call | flops 2000000 | bytes 200000 | tf_op jit(solution)/shard_map/pallas_call | solution.py:414
  14.9 0.1 pad_add_fusion.where_ref
  15.0 1.1 %collective-permute-done.1.second = f32[35,1024]{1,0:T(8,128)S(1)} collective-permute-done((f32[35,1024]{1,0:T(8,128)S(1)}, f32[35,1024]{1,0:T(8,128)S(1)}, u32[]{:S(2)}, u32[]{:S(2)}) %collective-permute-start.1) | collective-permute-done | bytes 143392 | tf_op jit(solution)/shard_map/ppermute | solution.py:370
  16.1 3.4 %collective-permute-done.first = f32[35,1024]{1,0:T(8,128)S(1)} collective-permute-done((f32[35,1024]{1,0:T(8,128)S(1)}, f32[35,1024]{1,0:T(8,128)S(1)}, u32[]{:S(2)}, u32[]{:S(2)}) %collective-permute-start) | collective-permute-done | bytes 143392 | tf_op jit(solution)/shard_map/ppermute | solution.py:370
  19.5 8.4 %shard_map.129 = (f32[24,1024]{1,0:T(8,128)S(1)}, s32[3,8,3328]{2,1,0:T(8,128)S(1)}, f32[10,8,3328]{2,1,0:T(8,128)S(1)}, f32[1,128]{1,0:T(1,128)S(1)}, bf16[32,1024]{1,0:T(8,128)(2,1)S(1)}) custom-call(s32[3]{0:T(128)S(1)} %pad_add_fusion.where_ref, f32[35,1024]{1,0:T(8,128)S(1)} %collective-permute-done.first, f32[35,1024]{1,0:T(8,128)S(1)} %shard_map.127.centre, ...), custom_call_target="tpu_custom_call" | custom-call | tf_op jit(solution)/shard_map/pallas_call | solution.py:429
  27.9 2.2 %collective-permute-start.3 = (f32[24,1024]{1,0:T(8,128)S(1)}, f32[24,1024]{1,0:T(8,128)S(1)}, u32[]{:S(2)}, u32[]{:S(2)}) collective-permute-start(f32[24,1024]{1,0:T(8,128)S(1)} %get-tuple-element.30.centre), channel_id=1, source_target_pairs={{0,7},{1,2},{2,1},{3,4},{4,3},{5,6},{6,5},{7,0},{8,15},{9,10},{10,... | collective-permute-start | bytes 294920 | tf_op jit(solution)/shard_map/ppermute | solution.py:370
  30.1 2.1 %collective-permute-start.2 = (f32[24,1024]{1,0:T(8,128)S(1)}, f32[24,1024]{1,0:T(8,128)S(1)}, u32[]{:S(2)}, u32[]{:S(2)}) collective-permute-start(f32[24,1024]{1,0:T(8,128)S(1)} %get-tuple-element.30.centre), channel_id=1, source_target_pairs={{0,1},{1,0},{2,3},{3,2},{4,5},{5,4},{6,7},{7,6},{8,9},{9,8},{10,11... | collective-permute-start | bytes 294920 | tf_op jit(solution)/shard_map/ppermute | solution.py:370
  32.2 1.8 %shard_map.131 = (f32[9,8,8,128]{3,2,1,0:T(8,128)S(1)}, f32[17,8,8,128]{3,2,1,0:T(8,128)S(1)}) custom-call(f32[4,4,256]{2,1,0:T(4,128)S(1)} %get-tuple-element.36.inverse_ref), custom_call_target="tpu_custom_call" | custom-call | flops 12000000 | bytes 900000 | tf_op jit(solution)/shard_map/pallas_call | solution.py:445
  34.0 1.6 %collective-permute-done.3.second = f32[24,1024]{1,0:T(8,128)S(1)} collective-permute-done((f32[24,1024]{1,0:T(8,128)S(1)}, f32[24,1024]{1,0:T(8,128)S(1)}, u32[]{:S(2)}, u32[]{:S(2)}) %collective-permute-start.3) | collective-permute-done | bytes 98336 | tf_op jit(solution)/shard_map/ppermute | solution.py:370
  35.6 1.0 %collective-permute-done.2.first = f32[24,1024]{1,0:T(8,128)S(1)} collective-permute-done((f32[24,1024]{1,0:T(8,128)S(1)}, f32[24,1024]{1,0:T(8,128)S(1)}, u32[]{:S(2)}, u32[]{:S(2)}) %collective-permute-start.2) | collective-permute-done | bytes 98336 | tf_op jit(solution)/shard_map/ppermute | solution.py:370
  36.6 8.7 %shard_map.130 = (f32[24,1024]{1,0:T(8,128)S(1)}, f32[64,2,128]{2,1,0:T(2,128)S(1)}) custom-call(s32[3]{0:T(128)S(1)} %pad_add_fusion.where_ref, f32[24,1024]{1,0:T(8,128)S(1)} %collective-permute-done.2.first, f32[24,1024]{1,0:T(8,128)S(1)} %get-tuple-element.30.centre, f32[24,1024]{1,0:T(8,128)S(1)} %collective-permute-done.3.second, ...), custom_call_target="tpu_custom_call" | custom-call | tf_op jit(solution)/shard_map/pallas_call | solution.py:456
  45.3 17.4 %all_to_all.10 = f32[64,2,128]{2,1,0:T(2,128)S(1)} all-to-all(f32[64,2,128]{2,1,0:T(2,128)S(1)} %get-tuple-element.40), channel_id=1, replica_groups={{0,1,2,3,4,5,6,7,8,9,10,11,12,13,14,15,16,17,18,19,20,21,22,23,24,25,26..., dimensions={0} | all-to-all | bytes 131072 | tf_op jit(solution)/shard_map/all_to_all | solution.py:478
  62.8 1.4 %shard_map.132 = (f32[8,8,128]{2,1,0:T(8,128)S(1)}, f32[2,8,128]{2,1,0:T(8,128)S(1)}) custom-call(s32[3]{0:T(128)S(1)} %pad_add_fusion.where_ref, f32[128,128]{1,0:T(8,128)S(1)} %bitcast.9, f32[9,8,8,128]{3,2,1,0:T(8,128)S(1)} %get-tuple-element.41.operator_ref), custom_call_target="tpu_custom_call" | custom-call | tf_op jit(solution)/shard_map/pallas_call | solution.py:479
  64.1 11.8 %all_to_all.11.ends = f32[8,8,128]{2,1,0:T(8,128)S(1)} all-to-all(f32[8,8,128]{2,1,0:T(8,128)S(1)} %get-tuple-element.42), channel_id=1, replica_groups={{0,64,128,192,256,320,384,448},{1,65,129,193,257,321,385,449},{2,66,130..., dimensions={0} | all-to-all | bytes 65536 | tf_op jit(solution)/shard_map/all_to_all | solution.py:490
  76.0 4.1 %shard_map.133 = f32[21,1,1024]{2,1,0:T(1,128)} custom-call(s32[3]{0:T(128)S(1)} %pad_add_fusion.where_ref, f32[8,8,128]{2,1,0:T(8,128)S(1)} %all_to_all.11.ends, f32[2,8,128]{2,1,0:T(8,128)S(1)} %get-tuple-element.43.own_ref, f32[9,8,8,128]{3,2,1,0:T(8,128)S(1)} %get-tuple-element.41.operator_ref, f32[17,8,8,128]{3,2,1,0:T(8,128)S(1)} %get-tuple-element.44.twice_ref, ...), custom_call_target="tpu_custom_call" | custom-call | tf_op jit(solution)/shard_map/pallas_call | solution.py:491
Async XLA Ops:
  1.0 15.1 %collective-permute-start.1 = (f32[35,1024]{1,0:T(8,128)S(1)}, f32[35,1024]{1,0:T(8,128)S(1)}, u32[]{:S(2)}, u32[]{:S(2)}) collective-permute-start(f32[35,1024]{1,0:T(8,128)S(1)} %shard_map.127.centre), channel_id=1, source_target_pairs={{0,7},{1,2},{2,1},{3,4},{4,3},{5,6},{6,5},{7,0},{8,15},{9,10},{10,... | collective-permute-start | bytes 430088 | tf_op jit(solution)/shard_map/ppermute | solution.py:370
  12.0 7.6 %collective-permute-start = (f32[35,1024]{1,0:T(8,128)S(1)}, f32[35,1024]{1,0:T(8,128)S(1)}, u32[]{:S(2)}, u32[]{:S(2)}) collective-permute-start(f32[35,1024]{1,0:T(8,128)S(1)} %shard_map.127.centre), channel_id=1, source_target_pairs={{0,1},{1,0},{2,3},{3,2},{4,5},{5,4},{6,7},{7,6},{8,9},{9,8},{10,11... | collective-permute-start | bytes 430088 | tf_op jit(solution)/shard_map/ppermute | solution.py:370
  27.9 7.7 %collective-permute-start.3 = (f32[24,1024]{1,0:T(8,128)S(1)}, f32[24,1024]{1,0:T(8,128)S(1)}, u32[]{:S(2)}, u32[]{:S(2)}) collective-permute-start(f32[24,1024]{1,0:T(8,128)S(1)} %get-tuple-element.30.centre), channel_id=1, source_target_pairs={{0,7},{1,2},{2,1},{3,4},{4,3},{5,6},{6,5},{7,0},{8,15},{9,10},{10,... | collective-permute-start | bytes 294920 | tf_op jit(solution)/shard_map/ppermute | solution.py:370
  30.1 6.5 %collective-permute-start.2 = (f32[24,1024]{1,0:T(8,128)S(1)}, f32[24,1024]{1,0:T(8,128)S(1)}, u32[]{:S(2)}, u32[]{:S(2)}) collective-permute-start(f32[24,1024]{1,0:T(8,128)S(1)} %get-tuple-element.30.centre), channel_id=1, source_target_pairs={{0,1},{1,0},{2,3},{3,2},{4,5},{5,4},{6,7},{7,6},{8,9},{9,8},{10,11... | collective-permute-start | bytes 294920 | tf_op jit(solution)/shard_map/ppermute | solution.py:370

commit v8 on v7

--- a/solution.py
+++ b/solution.py
@@ -54,36 +54,43 @@
     return slice(block * LANES, (block + count) * LANES)
 
 
-def sides(odd, first, second, rows):
-    one, two = first[rows, :], second[rows, :]
-    return jnp.where(odd, one, two), jnp.where(odd, two, one)
-
-
-def in_order(odd, refs, rows):
-    left, right = sides(odd, refs[0], refs[2], rows)
-    return left, refs[1][rows, :], right
+def in_order(odd, refs, place):
+    one, two = refs[0][place], refs[2][place]
+    return jnp.where(odd, one, two), refs[1][place], jnp.where(odd, two, one)
 
 
 def fill_field(odd, state_refs, field):
-    inside = lax.broadcasted_iota(jnp.int32, (ROWS, CELLS_DEV), 0) < DOF
     edge = jnp.zeros((ROWS, LANES), f32)
     field[:, lanes_of(0)] = edge
     field[:, lanes_of(WINDOW + 1)] = edge
-    for part, state in enumerate(in_order(odd, state_refs, slice(0, ROWS))):
-        field[:, lanes_of(1 + part * BLOCKS, BLOCKS)] = jnp.where(inside, state, 0.0)
+    rest = jnp.zeros((ROWS - DOF, LANES), f32)
+    for b in range(BLOCKS):
+        whole = in_order(odd, state_refs, (slice(0, 16), b, slice(None)))
+        tail = in_order(odd, state_refs, (slice(16, DOF), b, slice(None)))
+        for part in range(3):
+            here = lanes_of(1 + part * BLOCKS + b)
+            field[0:16, here] = whole[part]
+            field[16:ROWS, here] = jnp.concatenate([tail[part], rest], axis=0)
 
 
 def fill_tables(odd, mesh_refs, places, coefs):
-    lane = lax.broadcasted_iota(jnp.int32, (8, CELLS_DEV), 1) % LANES
-    for part, mesh in enumerate(in_order(odd, mesh_refs, slice(DOF, MESH_END))):
-        cells = lanes_of(1 + part * BLOCKS, BLOCKS)
-        for e in range(3):
-            offset = mesh[e : e + 1, :].astype(jnp.int32)
-            target = jnp.broadcast_to(offset, (8, CELLS_DEV)) + lane
-            within = (target >= 0) & (target < LANES)
-            places[e, :, cells] = (target & (LANES - 1)) + jnp.where(within, 0, LANES)
-        for row in range(10):
-            coefs[row, :, cells] = jnp.broadcast_to(mesh[3 + row : 4 + row, :], (8, CELLS_DEV))
+    lane = lax.broadcasted_iota(jnp.int32, (BLOCKS, LANES), 1)
+
+    def spread(table, row, part, tile):
+        for b in range(BLOCKS):
+            here = lanes_of(1 + part * BLOCKS + b)
+            table[row, :, here] = jnp.broadcast_to(tile[b : b + 1, :], (8, LANES))
+
+    for row in range(MESH_END - DOF):
+        for part, tile in enumerate(in_order(odd, mesh_refs, DOF + row)):
+            if row < 3:
+                target = tile.astype(jnp.int32) + lane
+                within = (target >= 0) & (target < LANES)
+                spread(
+                    places, row, part, (target & (LANES - 1)) + jnp.where(within, 0, LANES)
+                )
+            else:
+                spread(coefs, row - 3, part, tile)
 
 
 def block_rate(source, block, places, coefs, stencil, low_half):
@@ -133,25 +140,24 @@
             field[:, here] = 0.5 * (field[:, here] + middle[:, here] + rate)
 
 
-def pack_kernel(*refs):
-    sources, out, buffers, done = refs[:7], refs[7], refs[8:15], refs[15]
+def pack_kernel(states, coriolis, neighbour, edge_x, edge_y, edge_damp, out, *scratch):
+    buffers, done = scratch[:4], scratch[4]
+    last = MESH_END - 1
+    pairs = [(states, out.at[0:DOF]), (coriolis, out.at[last : last + 1])]
+    pairs += list(zip((neighbour, edge_x, edge_y, edge_damp), buffers))
     copies = [
-        pltpu.make_async_copy(source, buffer, done.at[i])
-        for i, (source, buffer) in enumerate(zip(sources, buffers))
+        pltpu.make_async_copy(source, target, done.at[i])
+        for i, (source, target) in enumerate(pairs)
     ]
     for copy in copies:
         copy.start()
-    row = 0
-    for copy, buffer in zip(copies, buffers):
+    for copy in copies:
         copy.wait()
-        if len(buffer.shape) == 3:
-            for d in range(DOF):
-                out[d : d + 1, :] = buffer[d]
-            row = DOF
-        else:
-            count = buffer.shape[0]
-            out[row : row + count, :] = buffer[...].astype(f32)
-            row += count
+    for i, buffer in enumerate(buffers):
+        rows = buffer[...].astype(f32)
+        for e in range(3):
+            for b in range(BLOCKS):
+                out[DOF + 3 * i + e, b : b + 1, :] = rows[e : e + 1, lanes_of(b)]
 
 
 def added(terms):
@@ -176,8 +182,8 @@
 
 
 def prepare_kernel(*refs):
-    sources, outs, buffers, done = refs[:6], refs[6:10], refs[10:15], refs[15]
-    stencil_out, means_out, spread_out, inverse_out = outs
+    sources, outs, buffers, done = refs[:7], refs[7:12], refs[12:18], refs[18]
+    stencil_out, means_out, spread_out, members_out, inverse_out = outs
     copies = [
         pltpu.make_async_copy(source, buffer, done.at[i])
         for i, (source, buffer) in enumerate(zip(sources, buffers + (inverse_out,)))
@@ -186,7 +192,7 @@
         copy.start()
     for copy in copies:
         copy.wait()
-    flux_x, flux_y, rotation, means, spread = [buffer[...] for buffer in buffers]
+    flux_x, flux_y, rotation, means, spread, index = [buffer[...] for buffer in buffers]
     side = ROWS - DOF
     wide = [jnp.pad(m, ((0, side), (0, side))) for m in (flux_x, flux_y, rotation)]
     stencil = jnp.concatenate(wide + [jnp.zeros((ROWS, 8), f32)], axis=1)
@@ -195,25 +201,23 @@
     means_out[...] = jnp.pad(means, ((0, 8 - CDOF), (0, LANES - DOF)))
     turned = jnp.pad(spread, ((0, 8 - CDOF), (0, LANES - DOF))).T
     spread_out[...] = turned[0:ROWS, :]
+    members = lax.broadcasted_iota(jnp.int32, (COARSE_DEV, CELLS_DEV), 0) == index
+    members_out[...] = members.astype(f32).astype(bf16)
 
 
 def first_phase_kernel(
-    where_ref, first, centre, second, stencil_ref, matrix_ref,
-    out, places, coefs, start_out, members_out, field, middle,
+    where_ref, first, centre, second, stencil_ref, members_ref, matrix_ref,
+    out, places, coefs, start_out, field, middle,
 ):
     odd = where_ref[2] % 2 == 1
     packs = (first, centre, second)
     fill_tables(odd, packs, places, coefs)
     fill_field(odd, packs, field)
     start = field[:, lanes_of(1 + BLOCKS, BLOCKS)]
-    index_row = centre[MESH_END : MESH_END + 1, :].astype(jnp.int32)
-    members = (
-        lax.broadcasted_iota(jnp.int32, (COARSE_DEV, CELLS_DEV), 0) == index_row
-    ).astype(f32).astype(bf16)
-    members_out[...] = members
-    start_out[...] = restricted(start, members, matrix_ref[...])
+    start_out[...] = restricted(start, members_ref[...], matrix_ref[...])
     march(field, middle, places, coefs, stencil_ref)
-    out[...] = field[:, lanes_of(1 + BLOCKS, BLOCKS)]
+    for b in range(BLOCKS):
+        out[:, b, :] = field[0:DOF, lanes_of(1 + BLOCKS + b)]
 
 
 def second_phase_kernel(
@@ -389,20 +393,19 @@
     coarse_inverse,
 ):
     parts = (
-        states.transpose(1, 0, 2),
+        states.transpose(1, 0, 2).reshape(DOF, BLOCKS, LANES),
+        coriolis.reshape(1, BLOCKS, LANES),
         neighbour,
         edge_x,
         edge_y,
         edge_damp,
-        coriolis[None, :],
-        restrict_index[None, :],
     )
     pack = pl.pallas_call(
         pack_kernel,
-        out_shape=jax.ShapeDtypeStruct((MESH_END + 1, CELLS_DEV), f32),
+        out_shape=jax.ShapeDtypeStruct((MESH_END, BLOCKS, LANES), f32),
         in_specs=[pl.BlockSpec(memory_space=pltpu.HBM)] * len(parts),
         out_specs=vmem,
-        scratch_shapes=[pltpu.VMEM(part.shape, part.dtype) for part in parts]
+        scratch_shapes=[pltpu.VMEM(part.shape, part.dtype) for part in parts[2:]]
         + [pltpu.SemaphoreType.DMA((len(parts),))],
         compiler_params=params,
     )(*[pltpu.with_memory_space_constraint(part, pltpu.HBM) for part in parts])
@@ -410,36 +413,44 @@
     slice_here = lax.axis_index("tm")
     where = jnp.stack([slice_here // GROUP, slice_here % GROUP, lax.axis_index("space")])
     where = where.astype(jnp.int32)
-    small = (flux_x, flux_y, rotation, restrict_matrix, prolong_matrix.T, coarse_inverse)
-    stencil_terms, means_matrix, spread_matrix, near_inverse = pl.pallas_call(
+    small = (
+        flux_x,
+        flux_y,
+        rotation,
+        restrict_matrix,
+        prolong_matrix.T,
+        restrict_index[None, :],
+        coarse_inverse,
+    )
+    stencil_terms, means_matrix, spread_matrix, members, near_inverse = pl.pallas_call(
         prepare_kernel,
         out_shape=(
             jax.ShapeDtypeStruct((ROWS, 240), bf16),
             jax.ShapeDtypeStruct((8, LANES), f32),
             jax.ShapeDtypeStruct((ROWS, 8), f32),
+            jax.ShapeDtypeStruct((COARSE_DEV, CELLS_DEV), bf16),
             jax.ShapeDtypeStruct(coarse_inverse.shape, f32),
         ),
         in_specs=[pl.BlockSpec(memory_space=pltpu.HBM)] * len(small),
-        out_specs=(vmem,) * 4,
-        scratch_shapes=[pltpu.VMEM(part.shape, part.dtype) for part in small[:5]]
+        out_specs=(vmem,) * 5,
+        scratch_shapes=[pltpu.VMEM(part.shape, part.dtype) for part in small[:6]]
         + [pltpu.SemaphoreType.DMA((len(small),))],
         compiler_params=params,
         cost_estimate=pl.CostEstimate(flops=2000000, bytes_accessed=200000, transcendentals=0),
     )(*[pltpu.with_memory_space_constraint(part, pltpu.HBM) for part in small])
-    half, places, coefs, start, members = pl.pallas_call(
+    half, places, coefs, start = pl.pallas_call(
         first_phase_kernel,
         out_shape=(
-            jax.ShapeDtypeStruct((ROWS, CELLS_DEV), f32),
+            jax.ShapeDtypeStruct((DOF, BLOCKS, LANES), f32),
             jax.ShapeDtypeStruct((3, 8, TABLE), jnp.int32),
             jax.ShapeDtypeStruct((10, 8, TABLE), f32),
             jax.ShapeDtypeStruct((1, LANES), f32),
-            jax.ShapeDtypeStruct((COARSE_DEV, CELLS_DEV), bf16),
         ),
-        in_specs=[smem] + [vmem] * 5,
-        out_specs=(vmem,) * 5,
+        in_specs=[smem] + [vmem] * 6,
+        out_specs=(vmem,) * 4,
         scratch_shapes=march_scratch,
         compiler_params=params,
-    )(where, first, pack, second, stencil_terms, means_matrix)
+    )(where, first, pack, second, stencil_terms, members, means_matrix)
     half_first, half_second = both_sides(half)
     late_inverse, half = lax.optimization_barrier((near_inverse, half))
     operator, operator_twice = pl.pallas_call(

time: 80.5 us -> 80.3 us (level)
  no operation moved by 1% of the time
where the time goes in v8:
time: 80.3 us; the launch traced here: 79.9 us
  blocking collectives  29.3 us (36%)
  Pallas kernels  26.9 us (33%)
  starting transfers between devices  17.2 us (21%)
  waiting for transfers between devices  6.35 us (8%)
    all_to_all x1, blocking collectives, local(): lax.all_to_all(message, axes, 0, 0, tiled=True, axis_index_groups=inside)  17.4 us
    ppermute x2, starting transfers between devices, both_sides(): lax.ppermute(values, 'space', others)  13.1 us
    all_to_all x1, blocking collectives, local(): lax.all_to_all(ends, axes, 0, 0, tiled=True, axis_index_groups=across)  11.8 us
    pallas_call x1, Pallas kernels, local(): pl.pallas_call(second_phase_kernel, out_shape=(jax.ShapeDtypeStruct((ROWS...  8.87 us
    pallas_call x1, Pallas kernels, local(): pl.pallas_call(first_phase_kernel, out_shape=(jax.ShapeDtypeStruct((DOF,...  8.62 us
    ppermute x2, waiting for transfers between devices, both_sides(): lax.ppermute(values, 'space', pairs)  4.37 us
    pallas_call x1, Pallas kernels, local(): pl.pallas_call(correct_kernel, out_shape=jax.ShapeDtypeStruct((DOF, 1, CE...  4.15 us
    ppermute x2, starting transfers between devices, both_sides(): lax.ppermute(values, 'space', pairs)  4.02 us
  transfers between devices with their start and end apart: 4, of which 4 were waited for; matrix products, arithmetic and copies ran while one was open for 0% of the time, Pallas kernels for 4%

profile of v8, /device:TPU:56, one launch (start us, length us, event | category | flops | bytes accessed | tf_op | source)
XLA Modules:
  0.0 79.9 jit_solution(9043936696104102541)
XLA Ops:
  0.0 1.0 %shard_map.127.centre = f32[34,8,128]{2,1,0:T(8,128)S(1)} custom-call(f32[21,8,128]{2,1,0:T(8,128)} %bitcast.10, f32[1,8,128]{2,1,0:T(8,128)} %bitcast.11, s32[3,1024]{1,0:T(4,128)} %neighbour.1, f32[3,1024]{1,0:T(4,128)} %edge_x.1, f32[3,1024]{1,0:T(4,128)} %edge_y.1, f32[3,1024]{1,0:T(4,128)} %edge_damp.1), custom_call_target="tpu_custom_call" | custom-call | tf_op jit(solution)/shard_map/pallas_call | solution.py:403
  1.0 10.9 %collective-permute-start.1 = (f32[34,8,128]{2,1,0:T(8,128)S(1)}, f32[34,8,128]{2,1,0:T(8,128)S(1)}, u32[]{:S(2)}, u32[]{:S(2)}) collective-permute-start(f32[34,8,128]{2,1,0:T(8,128)S(1)} %shard_map.127.centre), channel_id=1, source_target_pairs={{0,7},{1,2},{2,1},{3,4},{4,3},{5,6},{6,5},{7,0},{8,15},{9,10},{10,... | collective-permute-start | bytes 417800 | tf_op jit(solution)/shard_map/ppermute | solution.py:374
  11.9 1.9 %collective-permute-start = (f32[34,8,128]{2,1,0:T(8,128)S(1)}, f32[34,8,128]{2,1,0:T(8,128)S(1)}, u32[]{:S(2)}, u32[]{:S(2)}) collective-permute-start(f32[34,8,128]{2,1,0:T(8,128)S(1)} %shard_map.127.centre), channel_id=1, source_target_pairs={{0,1},{1,0},{2,3},{3,2},{4,5},{5,4},{6,7},{7,6},{8,9},{9,8},{10,11... | collective-permute-start | bytes 417800 | tf_op jit(solution)/shard_map/ppermute | solution.py:374
  13.9 1.1 %shard_map.128 = (bf16[24,240]{1,0:T(8,128)(2,1)S(1)}, f32[8,128]{1,0:T(8,128)S(1)}, f32[24,8]{1,0:T(8,128)S(1)}, bf16[32,1024]{1,0:T(8,128)(2,1)S(1)}, f32[4,4,256]{2,1,0:T(4,128)S(1)}) custom-call(f32[21,21]{1,0:T(8,128)} %refs_0_.1, f32[21,21]{1,0:T(8,128)} %refs_1_.1, f32[21,21]{1,0:T(8,128)} %refs_2_.1, f32[4,21]{1,0:T(4,128)} %refs_3_.1, ...), custom_call_target="tpu_custom_call" | custom-call | flops 2000000 | bytes 200000 | tf_op jit(solution)/shard_map/pallas_call | solution.py:425
  15.0 0.1 pad_add_fusion.where_ref
  15.0 0.6 collective-permute-done.1.second
  15.6 3.4 %collective-permute-done.first = f32[34,8,128]{2,1,0:T(8,128)S(1)} collective-permute-done((f32[34,8,128]{2,1,0:T(8,128)S(1)}, f32[34,8,128]{2,1,0:T(8,128)S(1)}, u32[]{:S(2)}, u32[]{:S(2)}) %collective-permute-start) | collective-permute-done | bytes 139296 | tf_op jit(solution)/shard_map/ppermute | solution.py:374
  19.0 8.6 %shard_map.129 = (f32[21,8,128]{2,1,0:T(8,128)S(1)}, s32[3,8,3328]{2,1,0:T(8,128)S(1)}, f32[10,8,3328]{2,1,0:T(8,128)S(1)}, f32[1,128]{1,0:T(1,128)S(1)}) custom-call(s32[3]{0:T(128)S(1)} %pad_add_fusion.where_ref, f32[34,8,128]{2,1,0:T(8,128)S(1)} %collective-permute-done.first, f32[34,8,128]{2,1,0:T(8,128)S(1)} %shard_map.127.centre, ...), custom_call_target="tpu_custom_call" | custom-call | tf_op jit(solution)/shard_map/pallas_call | solution.py:441
  27.6 2.2 %collective-permute-start.3 = (f32[21,8,128]{2,1,0:T(8,128)S(1)}, f32[21,8,128]{2,1,0:T(8,128)S(1)}, u32[]{:S(2)}, u32[]{:S(2)}) collective-permute-start(f32[21,8,128]{2,1,0:T(8,128)S(1)} %get-tuple-element.31.centre), channel_id=1, source_target_pairs={{0,7},{1,2},{2,1},{3,4},{4,3},{5,6},{6,5},{7,0},{8,15},{9,10},{10,... | collective-permute-start | bytes 258056 | tf_op jit(solution)/shard_map/ppermute | solution.py:374
  29.8 2.1 %collective-permute-start.2 = (f32[21,8,128]{2,1,0:T(8,128)S(1)}, f32[21,8,128]{2,1,0:T(8,128)S(1)}, u32[]{:S(2)}, u32[]{:S(2)}) collective-permute-start(f32[21,8,128]{2,1,0:T(8,128)S(1)} %get-tuple-element.31.centre), channel_id=1, source_target_pairs={{0,1},{1,0},{2,3},{3,2},{4,5},{5,4},{6,7},{7,6},{8,9},{9,8},{10,11... | collective-permute-start | bytes 258056 | tf_op jit(solution)/shard_map/ppermute | solution.py:374
  31.9 1.8 %shard_map.131 = (f32[9,8,8,128]{3,2,1,0:T(8,128)S(1)}, f32[17,8,8,128]{3,2,1,0:T(8,128)S(1)}) custom-call(f32[4,4,256]{2,1,0:T(4,128)S(1)} %get-tuple-element.36.inverse_ref), custom_call_target="tpu_custom_call" | custom-call | flops 12000000 | bytes 900000 | tf_op jit(solution)/shard_map/pallas_call | solution.py:456
  33.7 1.4 %collective-permute-done.3.second = f32[21,8,128]{2,1,0:T(8,128)S(1)} collective-permute-done((f32[21,8,128]{2,1,0:T(8,128)S(1)}, f32[21,8,128]{2,1,0:T(8,128)S(1)}, u32[]{:S(2)}, u32[]{:S(2)}) %collective-permute-start.3) | collective-permute-done | bytes 86048 | tf_op jit(solution)/shard_map/ppermute | solution.py:374
  35.2 1.0 %collective-permute-done.2.first = f32[21,8,128]{2,1,0:T(8,128)S(1)} collective-permute-done((f32[21,8,128]{2,1,0:T(8,128)S(1)}, f32[21,8,128]{2,1,0:T(8,128)S(1)}, u32[]{:S(2)}, u32[]{:S(2)}) %collective-permute-start.2) | collective-permute-done | bytes 86048 | tf_op jit(solution)/shard_map/ppermute | solution.py:374
  36.2 8.9 %shard_map.130 = (f32[24,1024]{1,0:T(8,128)S(1)}, f32[64,2,128]{2,1,0:T(2,128)S(1)}) custom-call(s32[3]{0:T(128)S(1)} %pad_add_fusion.where_ref, f32[21,8,128]{2,1,0:T(8,128)S(1)} %collective-permute-done.2.first, f32[21,8,128]{2,1,0:T(8,128)S(1)} %get-tuple-element.31.centre, f32[21,8,128]{2,1,0:T(8,128)S(1)} %collective-permute-done.3.second, ...), custom_call_target="tpu_custom_call" | custom-call | tf_op jit(solution)/shard_map/pallas_call | solution.py:467
  45.1 17.4 %all_to_all.10 = f32[64,2,128]{2,1,0:T(2,128)S(1)} all-to-all(f32[64,2,128]{2,1,0:T(2,128)S(1)} %get-tuple-element.40), channel_id=1, replica_groups={{0,1,2,3,4,5,6,7,8,9,10,11,12,13,14,15,16,17,18,19,20,21,22,23,24,25,26..., dimensions={0} | all-to-all | bytes 131072 | tf_op jit(solution)/shard_map/all_to_all | solution.py:489
  62.5 1.4 %shard_map.132 = (f32[8,8,128]{2,1,0:T(8,128)S(1)}, f32[2,8,128]{2,1,0:T(8,128)S(1)}) custom-call(s32[3]{0:T(128)S(1)} %pad_add_fusion.where_ref, f32[128,128]{1,0:T(8,128)S(1)} %bitcast.9, f32[9,8,8,128]{3,2,1,0:T(8,128)S(1)} %get-tuple-element.41.operator_ref), custom_call_target="tpu_custom_call" | custom-call | tf_op jit(solution)/shard_map/pallas_call | solution.py:490
  63.9 11.8 %all_to_all.11.ends = f32[8,8,128]{2,1,0:T(8,128)S(1)} all-to-all(f32[8,8,128]{2,1,0:T(8,128)S(1)} %get-tuple-element.42), channel_id=1, replica_groups={{0,64,128,192,256,320,384,448},{1,65,129,193,257,321,385,449},{2,66,130..., dimensions={0} | all-to-all | bytes 65536 | tf_op jit(solution)/shard_map/all_to_all | solution.py:501
  75.7 4.1 %shard_map.133 = f32[21,1,1024]{2,1,0:T(1,128)} custom-call(s32[3]{0:T(128)S(1)} %pad_add_fusion.where_ref, f32[8,8,128]{2,1,0:T(8,128)S(1)} %all_to_all.11.ends, f32[2,8,128]{2,1,0:T(8,128)S(1)} %get-tuple-element.43.own_ref, f32[9,8,8,128]{3,2,1,0:T(8,128)S(1)} %get-tuple-element.41.operator_ref, f32[17,8,8,128]{3,2,1,0:T(8,128)S(1)} %get-tuple-element.44.twice_ref, ...), custom_call_target="tpu_custom_call" | custom-call | tf_op jit(solution)/shard_map/pallas_call | solution.py:502
Async XLA Ops:
  1.0 14.6 %collective-permute-start.1 = (f32[34,8,128]{2,1,0:T(8,128)S(1)}, f32[34,8,128]{2,1,0:T(8,128)S(1)}, u32[]{:S(2)}, u32[]{:S(2)}) collective-permute-start(f32[34,8,128]{2,1,0:T(8,128)S(1)} %shard_map.127.centre), channel_id=1, source_target_pairs={{0,7},{1,2},{2,1},{3,4},{4,3},{5,6},{6,5},{7,0},{8,15},{9,10},{10,... | collective-permute-start | bytes 417800 | tf_op jit(solution)/shard_map/ppermute | solution.py:374
  11.9 7.0 %collective-permute-start = (f32[34,8,128]{2,1,0:T(8,128)S(1)}, f32[34,8,128]{2,1,0:T(8,128)S(1)}, u32[]{:S(2)}, u32[]{:S(2)}) collective-permute-start(f32[34,8,128]{2,1,0:T(8,128)S(1)} %shard_map.127.centre), channel_id=1, source_target_pairs={{0,1},{1,0},{2,3},{3,2},{4,5},{5,4},{6,7},{7,6},{8,9},{9,8},{10,11... | collective-permute-start | bytes 417800 | tf_op jit(solution)/shard_map/ppermute | solution.py:374
  27.6 7.6 %collective-permute-start.3 = (f32[21,8,128]{2,1,0:T(8,128)S(1)}, f32[21,8,128]{2,1,0:T(8,128)S(1)}, u32[]{:S(2)}, u32[]{:S(2)}) collective-permute-start(f32[21,8,128]{2,1,0:T(8,128)S(1)} %get-tuple-element.31.centre), channel_id=1, source_target_pairs={{0,7},{1,2},{2,1},{3,4},{4,3},{5,6},{6,5},{7,0},{8,15},{9,10},{10,... | collective-permute-start | bytes 258056 | tf_op jit(solution)/shard_map/ppermute | solution.py:374
  29.8 6.4 %collective-permute-start.2 = (f32[21,8,128]{2,1,0:T(8,128)S(1)}, f32[21,8,128]{2,1,0:T(8,128)S(1)}, u32[]{:S(2)}, u32[]{:S(2)}) collective-permute-start(f32[21,8,128]{2,1,0:T(8,128)S(1)} %get-tuple-element.31.centre), channel_id=1, source_target_pairs={{0,1},{1,0},{2,3},{3,2},{4,5},{5,4},{6,7},{7,6},{8,9},{9,8},{10,11... | collective-permute-start | bytes 258056 | tf_op jit(solution)/shard_map/ppermute | solution.py:374

commit v9 on v8

--- a/solution.py
+++ b/solution.py
@@ -181,71 +181,16 @@
     return jnp.concatenate([result[i : i + 1, :] for i in range(CDOF)], axis=1)
 
 
-def prepare_kernel(*refs):
-    sources, outs, buffers, done = refs[:7], refs[7:12], refs[12:18], refs[18]
-    stencil_out, means_out, spread_out, members_out, inverse_out = outs
-    copies = [
-        pltpu.make_async_copy(source, buffer, done.at[i])
-        for i, (source, buffer) in enumerate(zip(sources, buffers + (inverse_out,)))
-    ]
-    for copy in copies:
-        copy.start()
-    for copy in copies:
-        copy.wait()
-    flux_x, flux_y, rotation, means, spread, index = [buffer[...] for buffer in buffers]
-    side = ROWS - DOF
-    wide = [jnp.pad(m, ((0, side), (0, side))) for m in (flux_x, flux_y, rotation)]
-    stencil = jnp.concatenate(wide + [jnp.zeros((ROWS, 8), f32)], axis=1)
-    high = stencil.astype(bf16).astype(f32)
-    stencil_out[...] = jnp.concatenate([high, high, stencil - high], axis=1).astype(bf16)
-    means_out[...] = jnp.pad(means, ((0, 8 - CDOF), (0, LANES - DOF)))
-    turned = jnp.pad(spread, ((0, 8 - CDOF), (0, LANES - DOF))).T
-    spread_out[...] = turned[0:ROWS, :]
-    members = lax.broadcasted_iota(jnp.int32, (COARSE_DEV, CELLS_DEV), 0) == index
-    members_out[...] = members.astype(f32).astype(bf16)
-
-
-def first_phase_kernel(
-    where_ref, first, centre, second, stencil_ref, members_ref, matrix_ref,
-    out, places, coefs, start_out, field, middle,
-):
-    odd = where_ref[2] % 2 == 1
-    packs = (first, centre, second)
-    fill_tables(odd, packs, places, coefs)
-    fill_field(odd, packs, field)
-    start = field[:, lanes_of(1 + BLOCKS, BLOCKS)]
-    start_out[...] = restricted(start, members_ref[...], matrix_ref[...])
-    march(field, middle, places, coefs, stencil_ref)
-    for b in range(BLOCKS):
-        out[:, b, :] = field[0:DOF, lanes_of(1 + BLOCKS + b)]
-
-
-def second_phase_kernel(
-    where_ref, first, centre, second, places, coefs, stencil_ref, members_ref, matrix_ref, start_ref,
-    out, message, field, middle,
-):
-    fill_field(where_ref[2] % 2 == 1, (first, centre, second), field)
-    march(field, middle, places, coefs, stencil_ref)
-    fine = field[:, lanes_of(1 + BLOCKS, BLOCKS)]
-    out[...] = fine
-    rows = jnp.concatenate(
-        [restricted(fine, members_ref[...], matrix_ref[...]), start_ref[...]], axis=0
-    )
-    for copy in range(GROUP * PARTS):
-        message[copy] = rows
-
-
 def flipped(tiles, even_row):
     up = pltpu.roll(jnp.concatenate([tiles[1:], tiles[:1]], axis=0), 7, axis=1)
     down = pltpu.roll(jnp.concatenate([tiles[7:], tiles[:7]], axis=0), 1, axis=1)
     return jnp.where(even_row, up, down)
 
 
-def compose_kernel(inverse_ref, out, out_twice):
+def composed(reach, inverse_ref, first, last):
     shape = (8, 8, LANES)
     row = lax.broadcasted_iota(jnp.int32, shape, 1)
     lane = lax.broadcasted_iota(jnp.int32, shape, 2)
-    turn = lax.broadcasted_iota(jnp.int32, shape, 0)
     even_row = row % 2 == 0
     first_lane = lane == 0
     last_lane = lane == LANES - 1
@@ -258,8 +203,7 @@
             for h in range(2):
                 pieces.append(inverse_ref[i, j : j + 1, lanes_of(h)])
         blocks.append(jnp.concatenate(pieces, axis=0)[None])
-    reach = {0: jnp.where(turn == 0, 1.0, 0.0)}
-    for repeat in range(2 * COARSE_STEPS):
+    for repeat in range(first, last):
         swapped = {o: flipped(tiles, even_row) for o, tiles in reach.items()}
         blended = {}
         for o in range(-repeat - 1, repeat + 2):
@@ -280,10 +224,78 @@
                 turned = jnp.concatenate([tiles[8 - 2 * by :], tiles[: 8 - 2 * by]], axis=0)
                 total = total + blocks[by] * pltpu.roll(turned, 2 * by, axis=1)
             reach[o] = total
-        if (repeat + 1) % COARSE_STEPS == 0:
-            held = out if repeat < COARSE_STEPS else out_twice
-            for o, tiles in reach.items():
-                held[o + repeat + 1] = tiles if o == 0 else pltpu.roll(tiles, -o % LANES, axis=2)
+    return reach
+
+
+def keep_operator(out, reach):
+    size = max(reach)
+    for o, tiles in reach.items():
+        out[o + size] = tiles if o == 0 else pltpu.roll(tiles, -o % LANES, axis=2)
+
+
+def prepare_kernel(*refs):
+    sources, outs, buffers, done = refs[:7], refs[7:14], refs[14:20], refs[20]
+    stencil_out, means_out, spread_out, members_out, operator_out, once_out, inverse_out = outs
+    copies = [
+        pltpu.make_async_copy(source, buffer, done.at[i])
+        for i, (source, buffer) in enumerate(zip(sources, buffers + (inverse_out,)))
+    ]
+    for copy in copies:
+        copy.start()
+    for copy in copies:
+        copy.wait()
+    flux_x, flux_y, rotation, means, spread, index = [buffer[...] for buffer in buffers]
+    side = ROWS - DOF
+    wide = [jnp.pad(m, ((0, side), (0, side))) for m in (flux_x, flux_y, rotation)]
+    stencil = jnp.concatenate(wide + [jnp.zeros((ROWS, 8), f32)], axis=1)
+    high = stencil.astype(bf16).astype(f32)
+    stencil_out[...] = jnp.concatenate([high, high, stencil - high], axis=1).astype(bf16)
+    means_out[...] = jnp.pad(means, ((0, 8 - CDOF), (0, LANES - DOF)))
+    turned = jnp.pad(spread, ((0, 8 - CDOF), (0, LANES - DOF))).T
+    spread_out[...] = turned[0:ROWS, :]
+    members = lax.broadcasted_iota(jnp.int32, (COARSE_DEV, CELLS_DEV), 0) == index
+    members_out[...] = members.astype(f32).astype(bf16)
+    turn = lax.broadcasted_iota(jnp.int32, (8, 8, LANES), 0)
+    reach = composed({0: jnp.where(turn == 0, 1.0, 0.0)}, inverse_out, 0, COARSE_STEPS)
+    keep_operator(operator_out, reach)
+    for o, tiles in reach.items():
+        once_out[o + COARSE_STEPS] = tiles
+
+
+def first_phase_kernel(
+    where_ref, first, centre, second, stencil_ref, members_ref, matrix_ref,
+    out, places, coefs, start_out, field, middle,
+):
+    odd = where_ref[2] % 2 == 1
+    packs = (first, centre, second)
+    fill_tables(odd, packs, places, coefs)
+    fill_field(odd, packs, field)
+    start = field[:, lanes_of(1 + BLOCKS, BLOCKS)]
+    start_out[...] = restricted(start, members_ref[...], matrix_ref[...])
+    march(field, middle, places, coefs, stencil_ref)
+    for b in range(BLOCKS):
+        out[:, b, :] = field[0:DOF, lanes_of(1 + BLOCKS + b)]
+
+
+def second_phase_kernel(
+    where_ref, first, centre, second, places, coefs, stencil_ref, members_ref, matrix_ref, start_ref,
+    out, message, field, middle,
+):
+    fill_field(where_ref[2] % 2 == 1, (first, centre, second), field)
+    march(field, middle, places, coefs, stencil_ref)
+    fine = field[:, lanes_of(1 + BLOCKS, BLOCKS)]
+    out[...] = fine
+    rows = jnp.concatenate(
+        [restricted(fine, members_ref[...], matrix_ref[...]), start_ref[...]], axis=0
+    )
+    for copy in range(GROUP * PARTS):
+        message[copy] = rows
+
+
+def compose_kernel(once_ref, inverse_ref, out):
+    size = COARSE_STEPS
+    reach = {o: once_ref[o + size] for o in range(-size, size + 1)}
+    keep_operator(out, composed(reach, inverse_ref, size, 2 * size))
 
 
 def coarse_slice(vector, operator_ref):
@@ -422,17 +434,22 @@
         restrict_index[None, :],
         coarse_inverse,
     )
-    stencil_terms, means_matrix, spread_matrix, members, near_inverse = pl.pallas_call(
+    once = jax.ShapeDtypeStruct((2 * COARSE_STEPS + 1, 8, 8, LANES), f32)
+    (
+        stencil_terms, means_matrix, spread_matrix, members, operator, reach, near_inverse
+    ) = pl.pallas_call(
         prepare_kernel,
         out_shape=(
             jax.ShapeDtypeStruct((ROWS, 240), bf16),
             jax.ShapeDtypeStruct((8, LANES), f32),
             jax.ShapeDtypeStruct((ROWS, 8), f32),
             jax.ShapeDtypeStruct((COARSE_DEV, CELLS_DEV), bf16),
+            once,
+            once,
             jax.ShapeDtypeStruct(coarse_inverse.shape, f32),
         ),
         in_specs=[pl.BlockSpec(memory_space=pltpu.HBM)] * len(small),
-        out_specs=(vmem,) * 5,
+        out_specs=(vmem,) * 7,
         scratch_shapes=[pltpu.VMEM(part.shape, part.dtype) for part in small[:6]]
         + [pltpu.SemaphoreType.DMA((len(small),))],
         compiler_params=params,
@@ -452,18 +469,15 @@
         compiler_params=params,
     )(where, first, pack, second, stencil_terms, members, means_matrix)
     half_first, half_second = both_sides(half)
-    late_inverse, half = lax.optimization_barrier((near_inverse, half))
-    operator, operator_twice = pl.pallas_call(
+    reach, late_inverse, half = lax.optimization_barrier((reach, near_inverse, half))
+    operator_twice = pl.pallas_call(
         compose_kernel,
-        out_shape=tuple(
-            jax.ShapeDtypeStruct((2 * reach + 1, 8, 8, LANES), f32)
-            for reach in (COARSE_STEPS, 2 * COARSE_STEPS)
-        ),
-        in_specs=[vmem],
-        out_specs=(vmem, vmem),
-        compiler_params=params,
-        cost_estimate=pl.CostEstimate(flops=12000000, bytes_accessed=900000, transcendentals=0),
-    )(late_inverse)
+        out_shape=jax.ShapeDtypeStruct((4 * COARSE_STEPS + 1, 8, 8, LANES), f32),
+        in_specs=[vmem] * 2,
+        out_specs=vmem,
+        compiler_params=params,
+        cost_estimate=pl.CostEstimate(flops=9000000, bytes_accessed=900000, transcendentals=0),
+    )(reach, late_inverse)
     fine, message = pl.pallas_call(
         second_phase_kernel,
         out_shape=(

time: 80.3 us -> 80.1 us (level)
  no operation moved by 1% of the time
where the time goes in v9:
time: 80.1 us; the launch traced here: 79.7 us
  blocking collectives  29.3 us (37%)
  Pallas kernels  26.6 us (33%)
  starting transfers between devices  17.2 us (21%)
  waiting for transfers between devices  6.42 us (8%)
    all_to_all x1, blocking collectives, local(): lax.all_to_all(message, axes, 0, 0, tiled=True, axis_index_groups=inside)  17.4 us
    ppermute x2, starting transfers between devices, both_sides(): lax.ppermute(values, 'space', others)  13.1 us
    all_to_all x1, blocking collectives, local(): lax.all_to_all(ends, axes, 0, 0, tiled=True, axis_index_groups=across)  11.8 us
    pallas_call x1, Pallas kernels, local(): pl.pallas_call(second_phase_kernel, out_shape=(jax.ShapeDtypeStruct((ROWS...  8.79 us
    pallas_call x1, Pallas kernels, local(): pl.pallas_call(first_phase_kernel, out_shape=(jax.ShapeDtypeStruct((DOF,...  8.53 us
    ppermute x2, waiting for transfers between devices, both_sides(): lax.ppermute(values, 'space', pairs)  4.37 us
    pallas_call x1, Pallas kernels, local(): pl.pallas_call(correct_kernel, out_shape=jax.ShapeDtypeStruct((DOF, 1, CE...  4.15 us
    ppermute x2, starting transfers between devices, both_sides(): lax.ppermute(values, 'space', pairs)  4.02 us
  transfers between devices with their start and end apart: 4, of which 4 were waited for; matrix products, arithmetic and copies ran while one was open for 0% of the time, Pallas kernels for 4%

profile of v9, /device:TPU:56, one launch (start us, length us, event | category | flops | bytes accessed | tf_op | source)
XLA Modules:
  0.0 79.7 jit_solution(11623107648896918026)
XLA Ops:
  0.0 1.0 %shard_map.127.centre = f32[34,8,128]{2,1,0:T(8,128)S(1)} custom-call(f32[21,8,128]{2,1,0:T(8,128)} %bitcast.10, f32[1,8,128]{2,1,0:T(8,128)} %bitcast.11, s32[3,1024]{1,0:T(4,128)} %neighbour.1, f32[3,1024]{1,0:T(4,128)} %edge_x.1, f32[3,1024]{1,0:T(4,128)} %edge_y.1, f32[3,1024]{1,0:T(4,128)} %edge_damp.1), custom_call_target="tpu_custom_call" | custom-call | tf_op jit(solution)/shard_map/pallas_call | solution.py:415
  1.0 10.9 %collective-permute-start.1 = (f32[34,8,128]{2,1,0:T(8,128)S(1)}, f32[34,8,128]{2,1,0:T(8,128)S(1)}, u32[]{:S(2)}, u32[]{:S(2)}) collective-permute-start(f32[34,8,128]{2,1,0:T(8,128)S(1)} %shard_map.127.centre), channel_id=1, source_target_pairs={{0,7},{1,2},{2,1},{3,4},{4,3},{5,6},{6,5},{7,0},{8,15},{9,10},{10,... | collective-permute-start | bytes 417800 | tf_op jit(solution)/shard_map/ppermute | solution.py:386
  11.9 1.9 %collective-permute-start = (f32[34,8,128]{2,1,0:T(8,128)S(1)}, f32[34,8,128]{2,1,0:T(8,128)S(1)}, u32[]{:S(2)}, u32[]{:S(2)}) collective-permute-start(f32[34,8,128]{2,1,0:T(8,128)S(1)} %shard_map.127.centre), channel_id=1, source_target_pairs={{0,1},{1,0},{2,3},{3,2},{4,5},{5,4},{6,7},{7,6},{8,9},{9,8},{10,11... | collective-permute-start | bytes 417800 | tf_op jit(solution)/shard_map/ppermute | solution.py:386
  13.9 1.5 %shard_map.128 = (bf16[24,240]{1,0:T(8,128)(2,1)S(1)}, f32[8,128]{1,0:T(8,128)S(1)}, f32[24,8]{1,0:T(8,128)S(1)}, bf16[32,1024]{1,0:T(8,128)(2,1)S(1)}, f32[9,8,...) custom-call(f32[21,21]{1,0:T(8,128)} %refs_0_.1, f32[21,21]{1,0:T(8,128)} %refs_1_.1, ...), custom_call_target="tpu_custom_call" | custom-call | flops 2000000 | bytes 200000 | tf_op jit(solution)/shard_map/pallas_call | solution.py:440
  15.4 0.1 pad_add_fusion.where_ref
  15.5 0.1 collective-permute-done.1.second
  15.6 3.4 %collective-permute-done.first = f32[34,8,128]{2,1,0:T(8,128)S(1)} collective-permute-done((f32[34,8,128]{2,1,0:T(8,128)S(1)}, f32[34,8,128]{2,1,0:T(8,128)S(1)}, u32[]{:S(2)}, u32[]{:S(2)}) %collective-permute-start) | collective-permute-done | bytes 139296 | tf_op jit(solution)/shard_map/ppermute | solution.py:386
  19.0 8.5 %shard_map.129 = (f32[21,8,128]{2,1,0:T(8,128)S(1)}, s32[3,8,3328]{2,1,0:T(8,128)S(1)}, f32[10,8,3328]{2,1,0:T(8,128)S(1)}, f32[1,128]{1,0:T(1,128)S(1)}) custom-call(s32[3]{0:T(128)S(1)} %pad_add_fusion.where_ref, f32[34,8,128]{2,1,0:T(8,128)S(1)} %collective-permute-done.first, f32[34,8,128]{2,1,0:T(8,128)S(1)} %shard_map.127.centre, ...), custom_call_target="tpu_custom_call" | custom-call | tf_op jit(solution)/shard_map/pallas_call | solution.py:458
  27.5 2.2 %collective-permute-start.3 = (f32[21,8,128]{2,1,0:T(8,128)S(1)}, f32[21,8,128]{2,1,0:T(8,128)S(1)}, u32[]{:S(2)}, u32[]{:S(2)}) collective-permute-start(f32[21,8,128]{2,1,0:T(8,128)S(1)} %get-tuple-element.33.centre), channel_id=1, source_target_pairs={{0,7},{1,2},{2,1},{3,4},{4,3},{5,6},{6,5},{7,0},{8,15},{9,10},{10,... | collective-permute-start | bytes 258056 | tf_op jit(solution)/shard_map/ppermute | solution.py:386
  29.7 2.1 %collective-permute-start.2 = (f32[21,8,128]{2,1,0:T(8,128)S(1)}, f32[21,8,128]{2,1,0:T(8,128)S(1)}, u32[]{:S(2)}, u32[]{:S(2)}) collective-permute-start(f32[21,8,128]{2,1,0:T(8,128)S(1)} %get-tuple-element.33.centre), channel_id=1, source_target_pairs={{0,1},{1,0},{2,3},{3,2},{4,5},{5,4},{6,7},{7,6},{8,9},{9,8},{10,11... | collective-permute-start | bytes 258056 | tf_op jit(solution)/shard_map/ppermute | solution.py:386
  31.8 1.3 %shard_map.131.twice_ref = f32[17,8,8,128]{3,2,1,0:T(8,128)S(1)} custom-call(f32[9,8,8,128]{3,2,1,0:T(8,128)S(1)} %get-tuple-element.39.once_ref, f32[4,4,256]{2,1,0:T(4,128)S(1)} %get-tuple-element.40.inverse_ref), custom_call_target="tpu_custom_call" | custom-call | flops 9000000 | bytes 900000 | tf_op jit(solution)/shard_map/pallas_call | solution.py:473
  33.1 1.9 %collective-permute-done.3.second = f32[21,8,128]{2,1,0:T(8,128)S(1)} collective-permute-done((f32[21,8,128]{2,1,0:T(8,128)S(1)}, f32[21,8,128]{2,1,0:T(8,128)S(1)}, u32[]{:S(2)}, u32[]{:S(2)}) %collective-permute-start.3) | collective-permute-done | bytes 86048 | tf_op jit(solution)/shard_map/ppermute | solution.py:386
  35.1 1.0 %collective-permute-done.2.first = f32[21,8,128]{2,1,0:T(8,128)S(1)} collective-permute-done((f32[21,8,128]{2,1,0:T(8,128)S(1)}, f32[21,8,128]{2,1,0:T(8,128)S(1)}, u32[]{:S(2)}, u32[]{:S(2)}) %collective-permute-start.2) | collective-permute-done | bytes 86048 | tf_op jit(solution)/shard_map/ppermute | solution.py:386
  36.1 8.8 %shard_map.130 = (f32[24,1024]{1,0:T(8,128)S(1)}, f32[64,2,128]{2,1,0:T(2,128)S(1)}) custom-call(s32[3]{0:T(128)S(1)} %pad_add_fusion.where_ref, f32[21,8,128]{2,1,0:T(8,128)S(1)} %collective-permute-done.2.first, f32[21,8,128]{2,1,0:T(8,128)S(1)} %get-tuple-element.33.centre, f32[21,8,128]{2,1,0:T(8,128)S(1)} %collective-permute-done.3.second, ...), custom_call_target="tpu_custom_call" | custom-call | tf_op jit(solution)/shard_map/pallas_call | solution.py:481
  44.9 17.4 %all_to_all.10 = f32[64,2,128]{2,1,0:T(2,128)S(1)} all-to-all(f32[64,2,128]{2,1,0:T(2,128)S(1)} %get-tuple-element.42), channel_id=1, replica_groups={{0,1,2,3,4,5,6,7,8,9,10,11,12,13,14,15,16,17,18,19,20,21,22,23,24,25,26..., dimensions={0} | all-to-all | bytes 131072 | tf_op jit(solution)/shard_map/all_to_all | solution.py:503
  62.3 1.4 %shard_map.132 = (f32[8,8,128]{2,1,0:T(8,128)S(1)}, f32[2,8,128]{2,1,0:T(8,128)S(1)}) custom-call(s32[3]{0:T(128)S(1)} %pad_add_fusion.where_ref, f32[128,128]{1,0:T(8,128)S(1)} %bitcast.9, f32[9,8,8,128]{3,2,1,0:T(8,128)S(1)} %get-tuple-element.43.operator_ref), custom_call_target="tpu_custom_call" | custom-call | tf_op jit(solution)/shard_map/pallas_call | solution.py:504
  63.7 11.8 %all_to_all.11.ends = f32[8,8,128]{2,1,0:T(8,128)S(1)} all-to-all(f32[8,8,128]{2,1,0:T(8,128)S(1)} %get-tuple-element.44), channel_id=1, replica_groups={{0,64,128,192,256,320,384,448},{1,65,129,193,257,321,385,449},{2,66,130..., dimensions={0} | all-to-all | bytes 65536 | tf_op jit(solution)/shard_map/all_to_all | solution.py:515
  75.5 4.1 %shard_map.133 = f32[21,1,1024]{2,1,0:T(1,128)} custom-call(s32[3]{0:T(128)S(1)} %pad_add_fusion.where_ref, f32[8,8,128]{2,1,0:T(8,128)S(1)} %all_to_all.11.ends, f32[2,8,128]{2,1,0:T(8,128)S(1)} %get-tuple-element.45.own_ref, f32[9,8,8,128]{3,2,1,0:T(8,128)S(1)} %get-tuple-element.43.operator_ref, f32[17,8,8,128]{3,2,1,0:T(8,128)S(1)} %shard_map.131.twice_ref, ...), custom_call_target="tpu_custom_call" | custom-call | tf_op jit(solution)/shard_map/pallas_call | solution.py:516
Async XLA Ops:
  1.0 14.6 %collective-permute-start.1 = (f32[34,8,128]{2,1,0:T(8,128)S(1)}, f32[34,8,128]{2,1,0:T(8,128)S(1)}, u32[]{:S(2)}, u32[]{:S(2)}) collective-permute-start(f32[34,8,128]{2,1,0:T(8,128)S(1)} %shard_map.127.centre), channel_id=1, source_target_pairs={{0,7},{1,2},{2,1},{3,4},{4,3},{5,6},{6,5},{7,0},{8,15},{9,10},{10,... | collective-permute-start | bytes 417800 | tf_op jit(solution)/shard_map/ppermute | solution.py:386
  11.9 7.0 %collective-permute-start = (f32[34,8,128]{2,1,0:T(8,128)S(1)}, f32[34,8,128]{2,1,0:T(8,128)S(1)}, u32[]{:S(2)}, u32[]{:S(2)}) collective-permute-start(f32[34,8,128]{2,1,0:T(8,128)S(1)} %shard_map.127.centre), channel_id=1, source_target_pairs={{0,1},{1,0},{2,3},{3,2},{4,5},{5,4},{6,7},{7,6},{8,9},{9,8},{10,11... | collective-permute-start | bytes 417800 | tf_op jit(solution)/shard_map/ppermute | solution.py:386
  27.5 7.6 %collective-permute-start.3 = (f32[21,8,128]{2,1,0:T(8,128)S(1)}, f32[21,8,128]{2,1,0:T(8,128)S(1)}, u32[]{:S(2)}, u32[]{:S(2)}) collective-permute-start(f32[21,8,128]{2,1,0:T(8,128)S(1)} %get-tuple-element.33.centre), channel_id=1, source_target_pairs={{0,7},{1,2},{2,1},{3,4},{4,3},{5,6},{6,5},{7,0},{8,15},{9,10},{10,... | collective-permute-start | bytes 258056 | tf_op jit(solution)/shard_map/ppermute | solution.py:386
  29.7 6.4 %collective-permute-start.2 = (f32[21,8,128]{2,1,0:T(8,128)S(1)}, f32[21,8,128]{2,1,0:T(8,128)S(1)}, u32[]{:S(2)}, u32[]{:S(2)}) collective-permute-start(f32[21,8,128]{2,1,0:T(8,128)S(1)} %get-tuple-element.33.centre), channel_id=1, source_target_pairs={{0,1},{1,0},{2,3},{3,2},{4,5},{5,4},{6,7},{7,6},{8,9},{9,8},{10,11... | collective-permute-start | bytes 258056 | tf_op jit(solution)/shard_map/ppermute | solution.py:386
